TPU v7x, 32 devices: a whole 2x2x4 slice. The times are simulated.
32 devices in a mesh: dp: 8 (over y, x, core), mp: 4 (over z).
Axes of the slice: x: 2, y: 2, z: 4, core: 2. Of those that a mesh axis runs over, the one named last changes fastest.
Arguments:
- tokens: bfloat16 [8, 2048, 1024], P('dp', 'mp'), may hold values from -6 to 6
- w_qkv: bfloat16 [1024, 3, 1024], P(None, None, 'mp'), may hold values from -0.1875 to 0.1875
- w_out: bfloat16 [1024, 1024], P('mp'), may hold values from -0.1875 to 0.1875
- w_up: bfloat16 [1024, 4096], P(None, 'mp'), may hold values from -0.1875 to 0.1875
- w_down: bfloat16 [4096, 1024], P('mp'), may hold values from -0.09375 to 0.09375
- norm_gains: float32 [4, 1024], replicated, may hold values from 0.5 to 1.5
- norm_shifts: float32 [4, 1024], replicated, may hold values from -1 to 1
- cotangent: bfloat16 [8, 2048, 1024], P('dp', 'mp'), may hold values from -6 to 6
- corpus_ids: int32 [8], P('dp'), may hold values from 0 to 7
- corpus_weight: float32 [8], replicated, may hold values from 0.25 to 4
Outputs:
- output: bfloat16 [8, 2048, 1024], P('dp', 'mp')
- input_grad: float32 [8, 2048, 1024], P('dp', 'mp')
- qkv_grad: float32 [1024, 3, 1024], P(None, None, 'mp')
- out_grad: float32 [1024, 1024], P('mp')
- up_grad: float32 [1024, 4096], P(None, 'mp')
- down_grad: float32 [4096, 1024], P('mp')
- gain_grad: float32 [4, 1024], replicated
- shift_grad: float32 [4, 1024], replicated
Inputs may be any that keep to these rules, and one draw needn't show every extreme that they name: `corpus_ids`: each entry names one of the 8 corpora.
All inputs are finite; a program needn't handle non-finite values.
Results may differ from a plain program's by a relative error of at most 0.018.
Values may be sent and summed in bfloat16 or wider, within the bound.
A program may use at most 256 MiB of HBM per device.

v0:
```python
import jax
import jax.numpy as jnp
from jax import lax
from jax.sharding import PartitionSpec as P

HEAD_DIM = 64
BLOCK = 512


def norm_forward(value, gain, shift):
    center = value - jnp.mean(value, axis=-1, keepdims=True)
    spread = jnp.mean(center * center, axis=-1, keepdims=True)
    inverse = lax.rsqrt(spread + 1e-05)
    unit = center * inverse
    return (unit * gain + shift, unit, inverse)


def norm_backward(grad, unit, inverse, gain):
    scaled = grad * gain
    back = inverse * (
        scaled
        - jnp.mean(scaled, axis=-1, keepdims=True)
        - unit * jnp.mean(scaled * unit, axis=-1, keepdims=True)
    )
    return (back, jnp.sum(grad * unit, axis=(0, 1)), jnp.sum(grad, axis=(0, 1)))


def rotary_tables(length, half):
    steps = jnp.arange(half, dtype=jnp.float32) / half
    freqs = 10000.0 ** (-steps)
    angles = jnp.arange(length, dtype=jnp.float32)[:, None] * freqs[None, :]
    return (jnp.cos(angles)[None, :, None, :], jnp.sin(angles)[None, :, None, :])


def rotate(value, cosine, sine):
    half = value.shape[-1] // 2
    first = value[..., :half]
    second = value[..., half:]
    return jnp.concatenate(
        [first * cosine - second * sine, second * cosine + first * sine], axis=-1
    )


def rotate_back(grad, cosine, sine):
    half = grad.shape[-1] // 2
    first = grad[..., :half]
    second = grad[..., half:]
    return jnp.concatenate(
        [first * cosine + second * sine, second * cosine - first * sine], axis=-1
    )


def causal_mask(start, end):
    query_pos = start + jnp.arange(BLOCK, dtype=jnp.int32)
    key_pos = jnp.arange(end, dtype=jnp.int32)
    return (key_pos[None, :] <= query_pos[:, None])[None, None]


def block_scores(rows, keys, start, end):
    scores = jnp.einsum("bqhe,bkhe->bhqk", rows, keys[:, :end], preferred_element_type=jnp.float32)
    return jnp.where(causal_mask(start, end), scores, -1e30)


def attend_forward(queries, keys, values):
    length = queries.shape[1]
    outputs = []
    totals = []
    for start in range(0, length, BLOCK):
        end = start + BLOCK
        scores = block_scores(queries[:, start:end], keys, start, end)
        top = jnp.max(scores, axis=-1, keepdims=True)
        expo = jnp.exp(scores - top)
        total = jnp.sum(expo, axis=-1, keepdims=True)
        probs = (expo / total).astype(jnp.bfloat16)
        outputs.append(
            jnp.einsum(
                "bhqk,bkhe->bqhe", probs, values[:, :end], preferred_element_type=jnp.float32
            )
        )
        totals.append(top + jnp.log(total))
    return (jnp.concatenate(outputs, axis=1), jnp.concatenate(totals, axis=2))


def attend_backward(queries, keys, values, grad_att, logsum):
    length = queries.shape[1]
    grad_q = []
    grad_k = jnp.zeros(keys.shape, jnp.float32)
    grad_v = jnp.zeros(values.shape, jnp.float32)
    for start in range(0, length, BLOCK):
        end = start + BLOCK
        rows = queries[:, start:end]
        scores = block_scores(rows, keys, start, end)
        probs = jnp.exp(scores - logsum[:, :, start:end])
        low_probs = probs.astype(jnp.bfloat16)
        grad_rows = grad_att[:, start:end]
        grad_prob = jnp.einsum(
            "bqhe,bkhe->bhqk", grad_rows, values[:, :end], preferred_element_type=jnp.float32
        )
        delta = jnp.sum(probs * grad_prob, axis=-1, keepdims=True)
        grad_score = (probs * (grad_prob - delta)).astype(jnp.bfloat16)
        grad_q.append(
            jnp.einsum(
                "bhqk,bkhe->bqhe", grad_score, keys[:, :end], preferred_element_type=jnp.float32
            )
        )
        grad_k = grad_k.at[:, :end].add(
            jnp.einsum("bhqk,bqhe->bkhe", grad_score, rows, preferred_element_type=jnp.float32)
        )
        grad_v = grad_v.at[:, :end].add(
            jnp.einsum("bhqk,bqhe->bkhe", low_probs, grad_rows, preferred_element_type=jnp.float32)
        )
    return (jnp.concatenate(grad_q, axis=1), grad_k, grad_v)


def on_device(
    tokens,
    w_qkv,
    w_out,
    w_up,
    w_down,
    norm_gains,
    norm_shifts,
    cotangent,
    corpus_ids,
    corpus_weight,
):
    batch, part, width = tokens.shape
    length = part * lax.axis_size("mp")
    local_cols = w_qkv.shape[2]
    heads = local_cols // HEAD_DIM
    qkv_flat = w_qkv.reshape(width, 3 * local_cols)
    cosine, sine = rotary_tables(length, HEAD_DIM // 2)
    factor = HEAD_DIM ** (-0.5)
    resid = tokens.astype(jnp.float32)
    normed_a, unit_0, inverse_0 = norm_forward(resid, norm_gains[0], norm_shifts[0])
    whole_a = lax.all_gather(normed_a.astype(jnp.bfloat16), "mp", axis=1, tiled=True)
    mixed = jnp.einsum("bsd,df->bsf", whole_a, qkv_flat, preferred_element_type=jnp.float32)
    query_raw = mixed[..., :local_cols].reshape(batch, length, heads, HEAD_DIM)
    key_raw = mixed[..., local_cols : 2 * local_cols].reshape(batch, length, heads, HEAD_DIM)
    value_raw = mixed[..., 2 * local_cols :].reshape(batch, length, heads, HEAD_DIM)
    queries = (factor * rotate(query_raw, cosine, sine)).astype(jnp.bfloat16)
    keys = rotate(key_raw, cosine, sine).astype(jnp.bfloat16)
    values = value_raw.astype(jnp.bfloat16)
    attended, logsum = attend_forward(queries, keys, values)
    attended = attended.reshape(batch, length, local_cols).astype(jnp.bfloat16)
    branch_a = lax.psum_scatter(
        jnp.einsum("bsf,fd->bsd", attended, w_out, preferred_element_type=jnp.float32),
        "mp",
        scatter_dimension=1,
        tiled=True,
    )
    out_a, unit_1, inverse_1 = norm_forward(branch_a, norm_gains[1], norm_shifts[1])
    middle = resid + out_a
    normed_f, unit_2, inverse_2 = norm_forward(middle, norm_gains[2], norm_shifts[2])
    whole_f = lax.all_gather(normed_f.astype(jnp.bfloat16), "mp", axis=1, tiled=True)
    hidden = jnp.einsum("bsd,df->bsf", whole_f, w_up, preferred_element_type=jnp.float32)
    active, gelu_pull = jax.vjp(jax.nn.gelu, hidden)
    active = active.astype(jnp.bfloat16)
    branch_f = lax.psum_scatter(
        jnp.einsum("bsf,fd->bsd", active, w_down, preferred_element_type=jnp.float32),
        "mp",
        scatter_dimension=1,
        tiled=True,
    )
    out_f, unit_3, inverse_3 = norm_forward(branch_f, norm_gains[3], norm_shifts[3])
    output = (middle + out_f).astype(jnp.bfloat16)
    picks = (
        corpus_ids[:, None] == jnp.arange(corpus_weight.shape[0], dtype=jnp.int32)[None, :]
    ).astype(jnp.float32)
    row_scale = jnp.dot(picks, corpus_weight, precision=lax.Precision.HIGHEST)
    grad_final = cotangent.astype(jnp.float32) * row_scale[:, None, None]
    back_3, gain_3, shift_3 = norm_backward(grad_final, unit_3, inverse_3, norm_gains[3])
    grad_branch_f = lax.all_gather(back_3.astype(jnp.bfloat16), "mp", axis=1, tiled=True)
    down_grad = jnp.einsum("bsf,bsd->fd", active, grad_branch_f, preferred_element_type=jnp.float32)
    grad_active = jnp.einsum(
        "bsd,fd->bsf", grad_branch_f, w_down, preferred_element_type=jnp.float32
    )
    grad_hidden = gelu_pull(grad_active)[0].astype(jnp.bfloat16)
    up_grad = jnp.einsum("bsd,bsf->df", whole_f, grad_hidden, preferred_element_type=jnp.float32)
    grad_normed_f = lax.psum_scatter(
        jnp.einsum("bsf,df->bsd", grad_hidden, w_up, preferred_element_type=jnp.float32),
        "mp",
        scatter_dimension=1,
        tiled=True,
    )
    back_2, gain_2, shift_2 = norm_backward(grad_normed_f, unit_2, inverse_2, norm_gains[2])
    grad_middle = grad_final + back_2
    back_1, gain_1, shift_1 = norm_backward(grad_middle, unit_1, inverse_1, norm_gains[1])
    grad_branch_a = lax.all_gather(back_1.astype(jnp.bfloat16), "mp", axis=1, tiled=True)
    out_grad = jnp.einsum(
        "bsf,bsd->fd", attended, grad_branch_a, preferred_element_type=jnp.float32
    )
    grad_attended = jnp.einsum(
        "bsd,fd->bsf", grad_branch_a, w_out, preferred_element_type=jnp.float32
    )
    grad_attended = grad_attended.astype(jnp.bfloat16).reshape(batch, length, heads, HEAD_DIM)
    grad_q, grad_k, grad_v = attend_backward(queries, keys, values, grad_attended, logsum)
    grad_q = factor * rotate_back(grad_q, cosine, sine)
    grad_k = rotate_back(grad_k, cosine, sine)
    grad_mixed = jnp.concatenate(
        [
            grad_q.reshape(batch, length, local_cols),
            grad_k.reshape(batch, length, local_cols),
            grad_v.reshape(batch, length, local_cols),
        ],
        axis=-1,
    ).astype(jnp.bfloat16)
    qkv_grad = jnp.einsum("bsd,bsf->df", whole_a, grad_mixed, preferred_element_type=jnp.float32)
    qkv_grad = qkv_grad.reshape(width, 3, local_cols)
    grad_normed_a = lax.psum_scatter(
        jnp.einsum("bsf,df->bsd", grad_mixed, qkv_flat, preferred_element_type=jnp.float32).astype(
            jnp.bfloat16
        ),
        "mp",
        scatter_dimension=1,
        tiled=True,
    ).astype(jnp.float32)
    back_0, gain_0, shift_0 = norm_backward(grad_normed_a, unit_0, inverse_0, norm_gains[0])
    input_grad = grad_middle + back_0
    gain_grad = jnp.stack([gain_0, gain_1, gain_2, gain_3])
    shift_grad = jnp.stack([shift_0, shift_1, shift_2, shift_3])
    gain_grad, shift_grad = (
        lax.psum(gain_grad.astype(jnp.bfloat16), "mp").astype(jnp.float32),
        lax.psum(shift_grad.astype(jnp.bfloat16), "mp").astype(jnp.float32),
    )
    qkv_grad, out_grad, up_grad, down_grad, gain_grad, shift_grad = (
        lax.psum(qkv_grad.astype(jnp.bfloat16), "dp").astype(jnp.float32),
        lax.psum(out_grad.astype(jnp.bfloat16), "dp").astype(jnp.float32),
        lax.psum(up_grad.astype(jnp.bfloat16), "dp").astype(jnp.float32),
        lax.psum(down_grad.astype(jnp.bfloat16), "dp").astype(jnp.float32),
        lax.psum(gain_grad.astype(jnp.bfloat16), "dp").astype(jnp.float32),
        lax.psum(shift_grad.astype(jnp.bfloat16), "dp").astype(jnp.float32),
    )
    return (output, input_grad, qkv_grad, out_grad, up_grad, down_grad, gain_grad, shift_grad)


def solution(mesh):
    placed = (
        P("dp", "mp", None),
        P(None, None, "mp"),
        P("mp", None),
        P(None, "mp"),
        P("mp", None),
        P(),
        P(),
        P("dp", "mp", None),
        P("dp"),
        P(),
    )
    return jax.shard_map(
        on_device,
        mesh=mesh,
        in_specs=placed,
        out_specs=(
            P("dp", "mp", None),
            P("dp", "mp", None),
            P(None, None, "mp"),
            P("mp", None),
            P(None, "mp"),
            P("mp", None),
            P(),
            P(),
        ),
        check_vma=False,
    )
```

profile of v0, /device:TPU:0, one launch (start us, length us, event | category | flops | bytes accessed | tf_op | source)
XLA Modules:
  0.0 1270.3 jit_solution(12614520165267679364)
XLA Ops:
  22.7 75.8 %all-gather.5.cloned.1.call-done = bf16[1,2048,1024]{2,1,0:T(8,128)(2,1)} async-done(((bf16[1,512,1024]{2,1,0:T(8,128)(2,1)}), bf16[1,2048,1024]{2,1,0:T(8,128)(2,1)}) %all-gather.5.cloned.1.call-update) | async-done | bytes 4194320 | tf_op jit(solution)/shard_map/all_gather | solution.py:136
  125.8 7.7 fusion.1
  159.5 143.1 %reduce-scatter.5.cloned.1.call-done = f32[1,512,1024]{2,1,0:T(8,128)} async-done(((f32[1,2048,1024]{2,1,0:T(8,128)}), f32[1,512,1024]{2,1,0:T(8,128)}) %reduce-scatter.5.cloned.1.call-update) | async-done | bytes 2097168 | tf_op jit(solution)/shard_map/reduce_scatter | solution.py:146
  311.6 81.6 %all-gather.7.cloned.1.call-done = bf16[1,2048,1024]{2,1,0:T(8,128)(2,1)} async-done(((bf16[1,512,1024]{2,1,0:T(8,128)(2,1)}), bf16[1,2048,1024]{2,1,0:T(8,128)(2,1)}) %all-gather.7.cloned.1.call-update) | async-done | bytes 4194320 | tf_op jit(solution)/shard_map/all_gather | solution.py:155
  393.2 6.9 fusion.39
  403.5 7.3 convolution_bitcast_fusion.1
  412.5 141.4 %reduce-scatter.7.cloned.1.call-done = f32[1,512,1024]{2,1,0:T(8,128)} async-done(((f32[1,2048,1024]{2,1,0:T(8,128)}), f32[1,512,1024]{2,1,0:T(8,128)}) %reduce-scatter.7.cloned.1.call-update) | async-done | bytes 2097168 | tf_op jit(solution)/shard_map/reduce_scatter | solution.py:159
  565.0 81.6 %all-gather.9.cloned.1.call-done = bf16[1,2048,1024]{2,1,0:T(8,128)(2,1)} async-done(((bf16[1,512,1024]{2,1,0:T(8,128)(2,1)}), bf16[1,2048,1024]{2,1,0:T(8,128)(2,1)}) %all-gather.9.cloned.1.call-update) | async-done | bytes 4194320 | tf_op jit(solution)/shard_map/all_gather | solution.py:173
  646.6 12.2 fusion.11
  667.8 143.1 %reduce-scatter.9.cloned.1.call-done = f32[1,512,1024]{2,1,0:T(8,128)} async-done(((f32[1,2048,1024]{2,1,0:T(8,128)}), f32[1,512,1024]{2,1,0:T(8,128)}) %reduce-scatter.9.cloned.1.call-update) | async-done | bytes 2097168 | tf_op jit(solution)/shard_map/reduce_scatter | solution.py:180
  822.7 9.5 fusion.104
  832.2 10.5 fusion.107
  842.7 60.8 %all-gather.11.cloned.1.call-done = bf16[1,2048,1024]{2,1,0:T(8,128)(2,1)} async-done(((bf16[1,512,1024]{2,1,0:T(8,128)(2,1)}), bf16[1,2048,1024]{2,1,0:T(8,128)(2,1)}) %all-gather.11.cloned.1.call-update) | async-done | bytes 4194320 | tf_op jit(solution)/shard_map/all_gather | solution.py:189
  927.6 11.8 multiply_reduce_fusion.1
  939.5 9.4 fusion.60
  948.9 11.4 multiply_reduce_fusion
  960.4 7.1 fusion.75
  969.1 9.2 multiply_convert_fusion.2
  987.4 9.5 multiply_convert_fusion.1
  1006.5 8.3 multiply_convert_fusion
  1038.8 96.2 %all-reduce.7.cloned.1.call-done = (bf16[1024,3,256]{2,0,1:T(8,128)(2,1)}, bf16[256,1024]{1,0:T(8,128)(2,1)}, bf16[1024,1024]{1,0:T(8,128)(2,1)}, bf16[1024,1024]{1,0:T(8,128)(2,1)}) async-done(((bf16[1024,3,256]{2,0,1:T(8,128)(2,1)}, bf16[256,1024]{1,0:T(8,128)(2,1)}, bf16[1024,1024]{1,0:T(8,128)(2,1)}, bf16[1024,1024]{1,0:T(8,128)(2,1)}), (bf16[1024,3,256]{2,0,1:T(8,128)(2,1)}, ...) | async-done | bytes 6291472 | tf_op jit(solution)/shard_map/psum | solution.py:227
  1145.6 68.7 %reduce-scatter.11.cloned.1.call-done = bf16[1,512,1024]{2,1,0:T(8,128)(2,1)} async-done(((bf16[1,2048,1024]{2,1,0:T(8,128)(2,1)}), bf16[1,512,1024]{2,1,0:T(8,128)(2,1)}) %reduce-scatter.11.cloned.1.call-update) | async-done | bytes 1048592 | tf_op jit(solution)/shard_map/reduce_scatter | solution.py:210
  1218.2 18.0 %all-reduce.4 = (bf16[4,1024]{1,0:T(4,128)(2,1)S(1)}, bf16[4,1024]{1,0:T(4,128)(2,1)S(1)}) all-reduce(bf16[4,1024]{1,0:T(4,128)(2,1)S(1)} %pad_maximum_fusion.8, bf16[4,1024]{1,0:T(4,128)(2,1)S(1)} %pad_maximum_fusion.9), channel_id=1, replica_groups=mesh['dp'=8,'mp'=4] {'mp'}, use_global_device_ids=true, to_apply=%region_40.41 | all-reduce | flops 8192 | bytes 32768 | tf_op jit(solution)/shard_map/psum | solution.py:223
  1236.1 22.3 %all-reduce.2 = (bf16[4,1024]{1,0:T(4,128)(2,1)S(1)}, bf16[4,1024]{1,0:T(4,128)(2,1)S(1)}) all-reduce(bf16[4,1024]{1,0:T(4,128)(2,1)S(1)} %get-tuple-element.141, bf16[4,1024]{1,0:T(4,128)(2,1)S(1)} %get-tuple-element.142), channel_id=1, replica_groups=mesh['dp'=8,'mp'=4] {'dp'}, use_global_device_ids=true, to_apply=%region_41.42 | all-reduce | flops 8192 | bytes 32768 | tf_op jit(solution)/shard_map/psum | solution.py:231
  (307 shorter events, 201.0 us)
Async XLA Ops:
  7.2 396.3 %copy-start = (bf16[1024,1024]{1,0:T(8,128)(2,1)S(1)}, bf16[1024,1024]{1,0:T(8,128)(2,1)}, u32[]{:S(2)}) copy-start(bf16[1024,1024]{1,0:T(8,128)(2,1)} %param.34) | copy-start | bytes 6291460
  7.2 91.4 %all-gather.5.cloned.1.call-start = ((), (), s32[]{:S(2)}) async-start(), calls=%async_computation.4 | async-start | bytes 5242880 | tf_op jit(solution)/shard_map/all_gather | solution.py:136
  14.9 287.6 %reduce-scatter.5.cloned.1.call-start = ((), (), s32[]{:S(2)}) async-start(), calls=%async_computation.5 | async-start | bytes 10485760 | tf_op jit(solution)/shard_map/reduce_scatter | solution.py:146
  17.7 93.5 %copy-start.29 = (pred[512,512]{0,1:T(8,128)(4,1)}, pred[512,512]{0,1:T(8,128)(4,1)S(1)}, u32[]{:S(2)}) copy-start(pred[512,512]{0,1:T(8,128)(4,1)S(1)} %iota_compare_fusion.3) | copy-start | bytes 786436
  104.4 43.4 %copy-start.24 = (bf16[1,2048,256]{1,2,0:T(8,128)(2,1)}, bf16[1,2048,256]{1,2,0:T(8,128)(2,1)S(1)}, u32[]{:S(2)}) copy-start(bf16[1,2048,256]{1,2,0:T(8,128)(2,1)S(1)} %slice.461) | copy-start | bytes 3145732
  106.5 33.3 %copy-start.12 = (bf16[1,2048,4,32]{1,3,2,0:T(8,128)(2,1)}, bf16[1,2048,4,32]{1,3,2,0:T(8,128)(2,1)S(1)}, u32[]{:S(2)}) copy-start(bf16[1,2048,4,32]{1,3,2,0:T(8,128)(2,1)S(1)} %get-tuple-element.160) | copy-start | bytes 1572868
  114.3 39.7 %copy-start.47 = (bf16[4,64,512]{2,1,0:T(8,128)(2,1)}, bf16[4,64,512]{2,1,0:T(8,128)(2,1)S(1)}, u32[]{:S(2)}) copy-start(bf16[4,64,512]{2,1,0:T(8,128)(2,1)S(1)} %fusion.131) | copy-start | bytes 786436
  119.1 35.0 %copy-start.49 = (bf16[4,64,512]{2,1,0:T(8,128)(2,1)}, bf16[4,64,512]{2,1,0:T(8,128)(2,1)S(1)}, u32[]{:S(2)}) copy-start(bf16[4,64,512]{2,1,0:T(8,128)(2,1)S(1)} %fusion.130) | copy-start | bytes 786436
  159.4 233.8 %all-gather.7.cloned.1.call-start = ((), (), s32[]{:S(2)}) async-start(), calls=%async_computation.6 | async-start | bytes 5242880 | tf_op jit(solution)/shard_map/all_gather | solution.py:155
  311.6 242.4 %reduce-scatter.7.cloned.1.call-start = ((), (), s32[]{:S(2)}) async-start(), calls=%async_computation.7 | async-start | bytes 10485760 | tf_op jit(solution)/shard_map/reduce_scatter | solution.py:159
  410.8 235.8 %all-gather.9.cloned.1.call-start = ((), (), s32[]{:S(2)}) async-start(), calls=%async_computation.8 | async-start | bytes 5242880 | tf_op jit(solution)/shard_map/all_gather | solution.py:173
  565.0 246.0 %reduce-scatter.9.cloned.1.call-start = ((), (), s32[]{:S(2)}) async-start(), calls=%async_computation.9 | async-start | bytes 10485760 | tf_op jit(solution)/shard_map/reduce_scatter | solution.py:180
  667.8 143.2 %copy-start.8 = (f32[1,512,1024]{2,1,0:T(8,128)S(1)}, f32[1,512,1024]{2,1,0:T(8,128)}, u32[]{:S(2)}) copy-start(f32[1,512,1024]{2,1,0:T(8,128)} %copy-done.6) | copy-start | bytes 6291460
  667.8 235.6 %all-gather.11.cloned.1.call-start = ((), (), s32[]{:S(2)}) async-start(), calls=%async_computation.10 | async-start | bytes 5242880 | tf_op jit(solution)/shard_map/all_gather | solution.py:189
  821.8 313.2 %all-reduce.7.cloned.1.call-start = ((), (), s32[]{:S(2)}) async-start(), calls=%async_computation.12 | async-start | bytes 12582912 | tf_op jit(solution)/shard_map/psum | solution.py:227
  822.0 105.6 %copy-start.55 = (f32[4,512]{1,0:T(4,128)}, f32[4,512]{1,0:T(4,128)S(1)}, u32[]{:S(2)}) copy-start(f32[4,512]{1,0:T(4,128)S(1)} %log_add_fusion.1) | copy-start | bytes 24580
  832.2 71.2 %copy-start.46 = (bf16[256,1024]{1,0:T(8,128)(2,1)S(1)}, bf16[256,1024]{1,0:T(8,128)(2,1)}, u32[]{:S(2)}) copy-start(bf16[256,1024]{1,0:T(8,128)(2,1)} %param.32) | copy-start | bytes 1572868
  842.7 64.4 %copy-start.30 = (pred[512,512]{0,1:T(8,128)(4,1)S(1)}, pred[512,512]{0,1:T(8,128)(4,1)}, u32[]{:S(2)}) copy-start(pred[512,512]{0,1:T(8,128)(4,1)} %copy-done.29) | copy-start | bytes 786436
  1031.5 182.7 %reduce-scatter.11.cloned.1.call-start = ((), (), s32[]{:S(2)}) async-start(), calls=%async_computation.11 | async-start | bytes 5242880 | tf_op jit(solution)/shard_map/reduce_scatter | solution.py:210
  1143.1 72.6 %copy-start.11 = (bf16[1,512,1024]{2,1,0:T(8,128)(2,1)S(1)}, bf16[1,512,1024]{2,1,0:T(8,128)(2,1)}, u32[]{:S(2)}) copy-start(bf16[1,512,1024]{2,1,0:T(8,128)(2,1)} %param.30) | copy-start | bytes 3145732
  1143.1 72.6 %copy-start.59 = (f32[1,1024]{1,0:T(1,128)S(1)}, f32[1,1024]{1,0:T(1,128)}, u32[]{:S(2)}) copy-start(f32[1,1024]{1,0:T(1,128)} %copy-done.58) | copy-start | bytes 12292
  1143.1 72.6 %copy-start.61 = (f32[512]{0:T(512)S(1)}, f32[512]{0:T(512)}, u32[]{:S(2)}) copy-start(f32[512]{0:T(512)} %copy-done.60) | copy-start | bytes 6148
  1143.1 72.6 %copy-start.65 = (f32[512]{0:T(512)S(1)}, f32[512]{0:T(512)}, u32[]{:S(2)}) copy-start(f32[512]{0:T(512)} %copy-done.64) | copy-start | bytes 6148
  1215.7 47.9 %copy-start.1 = (bf16[1024,1024]{1,0:T(8,128)(2,1)S(1)}, bf16[1024,1024]{1,0:T(8,128)(2,1)}, u32[]{:S(2)}) copy-start(bf16[1024,1024]{1,0:T(8,128)(2,1)} %param.34) | copy-start | bytes 6291460
  (73 other events, 458.5 us)
Sparse Core Ops, SparseCore 0:
  15.1 83.4 all-gather.4
  159.5 142.9 reduce-scatter.4
  311.7 81.4 all-gather.6
  410.9 142.9 reduce-scatter.6
  565.1 81.4 all-gather.8
  667.9 142.9 reduce-scatter.8
  821.9 81.4 all-gather.10
  1031.6 103.2 all-reduce.6
  1137.4 76.8 reduce-scatter.10
where the time goes:
time: 1280 us; the launch traced here: 1270 us
  waiting for transfers between devices  892 us (70%)
  matrix products  189 us (15%)
  other arithmetic  106 us (8%)
  blocking collectives  40.3 us (3%)
  local copies, waits for them, and re-layouts  26 us (2%)
  between operations  15.8 us (1%)
    reduce_scatter x1, waiting for transfers between devices, on_device(): lax.psum_scatter(jnp.einsum('bsf,fd->bsd', attended, w_out, preferred_ele...  143 us
    reduce_scatter x1, waiting for transfers between devices, on_device(): lax.psum_scatter(jnp.einsum('bsf,df->bsd', grad_hidden, w_up, preferred_e...  143 us
    reduce_scatter x1, waiting for transfers between devices, on_device(): lax.psum_scatter(jnp.einsum('bsf,fd->bsd', active, w_down, preferred_elem...  141 us
    psum x1, waiting for transfers between devices, on_device(): lax.psum(qkv_grad.astype(jnp.bfloat16), 'dp').astype(jnp.float32)  96.2 us
    all_gather x1, waiting for transfers between devices, on_device(): lax.all_gather(normed_f.astype(jnp.bfloat16), 'mp', axis=1, tiled=True)  81.6 us
    all_gather x1, waiting for transfers between devices, on_device(): lax.all_gather(back_3.astype(jnp.bfloat16), 'mp', axis=1, tiled=True)  81.6 us
    all_gather x1, waiting for transfers between devices, on_device(): lax.all_gather(normed_a.astype(jnp.bfloat16), 'mp', axis=1, tiled=True)  75.8 us
    reduce_scatter x1, waiting for transfers between devices, on_device(): lax.psum_scatter(jnp.einsum('bsf,df->bsd', grad_mixed, qkv_flat, preferre...  68.7 us
  transfers between devices with their start and end apart: 9, of which 9 were waited for; matrix products, arithmetic and copies ran while one was open for 4% of the time, Pallas kernels for 0%

commit v1 on v0

v1 whole, which is shorter than its diff:
```python
import functools

import jax
import jax.numpy as jnp
from jax import lax
from jax.experimental import pallas as pl
from jax.experimental.pallas import tpu as pltpu
from jax.sharding import Mesh, PartitionSpec as P

HEAD_DIM = 64
BLOCK = 512
EPS = 1e-05
LOG2E = 1.4426950408889634
NN = (((1,), (0,)), ((), ()))
NT = (((1,), (1,)), ((), ()))
TN = (((0,), (0,)), ((), ()))
f32 = jnp.float32
bf16 = jnp.bfloat16


def head_lanes(shape, head):
    return lax.broadcasted_iota(jnp.int32, shape, 1) // HEAD_DIM == head


def swap_halves(value, sign):
    half = HEAD_DIM // 2
    width = value.shape[1]
    first = (lax.broadcasted_iota(jnp.int32, value.shape, 1) // half) % 2 == 0
    return jnp.where(
        first, sign * pltpu.roll(value, width - half, 1), -sign * pltpu.roll(value, half, 1)
    )


def qkv_kernel(place_ref, x_ref, w_ref, gain_ref, shift_ref, cos_ref, sin_ref, *refs):
    q_ref, k_ref, v_ref, normed_ref = refs[-4:]
    width = q_ref.shape[1]
    value = x_ref[...].astype(f32)
    center = value - jnp.mean(value, axis=1, keepdims=True)
    inverse = lax.rsqrt(jnp.mean(center * center, axis=1, keepdims=True) + EPS)
    normed = (center * inverse * gain_ref[...] + shift_ref[...]).astype(bf16)
    normed_ref[...] = normed
    mixed = jnp.dot(normed, w_ref[...], preferred_element_type=f32)
    cosine, sine = cos_ref[...], sin_ref[...]
    query, key = mixed[:, :width], mixed[:, width : 2 * width]
    query = HEAD_DIM ** (-0.5) * (query * cosine + swap_halves(query, -1.0) * sine)
    q_ref[...] = query.astype(bf16)
    k_ref[...] = (key * cosine + swap_halves(key, -1.0) * sine).astype(bf16)
    v_ref[...] = mixed[:, 2 * width :].astype(bf16)


def project(place, x, w, gain, shift, cosine, sine, length, filled, rows=256):
    part, depth = x.shape
    width = w.shape[1] // 3
    steps = part // rows

    def there(i, place_ref):
        return (place_ref[0] * steps + i, 0)

    def whole(i, place_ref):
        return (0, 0)

    return pl.pallas_call(
        qkv_kernel,
        out_shape=tuple(
            jax.ShapeDtypeStruct((length, n), bf16) for n in (width, width, width, depth)
        ),
        grid_spec=pltpu.PrefetchScalarGridSpec(
            num_scalar_prefetch=1,
            grid=(steps,),
            in_specs=[
                pl.BlockSpec((rows, depth), lambda i, place_ref: (i, 0)),
                pl.BlockSpec(w.shape, whole),
                pl.BlockSpec((1, depth), whole),
                pl.BlockSpec((1, depth), whole),
                pl.BlockSpec((rows, width), there),
                pl.BlockSpec((rows, width), there),
            ]
            + [pl.BlockSpec(memory_space=pl.ANY)] * len(filled),
            out_specs=tuple(pl.BlockSpec((rows, n), there) for n in (width, width, width, depth)),
        ),
        input_output_aliases={7 + i: i for i in range(len(filled))},
        compiler_params=pltpu.CompilerParams(vmem_limit_bytes=40 * 2**20),
        cost_estimate=pl.CostEstimate(
            flops=2 * part * depth * 3 * width, bytes_accessed=5 * 2**20, transcendentals=0
        ),
    )(place, x, w, gain, shift, cosine, sine, *filled)


def forward_kernel(q_ref, k_ref, v_ref, o_ref, lse_ref, *, rows, blocks):
    width = q_ref.shape[1]
    heads = width // HEAD_DIM

    def branch(last):
        n = (last + 1) * rows
        acc = jnp.zeros((rows, width), f32)
        logs = jnp.zeros((rows, width), f32)
        for h in range(heads):
            mine = head_lanes((rows, width), h)
            qm = jnp.where(mine, q_ref[...], jnp.zeros((), bf16))
            s = lax.dot_general(qm, k_ref[:n], NT, preferred_element_type=f32)
            row = lax.broadcasted_iota(jnp.int32, (rows, rows), 0)
            column = lax.broadcasted_iota(jnp.int32, (rows, rows), 1)
            tail = jnp.where(column <= row, s[:, n - rows :], -1e30)
            top = jnp.max(tail, axis=1, keepdims=True)
            if last:
                top = jnp.maximum(top, jnp.max(s[:, : n - rows], axis=1, keepdims=True))
            top = top * LOG2E
            vm = jnp.where(head_lanes((n, width), h), v_ref[:n], jnp.ones((), bf16))
            low = jnp.exp2(tail * LOG2E - top).astype(bf16)
            out = lax.dot_general(low, vm[n - rows :], NN, preferred_element_type=f32)
            if last:
                low = jnp.exp2(s[:, : n - rows] * LOG2E - top).astype(bf16)
                out = out + lax.dot_general(low, vm[: n - rows], NN, preferred_element_type=f32)
            total = pltpu.roll(out, HEAD_DIM, 1)
            acc = jnp.where(mine, out / total, acc)
            logs = jnp.where(mine, top + jnp.log2(total), logs)
        o_ref[...] = acc.astype(bf16)
        lane = lax.broadcasted_iota(jnp.int32, (8, width), 1)
        pick = (lane == HEAD_DIM * lax.broadcasted_iota(jnp.int32, (8, width), 0)).astype(f32)
        lse_ref[...] = lax.dot_general(
            pick, logs, NT, precision=lax.Precision.HIGHEST, preferred_element_type=f32
        )

    for i in range(blocks):
        pl.when(pl.program_id(0) == i)(functools.partial(branch, i))


def attend_forward(q, k, v, rows=BLOCK):
    length, width = q.shape
    blocks = length // rows
    return pl.pallas_call(
        functools.partial(forward_kernel, rows=rows, blocks=blocks),
        grid=(blocks,),
        out_shape=(
            jax.ShapeDtypeStruct((length, width), bf16),
            jax.ShapeDtypeStruct((8, length), f32),
        ),
        in_specs=[
            pl.BlockSpec((rows, width), lambda i: (i, 0)),
            pl.BlockSpec((length, width), lambda i: (0, 0)),
            pl.BlockSpec((length, width), lambda i: (0, 0)),
        ],
        out_specs=(
            pl.BlockSpec((rows, width), lambda i: (i, 0)),
            pl.BlockSpec((8, rows), lambda i: (0, i)),
        ),
        compiler_params=pltpu.CompilerParams(vmem_limit_bytes=48 * 2**20),
        cost_estimate=pl.CostEstimate(
            flops=20_000_000_000, bytes_accessed=6 * 2**20, transcendentals=0
        ),
    )(q, k, v)


def backward_kernel(
    q_ref, k_ref, v_ref, o_ref, do_ref, lse_ref, cos_ref, sin_ref, out_ref, dq, delta, *, rows
):
    length, width = q_ref.shape
    heads = width // HEAD_DIM
    blocks = length // rows
    lane_head = lax.broadcasted_iota(jnp.int32, (8, width), 1) // HEAD_DIM
    marks = (lane_head == lax.broadcasted_iota(jnp.int32, (8, width), 0)).astype(f32)

    def span(i):
        return pl.ds(pl.multiple_of(i * rows, rows), rows)

    @pl.loop(0, blocks)
    def _(i):
        product = do_ref[span(i)].astype(f32) * o_ref[span(i)].astype(f32)
        delta[:, span(i)] = lax.dot_general(
            marks, product, NT, precision=lax.Precision.HIGHEST, preferred_element_type=f32
        )

    dq[...] = jnp.zeros_like(dq)

    def tile(i, j, diagonal):
        at = span(i)
        keys, values = k_ref[span(j)], v_ref[span(j)]
        queries, grads = q_ref[at], do_ref[at]
        dk = jnp.zeros((rows, width), f32)
        dv = jnp.zeros((rows, width), f32)
        dqi = dq[at]
        zero = jnp.zeros((), bf16)
        for h in range(heads):
            mine = head_lanes((rows, width), h)
            qm = jnp.where(mine, queries, zero)
            dom = jnp.where(mine, grads, zero)
            km = jnp.where(mine, keys, zero)
            st = lax.dot_general(keys, qm, NT, preferred_element_type=f32)
            pt = jnp.exp2(st * LOG2E - lse_ref[h : h + 1, at])
            if diagonal:
                key = lax.broadcasted_iota(jnp.int32, (rows, rows), 0)
                query = lax.broadcasted_iota(jnp.int32, (rows, rows), 1)
                pt = jnp.where(key <= query, pt, 0.0)
            dpt = lax.dot_general(values, dom, NT, preferred_element_type=f32)
            dst = (pt * (dpt - delta[h : h + 1, at])).astype(bf16)
            dv = dv + jnp.dot(pt.astype(bf16), dom, preferred_element_type=f32)
            dk = dk + jnp.dot(dst, qm, preferred_element_type=f32)
            dqi = dqi + lax.dot_general(dst, km, TN, preferred_element_type=f32)
        dq[at] = dqi
        return dk, dv

    def turn_back(grad, at):
        return grad * cos_ref[at] + swap_halves(grad, 1.0) * sin_ref[at]

    @pl.loop(0, blocks)
    def _(j):
        def more(i, carry):
            dk, dv = tile(i, j, False)
            return carry[0] + dk, carry[1] + dv

        dk, dv = lax.fori_loop(j + 1, blocks, more, tile(j, j, True))
        out_ref[span(j), width : 2 * width] = turn_back(dk, span(j)).astype(bf16)
        out_ref[span(j), 2 * width :] = dv.astype(bf16)

    @pl.loop(0, blocks)
    def _(i):
        turned = turn_back(dq[span(i)], span(i))
        out_ref[span(i), :width] = (HEAD_DIM ** (-0.5) * turned).astype(bf16)


def attend_backward(q, k, v, o, do, lse, cosine, sine, rows=BLOCK):
    length, width = q.shape
    vmem = pl.BlockSpec(memory_space=pltpu.VMEM)
    return pl.pallas_call(
        functools.partial(backward_kernel, rows=rows),
        out_shape=jax.ShapeDtypeStruct((length, 3 * width), bf16),
        in_specs=[vmem] * 8,
        out_specs=vmem,
        scratch_shapes=[pltpu.VMEM((length, width), f32), pltpu.VMEM((8, length), f32)],
        compiler_params=pltpu.CompilerParams(vmem_limit_bytes=56 * 2**20),
        cost_estimate=pl.CostEstimate(
            flops=45_000_000_000, bytes_accessed=12 * 2**20, transcendentals=0
        ),
    )(q, k, v, o, do, lse, cosine, sine)


def norm_forward(value, gain, shift):
    center = value - jnp.mean(value, axis=-1, keepdims=True)
    inverse = lax.rsqrt(jnp.mean(center * center, axis=-1, keepdims=True) + EPS)
    unit = center * inverse
    return (unit * gain + shift, unit, inverse)


def norm_backward(grad, unit, inverse, gain):
    scaled = grad * gain
    back = inverse * (
        scaled
        - jnp.mean(scaled, axis=-1, keepdims=True)
        - unit * jnp.mean(scaled * unit, axis=-1, keepdims=True)
    )
    return (back, jnp.sum(grad * unit, axis=0), jnp.sum(grad, axis=0))


def rotary_tables(length, width):
    half = HEAD_DIM // 2
    lane = jnp.arange(width, dtype=jnp.int32) % half
    freqs = 10000.0 ** (-(lane.astype(f32) / half))
    angles = jnp.arange(length, dtype=f32)[:, None] * freqs[None, :]
    return (jnp.cos(angles), jnp.sin(angles))


SWAP = [(0, 1), (1, 0)]


def dot(left, right, dims=NN):
    return lax.dot_general(left, right, dims, preferred_element_type=f32)


def across(value, axis):
    return lax.ppermute(value, axis, SWAP)


def turn(value):
    return lax.ppermute(value, ("b", "h"), [(0, 0), (1, 2), (2, 1), (3, 3)])


def quad_swap(value, far_b, far_l):
    mask = 2 * far_b + far_l
    return lax.ppermute(value, ("b", "l"), [(i, i ^ mask) for i in range(4)])


def gather_axis(value, axis, dim=0):
    other = across(value, axis)
    first = lax.axis_index(axis) == 0
    return jnp.where(
        first, jnp.concatenate([value, other], dim), jnp.concatenate([other, value], dim)
    )


def scatter_axis(value, axis):
    low, high = jnp.split(value.astype(f32), 2, axis=0)
    first = lax.axis_index(axis) == 0
    kept = jnp.where(first, low, high)
    sent = jnp.where(first, high, low).astype(bf16)
    return kept + across(sent, axis).astype(f32)


def on_device(
    tokens,
    w_qkv,
    w_out,
    w_up,
    w_down,
    norm_gains,
    norm_shifts,
    cotangent,
    corpus_ids,
    corpus_weight,
    *,
    groups,
):
    _, part, depth = tokens.shape
    cols = w_qkv.shape[2]
    units = w_up.shape[1]
    core, half, near = lax.axis_index("b"), lax.axis_index("h"), lax.axis_index("l")
    length = 4 * part
    place = 2 * core + near
    group = jnp.int32(0)
    for axis in groups:
        group = 2 * group + lax.axis_index(axis)
    n_groups = 2 ** len(groups)
    stack = ("h", "l")
    cosine, sine = rotary_tables(length, cols)
    gains = [norm_gains[i : i + 1] for i in range(4)]
    shifts = [norm_shifts[i : i + 1] for i in range(4)]

    resid_low = turn(tokens[0])
    w_attn = turn(w_qkv.reshape(depth, 3 * cols))
    near_block = across(resid_low, "l")
    blocks = [resid_low, across(resid_low, "b"), near_block, across(near_block, "b")]

    slice_out = cols // (2 * n_groups)
    out_piece = lax.dynamic_slice_in_dim(w_out, (2 * group + core) * slice_out, slice_out, 0)
    out_whole = lax.all_gather(out_piece, stack + groups + ("b",), axis=0, tiled=True)
    slice_unit = units // (2 * n_groups)
    unit_at = (core * n_groups + group) * slice_unit
    up_piece = lax.dynamic_slice_in_dim(w_up, unit_at, slice_unit, 1)
    down_piece = lax.dynamic_slice_in_dim(w_down, unit_at, slice_unit, 0)
    up_half = lax.all_gather(up_piece, stack + groups, axis=1, tiled=True)
    down_half = lax.all_gather(down_piece, stack + groups, axis=0, tiled=True)

    filled = ()
    for mask, block in zip((0, 2, 1, 3), blocks):
        filled = project(
            jnp.reshape(place ^ mask, (1,)),
            block,
            w_attn,
            gains[0],
            shifts[0],
            cosine,
            sine,
            length,
            filled,
        )
    q, k, v, whole_a = filled
    attended, lse = attend_forward(q, k, v)

    def block_of(value, mask):
        return lax.dynamic_slice_in_dim(value, (place ^ mask) * part, part, 0)

    def out_rows(mask):
        return lax.dynamic_slice_in_dim(out_whole, (place ^ mask) * cols, cols, 0)

    heads = {0: block_of(attended, 0)}
    for mask in (1, 3, 2):
        heads[mask] = quad_swap(block_of(attended, mask), mask // 2, mask % 2)
    branch_a = sum(dot(heads[mask], out_rows(mask)) for mask in (0, 2, 1, 3))

    resid = resid_low.astype(f32)
    normed_a, unit_0, inverse_0 = norm_forward(resid, gains[0], shifts[0])
    out_a, unit_1, inverse_1 = norm_forward(branch_a, gains[1], shifts[1])
    middle = resid + out_a
    normed_f, unit_2, inverse_2 = norm_forward(middle, gains[2], shifts[2])
    own_f = normed_f.astype(bf16)
    pair_f = jnp.concatenate([own_f, across(own_f, "b")], axis=0)
    hidden = dot(pair_f, up_half)
    cube = 0.7978845608028654 * (hidden + 0.044715 * hidden * hidden * hidden)
    bend = jnp.tanh(cube)
    active = (0.5 * hidden * (1.0 + bend)).astype(bf16)
    slope = 0.5 * (1.0 + bend) + 0.5 * hidden * (1.0 - bend * bend) * 0.7978845608028654 * (
        1.0 + 3 * 0.044715 * hidden * hidden
    )
    slope = slope.astype(bf16)
    branch_f = dot(active[part:], down_half).astype(bf16)
    branch_f = dot(active[:part], down_half) + across(branch_f, "b").astype(f32)
    out_f, unit_3, inverse_3 = norm_forward(branch_f, gains[3], shifts[3])
    output = turn((middle + out_f).astype(bf16))

    picks = (
        corpus_ids[:, None] == jnp.arange(corpus_weight.shape[0], dtype=jnp.int32)[None, :]
    ).astype(f32)
    row_scale = turn(jnp.dot(picks, corpus_weight, precision=lax.Precision.HIGHEST))
    grad_final = turn(cotangent[0]).astype(f32) * row_scale[:, None]
    back_3, gain_3, shift_3 = norm_backward(grad_final, unit_3, inverse_3, gains[3])
    own_g = back_3.astype(bf16)
    pair_g = jnp.concatenate([own_g, across(own_g, "b")], axis=0)
    grad_active = dot(pair_g, down_half, NT)
    grad_hidden = (slope.astype(f32) * grad_active).astype(bf16)
    down_grad = dot(active, pair_g, TN).astype(bf16)
    up_grad = dot(pair_f, grad_hidden, TN).astype(bf16)
    down_sum = lax.psum_scatter(down_grad, stack + groups, scatter_dimension=0, tiled=True)
    up_sum = lax.psum_scatter(up_grad, stack + groups, scatter_dimension=1, tiled=True)
    down_grad = lax.all_gather(down_sum, ("b",) + groups, axis=0, tiled=True).astype(f32)
    up_grad = lax.all_gather(up_sum, ("b",) + groups, axis=1, tiled=True).astype(f32)

    grad_f = dot(grad_hidden[part:], up_half, NT).astype(bf16)
    grad_f = dot(grad_hidden[:part], up_half, NT) + across(grad_f, "b").astype(f32)
    back_2, gain_2, shift_2 = norm_backward(grad_f, unit_2, inverse_2, gains[2])
    grad_middle = grad_final + back_2
    back_1, gain_1, shift_1 = norm_backward(grad_middle, unit_1, inverse_1, gains[1])
    grad_a = back_1.astype(bf16)
    grad_attended = jnp.zeros((length, cols), bf16)
    for mask in (3, 1, 2, 0):
        sent = dot(grad_a, out_rows(mask), NT).astype(bf16)
        if mask:
            sent = quad_swap(sent, mask // 2, mask % 2)
        grad_attended = lax.dynamic_update_slice_in_dim(
            grad_attended, sent, (place ^ mask) * part, 0
        )
    out_grad = jnp.zeros((4 * cols, depth), bf16)
    for mask in range(4):
        out_grad = lax.dynamic_update_slice_in_dim(
            out_grad, dot(heads[mask], grad_a, TN).astype(bf16), (place ^ mask) * cols, 0
        )
    out_sum = lax.psum_scatter(
        out_grad, stack + groups + ("b",), scatter_dimension=0, tiled=True
    )
    out_grad = lax.all_gather(out_sum, groups + ("b",), axis=0, tiled=True).astype(f32)

    grad_mixed = attend_backward(q, k, v, attended, grad_attended, lse, cosine, sine)

    pair = 2 * part
    sent = lax.dynamic_slice_in_dim(grad_mixed, (1 - core) * pair, pair, 0)
    from_core = across(dot(sent, w_attn, NT).astype(bf16), "b")
    sent = dot(block_of(grad_mixed, 1), w_attn, NT)
    sent = sent + lax.dynamic_slice_in_dim(from_core, (1 - near) * part, part, 0).astype(f32)
    from_near = across(sent.astype(bf16), "l")
    grad_normed_a = dot(block_of(grad_mixed, 0), w_attn, NT)
    grad_normed_a = grad_normed_a + lax.dynamic_slice_in_dim(
        from_core, near * part, part, 0
    ).astype(f32)
    grad_normed_a = grad_normed_a + from_near.astype(f32)

    qkv_grad = dot(whole_a, grad_mixed, TN)
    for axis in groups:
        qkv_grad = scatter_axis(qkv_grad, axis)
    qkv_grad = turn(qkv_grad.astype(bf16))
    qkv_grad = scatter_axis(qkv_grad, "b").astype(bf16)
    qkv_grad = gather_axis(qkv_grad, "b")
    for axis in reversed(groups):
        qkv_grad = gather_axis(qkv_grad, axis)
    qkv_grad = qkv_grad.astype(f32).reshape(depth, 3, cols)

    back_0, gain_0, shift_0 = norm_backward(grad_normed_a, unit_0, inverse_0, gains[0])
    input_grad = turn((grad_middle + back_0).astype(bf16)).astype(f32)
    norm_grads = jnp.stack([gain_0, gain_1, gain_2, gain_3, shift_0, shift_1, shift_2, shift_3])
    norm_grads = lax.psum(norm_grads, groups + ("b",) + stack)
    return (
        output[None],
        input_grad[None],
        qkv_grad,
        out_grad,
        up_grad,
        down_grad,
        norm_grads[:4],
        norm_grads[4:],
    )


def solution(mesh):
    rows, parts = mesh.shape["dp"], mesh.shape["mp"]
    bits = (rows // 2).bit_length() - 1
    assert parts == 4 and rows == 2 ** (bits + 1)
    groups = tuple(f"g{i}" for i in range(bits))
    fine = Mesh(mesh.devices.reshape((2,) * (bits + 3)), groups + ("b", "h", "l"))
    dp, mp = groups + ("b",), ("h", "l")
    placed = (
        P(dp, mp, None),
        P(None, None, mp),
        P(mp, None),
        P(None, mp),
        P(mp, None),
        P(),
        P(),
        P(dp, mp, None),
        P(dp),
        P(),
    )
    return jax.shard_map(
        functools.partial(on_device, groups=groups),
        mesh=fine,
        in_specs=placed,
        out_specs=(
            P(dp, mp, None),
            P(dp, mp, None),
            P(None, None, mp),
            P(mp, None),
            P(None, mp),
            P(mp, None),
            P(),
            P(),
        ),
        check_vma=False,
    )
```

time: 1280 us -> 751 us (0.59)
  waiting for transfers between devices: 892 us -> 277 us
  starting transfers between devices: 0.95 us -> 130 us
  matrix products: 189 us -> 94 us
  Pallas kernels: 0 us -> 93.8 us
  other arithmetic: 106 us -> 41.4 us
    reduce_scatter x4 -> x2, waiting for transfers between devices: 496 us -> 40.7 us  [the longest x1 40.7 us: on_device(): lax.psum_scatter(out_grad, stack + groups + ('b',), scatter_dimension=0,...]
    all_gather x4 -> x5, waiting for transfers between devices: 300 us -> 116 us  [the longest x1 64.7 us: on_device(): down_half = lax.all_gather(down_piece, stack + groups, axis=0, tiled=True)]
    ppermute x0 -> x28, starting transfers between devices: none -> 129 us  [the longest x15 73.1 us: across(): return lax.ppermute(value, axis, SWAP)]
    ppermute x0 -> x28, waiting for transfers between devices: none -> 120 us  [the longest x15 86.9 us: across(): return lax.ppermute(value, axis, SWAP)]
    psum x1 -> x0, waiting for transfers between devices: 96.2 us -> none  [on_device(): lax.psum(qkv_grad.astype(jnp.bfloat16), 'dp').astype(jnp.float32)]
    dot_general x36 -> x24, matrix products: 189 us -> 94 us  [dot(): return lax.dot_general(left, right, dims, preferred_element_type=f32)]
    pallas_call x0 -> x6, Pallas kernels: none -> 93.8 us  [the longest x1 45.1 us: attend_backward(): pl.pallas_call(functools.partial(backward_kernel, rows=rows), out_shape=j...]
    convert_element_type x15 -> x14, other arithmetic: 48.7 us -> 17.3 us  [the longest x1 4.22 us: on_device(): lax.all_gather(down_sum, ('b',) + groups, axis=0, tiled=True).astype(f32)]
  transfers between devices with their start and end apart: 9 -> 36, of which waited for: 9 -> 16; matrix products, arithmetic and copies ran while one was open for 4% -> 17% of each run, Pallas kernels for 0% -> 13%
where the time goes in v1:
time: 751 us; the launch traced here: 742 us
  waiting for transfers between devices  277 us (37%)
  starting transfers between devices  130 us (17%)
  matrix products  94 us (13%)
  Pallas kernels  93.8 us (12%)
  blocking collectives  51.6 us (7%)
  other arithmetic  41.4 us (6%)
  local copies, waits for them, and re-layouts  38.5 us (5%)
  between operations  15.9 us (2%)
    dot_general x24, matrix products, dot(): return lax.dot_general(left, right, dims, preferred_element_type=f32)  94 us
    ppermute x15, waiting for transfers between devices, across(): return lax.ppermute(value, axis, SWAP)  86.9 us
    ppermute x15, starting transfers between devices, across(): return lax.ppermute(value, axis, SWAP)  73.1 us
    all_gather x1, waiting for transfers between devices, on_device(): down_half = lax.all_gather(down_piece, stack + groups, axis=0, tiled=True)  64.7 us
    pallas_call x1, Pallas kernels, attend_backward(): pl.pallas_call(functools.partial(backward_kernel, rows=rows), out_shape=j...  45.1 us
    psum x1, blocking collectives, on_device(): norm_grads = lax.psum(norm_grads, groups + ('b',) + stack)  42.4 us
    reduce_scatter x1, waiting for transfers between devices, on_device(): lax.psum_scatter(out_grad, stack + groups + ('b',), scatter_dimension=0,...  40.7 us
    ppermute x6, waiting for transfers between devices, quad_swap(): return lax.ppermute(value, ('b', 'l'), [(i, i ^ mask) for i in range(4)])  33.1 us
  transfers between devices with their start and end apart: 36, of which 16 were waited for; matrix products, arithmetic and copies ran while one was open for 17% of the time, Pallas kernels for 13%

profile of v1, /device:TPU:0, one launch (start us, length us, event | category | flops | bytes accessed | tf_op | source)
XLA Modules:
  0.0 741.6 jit_solution(2526215184111427515)
XLA Ops:
  19.9 13.3 %collective-permute-start.3 = (bf16[1024,768]{1,0:T(8,128)(2,1)}, bf16[1024,768]{1,0:T(8,128)(2,1)}, u32[]{:S(2)}, u32[]{:S(2)}) collective-permute-start(bf16[1024,768]{1,0:T(8,128)(2,1)} %copy.47), channel_id=1, source_target_pairs={{0,0},{2,4},{4,2},{6,6},{1,1},{3,5},{5,3},{7,7},{8,8},{10,12},{12,... | collective-permute-start | bytes 4718600 | tf_op jit(solution)/shard_map/ppermute | solution.py:274
  35.0 20.3 %collective-permute-start.4 = (bf16[512,1024]{1,0:T(8,128)(2,1)S(1)}, bf16[512,1024]{1,0:T(8,128)(2,1)S(1)}, u32[]{:S(2)}, u32[]{:S(2)}) collective-permute-start(bf16[512,1024]{1,0:T(8,128)(2,1)S(1)} %collective-permute-done.x_ref), channel_id=1, source_target_pairs={{0,4},{4,0},{1,5},{5,1},{2,6},{6,2},{3,7},{7,3},{8,12},{12,8},{9,1... | collective-permute-start | bytes 3145736 | tf_op jit(solution)/shard_map/ppermute | solution.py:270
  55.3 9.6 %collective-permute-start.2 = (bf16[512,1024]{1,0:T(8,128)(2,1)}, bf16[512,1024]{1,0:T(8,128)(2,1)S(1)}, u32[]{:S(2)}, u32[]{:S(2)}) collective-permute-start(bf16[512,1024]{1,0:T(8,128)(2,1)} %collective-permute-done.1.x_ref), channel_id=1, source_target_pairs={{0,4},{4,0},{1,5},{5,1},{2,6},{6,2},{3,7},{7,3},{8,12},{12,8},{9,1... | collective-permute-start | bytes 3145736 | tf_op jit(solution)/shard_map/ppermute | solution.py:270
  72.6 18.3 %shard_map.161 = (bf16[2048,256]{1,0:T(8,128)(2,1)S(1)}, bf16[2048,256]{1,0:T(8,128)(2,1)S(1)}, bf16[2048,256]{1,0:T(8,128)(2,1)S(1)}, bf16[2048,1024]{1,0:T(8,128)(2,1)S(1)}) custom-call(s32[1]{0:T(128)} %bitcast.5.place_ref, bf16[512,1024]{1,0:T(8,128)(2,1)S(1)} %collective-permute-done.x_ref, bf16[1024,768]{1,0:T(8,128)(2,1)} %collective-permute-done.3.w_ref, ...), custom_call_target="tpu_custom_call" | custom-call | flops 805306368 | bytes 5242880 | tf_op jit(solution)/shard_map/pallas_call | solution.py:62
  101.5 19.9 %shard_map.165 = (bf16[2048,256]{1,0:T(8,128)(2,1)S(1)}, f32[8,2048]{1,0:T(8,128)S(1)}) custom-call(bf16[2048,256]{1,0:T(8,128)(2,1)S(1)} %get-tuple-element.38.q_ref, bf16[2048,256]{1,0:T(8,128)(2,1)S(1)} %get-tuple-element.39.k_ref, bf16[2048,256]{1,0:T(8,128)(2,1)S(1)} %get-tuple-element.40.v_ref), custom_call_target="tpu_custom_call" | custom-call | flops 20000000000 | bytes 6291456 | tf_op jit(solution)/shard_map/pallas_call | solution.py:131
  122.3 22.9 %collective-permute-start.7 = (bf16[512,256]{1,0:T(8,128)(2,1)S(1)}, bf16[512,256]{1,0:T(8,128)(2,1)}, u32[]{:S(2)}, u32[]{:S(2)}) collective-permute-start(bf16[512,256]{1,0:T(8,128)(2,1)S(1)} %get-tuple-element.85), channel_id=1, source_target_pairs={{0,5},{1,4},{4,1},{5,0},{2,7},{3,6},{6,3},{7,2},{8,13},{9,12},{12,... | collective-permute-start | bytes 786440 | tf_op jit(solution)/shard_map/ppermute | solution.py:279
  147.9 21.1 %collective-permute-done.7 = bf16[512,256]{1,0:T(8,128)(2,1)} collective-permute-done((bf16[512,256]{1,0:T(8,128)(2,1)S(1)}, bf16[512,256]{1,0:T(8,128)(2,1)}, u32[]{:S(2)}, u32[]{:S(2)}) %collective-permute-start.7) | collective-permute-done | bytes 262176 | tf_op jit(solution)/shard_map/ppermute | solution.py:279
  176.3 10.8 %all-gather.8.cloned.1.call-done = bf16[1024,2048]{1,0:T(8,128)(2,1)} async-done(((bf16[1024,128]{1,0:T(8,128)(2,1)}), bf16[1024,2048]{1,0:T(8,128)(2,1)}) %all-gather.8.cloned.1.call-update) | async-done | bytes 4194320 | tf_op jit(solution)/shard_map/all_gather | solution.py:339
  187.1 12.9 %multiply_convert_fusion.1 = (bf16[1024,2048]{1,0:T(8,128)(2,1)}, f32[1024,2048]{1,0:T(8,128)}) fusion(bf16[1024,2048]{1,0:T(8,128)(2,1)} %all-gather.8.cloned.1.call-done, bf16[512,1024]{1,0:T(8,128)(2,1)} %collective-permute-done.8, bf16[512,1024]{1,0:T(8,128)(2,1)S(1)} %add_convert_fusion.2), kind=kOutput, calls=%fused_computation.9 | convolution fusion | flops 4318035968 | bytes 18874368 | tf_op jit(solution)/shard_map/dot_general | solution.py:266
  200.0 64.7 %all-gather.10.cloned.1.call-done = bf16[2048,1024]{1,0:T(8,128)(2,1)} async-done(((bf16[128,1024]{1,0:T(8,128)(2,1)}), bf16[2048,1024]{1,0:T(8,128)(2,1)}) %all-gather.10.cloned.1.call-update) | async-done | bytes 4194320 | tf_op jit(solution)/shard_map/all_gather | solution.py:340
  281.7 21.2 %collective-permute-start.13 = (bf16[512,1024]{1,0:T(8,128)(2,1)S(1)}, bf16[512,1024]{1,0:T(8,128)(2,1)S(1)}, u32[]{:S(2)}, u32[]{:S(2)}) collective-permute-start(bf16[512,1024]{1,0:T(8,128)(2,1)S(1)} %get-tuple-element.82), channel_id=1, source_target_pairs={{0,4},{4,0},{1,5},{5,1},{2,6},{6,2},{3,7},{7,3},{8,12},{12,8},{9,1... | collective-permute-start | bytes 3145736 | tf_op jit(solution)/shard_map/ppermute | solution.py:270
  305.2 9.9 %multiply_convert_fusion = bf16[1024,2048]{1,0:T(8,128)(2,1)S(1)} fusion(bf16[2048,1024]{1,0:T(8,128)(2,1)S(1)} %copy-done.32, f32[1024,2048]{1,0:T(8,128)S(1)} %bitcast.94, bf16[512,1024]{1,0:T(8,128)(2,1)S(1)} %collective-permute-done.13, bf16[512,1024]{1,0:T(8,128)(2,1)S(1)} %get-tuple-element.82), kind=kOutput, calls=%fused_computation.8 | convolution fusion | flops 4343201792 | bytes 18874368 | tf_op jit(solution)/shard_map/dot_general | solution.py:266
  331.2 9.3 %convolution_convert_fusion = bf16[2048,1024]{1,0:T(8,128)(2,1)} fusion(bf16[1024,2048]{1,0:T(8,128)(2,1)} %get-tuple-element.102, bf16[512,1024]{1,0:T(8,128)(2,1)} %copy-done.34, bf16[512,1024]{1,0:T(8,128)(2,1)} %copy-done.25), kind=kOutput, calls=%fused_computation.10 | convolution fusion | flops 4301258752 | bytes 10485760 | tf_op jit(solution)/shard_map/dot_general | solution.py:266
  379.6 10.7 %collective-permute-done.16 = bf16[512,256]{1,0:T(8,128)(2,1)} collective-permute-done((bf16[512,256]{1,0:T(8,128)(2,1)}, bf16[512,256]{1,0:T(8,128)(2,1)}, u32[]{:S(2)}, u32[]{:S(2)}) %collective-permute-start.16) | collective-permute-done | bytes 262176 | tf_op jit(solution)/shard_map/ppermute | solution.py:279
  394.8 45.1 %shard_map.166 = bf16[2048,768]{1,0:T(8,128)(2,1)} custom-call(bf16[2048,256]{1,0:T(8,128)(2,1)} %copy-done.5, bf16[2048,256]{1,0:T(8,128)(2,1)} %copy-done.6, bf16[2048,256]{1,0:T(8,128)(2,1)} %copy-done.7, bf16[2048,256]{1,0:T(8,128)(2,1)} %copy-done.8, bf16[2048,256]{1,0:T(8,128)(2,1)} %copy-done.24, f32[8,2048]{1,0:T(8,128)} %copy-done.11, ...), custom_call_target="tpu_custom_call" | custom-call | flops 44999999488 | bytes 12582912 | tf_op jit(solution)/shard_map/pallas_call | solution.py:224
  455.0 30.7 %collective-permute-done.21 = bf16[512,768]{1,0:T(8,128)(2,1)S(1)} collective-permute-done((bf16[512,768]{1,0:T(8,128)(2,1)S(1)}, bf16[512,768]{1,0:T(8,128)(2,1)S(1)}, u32[]{:S(2)}, u32[]{:S(2)}) %collective-permute-start.21) | collective-permute-done | bytes 786464 | tf_op jit(solution)/shard_map/ppermute | solution.py:270
  488.0 25.0 %collective-permute-done.22 = bf16[256,768]{1,0:T(8,128)(2,1)S(1)} collective-permute-done((bf16[256,768]{1,0:T(8,128)(2,1)S(1)}, bf16[256,768]{1,0:T(8,128)(2,1)S(1)}, u32[]{:S(2)}, u32[]{:S(2)}) %collective-permute-start.22) | collective-permute-done | bytes 393248 | tf_op jit(solution)/shard_map/ppermute | solution.py:270
  514.2 16.2 %collective-permute-start.24 = (bf16[128,768]{1,0:T(8,128)(2,1)S(1)}, bf16[128,768]{1,0:T(8,128)(2,1)S(1)}, u32[]{:S(2)}, u32[]{:S(2)}) collective-permute-start(bf16[128,768]{1,0:T(8,128)(2,1)S(1)} %select_convert_fusion.2), channel_id=1, source_target_pairs={{0,4},{4,0},{1,5},{5,1},{2,6},{6,2},{3,7},{7,3},{8,12},{12,8},{9,1... | collective-permute-start | bytes 589832 | tf_op jit(solution)/shard_map/ppermute | solution.py:270
  536.4 9.5 %collective-permute-start.10 = (bf16[512,1024]{1,0:T(8,128)(2,1)}, bf16[512,1024]{1,0:T(8,128)(2,1)}, u32[]{:S(2)}, u32[]{:S(2)}) collective-permute-start(bf16[512,1024]{1,0:T(8,128)(2,1)} %get-tuple-element.83), channel_id=1, source_target_pairs={{0,0},{2,4},{4,2},{6,6},{1,1},{3,5},{5,3},{7,7},{8,8},{10,12},{12,... | collective-permute-start | bytes 3145736 | tf_op jit(solution)/shard_map/ppermute | solution.py:274
  552.9 20.6 %collective-permute-done.19 = bf16[512,1024]{1,0:T(8,128)(2,1)S(1)} collective-permute-done((bf16[512,1024]{1,0:T(8,128)(2,1)}, bf16[512,1024]{1,0:T(8,128)(2,1)S(1)}, u32[]{:S(2)}, u32[]{:S(2)}) %collective-permute-start.19) | collective-permute-done | bytes 1048608 | tf_op jit(solution)/shard_map/ppermute | solution.py:270
  587.9 42.4 %psum.7 = f32[8,1024]{1,0:T(8,128)S(1)} all-reduce(f32[8,1024]{1,0:T(8,128)S(1)} %stack.35), channel_id=1, replica_groups=mesh['g0'=2,'g1'=2,'b'=2,'h'=2,'l'=2] {'g0','g1','b','h','l'}, use_global_device_ids=true, to_apply=%region_27.28 | all-reduce | flops 8192 | bytes 65536 | tf_op jit(solution)/shard_map/psum | solution.py:457
  630.9 40.7 %reduce-scatter.6.cloned.1.call-done = bf16[32,1024]{1,0:T(8,128)(2,1)} async-done(((bf16[1024,1024]{1,0:T(8,128)(2,1)}), bf16[32,1024]{1,0:T(8,128)(2,1)}) %reduce-scatter.6.cloned.1.call-update) | async-done | bytes 65552 | tf_op jit(solution)/shard_map/reduce_scatter | solution.py:425
  683.4 14.7 %all-gather.12.cloned.1.call-done = bf16[1024,1024]{1,0:T(8,128)(2,1)} async-done(((bf16[1024,128]{1,0:T(8,128)(2,1)}), bf16[1024,1024]{1,0:T(8,128)(2,1)}) %all-gather.12.cloned.1.call-update) | async-done | bytes 2097168 | tf_op jit(solution)/shard_map/all_gather | solution.py:404
  702.2 25.9 %all-gather.14.cloned.1.call-done = bf16[1024,1024]{1,0:T(8,128)(2,1)} async-done(((bf16[128,1024]{1,0:T(8,128)(2,1)}), bf16[1024,1024]{1,0:T(8,128)(2,1)}) %all-gather.14.cloned.1.call-update) | async-done | bytes 2097168 | tf_op jit(solution)/shard_map/all_gather | solution.py:403
  (238 shorter events, 190.2 us)
Async XLA Ops:
  7.2 138.1 %all-gather.6.cloned.1.call-start = ((), (), s32[]{:S(2)}) async-start(), calls=%async_computation.3 | async-start | bytes 2162688 | tf_op jit(solution)/shard_map/all_gather | solution.py:334
  8.9 178.2 %all-gather.8.cloned.1.call-start = ((), (), s32[]{:S(2)}) async-start(), calls=%async_computation.4 | async-start | bytes 4456448 | tf_op jit(solution)/shard_map/all_gather | solution.py:339
  9.8 255.0 %all-gather.10.cloned.1.call-start = ((), (), s32[]{:S(2)}) async-start(), calls=%async_computation.5 | async-start | bytes 4456448 | tf_op jit(solution)/shard_map/all_gather | solution.py:340
  11.7 43.6 %collective-permute-start.1 = (bf16[512,1024]{1,0:T(8,128)(2,1)S(1)}, bf16[512,1024]{1,0:T(8,128)(2,1)}, u32[]{:S(2)}, u32[]{:S(2)}) collective-permute-start(bf16[512,1024]{1,0:T(8,128)(2,1)S(1)} %collective-permute-done.x_ref), channel_id=1, source_target_pairs={{0,1},{1,0},{2,3},{3,2},{4,5},{5,4},{6,7},{7,6},{8,9},{9,8},{10,11... | collective-permute-start | bytes 3145736 | tf_op jit(solution)/shard_map/ppermute | solution.py:270
  19.9 52.7 %collective-permute-start.3 = (bf16[1024,768]{1,0:T(8,128)(2,1)}, bf16[1024,768]{1,0:T(8,128)(2,1)}, u32[]{:S(2)}, u32[]{:S(2)}) collective-permute-start(bf16[1024,768]{1,0:T(8,128)(2,1)} %copy.47), channel_id=1, source_target_pairs={{0,0},{2,4},{4,2},{6,6},{1,1},{3,5},{5,3},{7,7},{8,8},{10,12},{12,... | collective-permute-start | bytes 4718600 | tf_op jit(solution)/shard_map/ppermute | solution.py:274
  34.9 405.0 %reduce-scatter.10.cloned.1.call-start = ((), (), s32[]{:S(2)}) async-start(), calls=%async_computation.10 | async-start | bytes 4456448
  35.0 55.9 %collective-permute-start.4 = (bf16[512,1024]{1,0:T(8,128)(2,1)S(1)}, bf16[512,1024]{1,0:T(8,128)(2,1)S(1)}, u32[]{:S(2)}, u32[]{:S(2)}) collective-permute-start(bf16[512,1024]{1,0:T(8,128)(2,1)S(1)} %collective-permute-done.x_ref), channel_id=1, source_target_pairs={{0,4},{4,0},{1,5},{5,1},{2,6},{6,2},{3,7},{7,3},{8,12},{12,8},{9,1... | collective-permute-start | bytes 3145736 | tf_op jit(solution)/shard_map/ppermute | solution.py:270
  55.3 42.7 %collective-permute-start.2 = (bf16[512,1024]{1,0:T(8,128)(2,1)}, bf16[512,1024]{1,0:T(8,128)(2,1)S(1)}, u32[]{:S(2)}, u32[]{:S(2)}) collective-permute-start(bf16[512,1024]{1,0:T(8,128)(2,1)} %collective-permute-done.1.x_ref), channel_id=1, source_target_pairs={{0,4},{4,0},{1,5},{5,1},{2,6},{6,2},{3,7},{7,3},{8,12},{12,8},{9,1... | collective-permute-start | bytes 3145736 | tf_op jit(solution)/shard_map/ppermute | solution.py:270
  122.3 24.6 %collective-permute-start.6 = (bf16[512,256]{1,0:T(8,128)(2,1)}, bf16[512,256]{1,0:T(8,128)(2,1)S(1)}, u32[]{:S(2)}, u32[]{:S(2)}) collective-permute-start(bf16[512,256]{1,0:T(8,128)(2,1)} %get-tuple-element.86), channel_id=1, source_target_pairs={{0,1},{1,0},{4,5},{5,4},{2,3},{3,2},{6,7},{7,6},{8,9},{9,8},{12,13... | collective-permute-start | bytes 786440 | tf_op jit(solution)/shard_map/ppermute | solution.py:279
  122.3 46.7 %collective-permute-start.7 = (bf16[512,256]{1,0:T(8,128)(2,1)S(1)}, bf16[512,256]{1,0:T(8,128)(2,1)}, u32[]{:S(2)}, u32[]{:S(2)}) collective-permute-start(bf16[512,256]{1,0:T(8,128)(2,1)S(1)} %get-tuple-element.85), channel_id=1, source_target_pairs={{0,5},{1,4},{4,1},{5,0},{2,7},{3,6},{6,3},{7,2},{8,13},{9,12},{12,... | collective-permute-start | bytes 786440 | tf_op jit(solution)/shard_map/ppermute | solution.py:279
  281.7 23.5 %collective-permute-start.13 = (bf16[512,1024]{1,0:T(8,128)(2,1)S(1)}, bf16[512,1024]{1,0:T(8,128)(2,1)S(1)}, u32[]{:S(2)}, u32[]{:S(2)}) collective-permute-start(bf16[512,1024]{1,0:T(8,128)(2,1)S(1)} %get-tuple-element.82), channel_id=1, source_target_pairs={{0,4},{4,0},{1,5},{5,1},{2,6},{6,2},{3,7},{7,3},{8,12},{12,8},{9,1... | collective-permute-start | bytes 3145736 | tf_op jit(solution)/shard_map/ppermute | solution.py:270
  331.1 203.5 %reduce-scatter.8.cloned.1.call-start = ((), (), s32[]{:S(2)}) async-start(), calls=%async_computation.8 | async-start | bytes 4456448 | tf_op jit(solution)/shard_map/reduce_scatter | solution.py:401
  340.5 331.1 %reduce-scatter.6.cloned.1.call-start = ((), (), s32[]{:S(2)}) async-start(), calls=%async_computation.6 | async-start | bytes 2162688 | tf_op jit(solution)/shard_map/reduce_scatter | solution.py:425
  365.9 24.4 %collective-permute-start.16 = (bf16[512,256]{1,0:T(8,128)(2,1)}, bf16[512,256]{1,0:T(8,128)(2,1)}, u32[]{:S(2)}, u32[]{:S(2)}) collective-permute-start(bf16[512,256]{1,0:T(8,128)(2,1)} %convolution_convert_fusion.9), channel_id=1, source_target_pairs={{0,1},{1,0},{4,5},{5,4},{2,3},{3,2},{6,7},{7,6},{8,9},{9,8},{12,13... | collective-permute-start | bytes 786440 | tf_op jit(solution)/shard_map/ppermute | solution.py:279
  369.1 22.2 %collective-permute-start.17 = (bf16[512,256]{1,0:T(8,128)(2,1)}, bf16[512,256]{1,0:T(8,128)(2,1)}, u32[]{:S(2)}, u32[]{:S(2)}) collective-permute-start(bf16[512,256]{1,0:T(8,128)(2,1)} %convolution_convert_fusion.8), channel_id=1, source_target_pairs={{0,4},{1,5},{4,0},{5,1},{2,6},{3,7},{6,2},{7,3},{8,12},{9,13},{12,... | collective-permute-start | bytes 786440 | tf_op jit(solution)/shard_map/ppermute | solution.py:279
  376.8 321.3 %all-gather.12.cloned.1.call-start = ((), (), s32[]{:S(2)}) async-start(), calls=%async_computation.7 | async-start | bytes 2359296 | tf_op jit(solution)/shard_map/all_gather | solution.py:404
  441.7 286.4 %all-gather.14.cloned.1.call-start = ((), (), s32[]{:S(2)}) async-start(), calls=%async_computation.9 | async-start | bytes 2359296 | tf_op jit(solution)/shard_map/all_gather | solution.py:403
  449.8 35.8 %collective-permute-start.21 = (bf16[512,768]{1,0:T(8,128)(2,1)S(1)}, bf16[512,768]{1,0:T(8,128)(2,1)S(1)}, u32[]{:S(2)}, u32[]{:S(2)}) collective-permute-start(bf16[512,768]{1,0:T(8,128)(2,1)S(1)} %select_convert_fusion), channel_id=1, source_target_pairs={{0,16},{16,0},{1,17},{17,1},{2,18},{18,2},{3,19},{19,3},{4,20},{20... | collective-permute-start | bytes 2359304 | tf_op jit(solution)/shard_map/ppermute | solution.py:270
  455.0 75.3 %collective-permute-start.18 = (bf16[1024,1024]{1,0:T(8,128)(2,1)}, bf16[1024,1024]{1,0:T(8,128)(2,1)}, u32[]{:S(2)}, u32[]{:S(2)}) collective-permute-start(bf16[1024,1024]{1,0:T(8,128)(2,1)} %convolution_convert_fusion.2), channel_id=1, source_target_pairs={{0,4},{4,0},{1,5},{5,1},{2,6},{6,2},{3,7},{7,3},{8,12},{12,8},{9,1... | collective-permute-start | bytes 6291464 | tf_op jit(solution)/shard_map/ppermute | solution.py:270
  487.9 25.1 %collective-permute-start.22 = (bf16[256,768]{1,0:T(8,128)(2,1)S(1)}, bf16[256,768]{1,0:T(8,128)(2,1)S(1)}, u32[]{:S(2)}, u32[]{:S(2)}) collective-permute-start(bf16[256,768]{1,0:T(8,128)(2,1)S(1)} %select_convert_fusion.1), channel_id=1, source_target_pairs={{0,8},{8,0},{1,9},{9,1},{2,10},{10,2},{3,11},{11,3},{4,12},{12,4},... | collective-permute-start | bytes 1179656 | tf_op jit(solution)/shard_map/ppermute | solution.py:270
  534.2 39.3 %collective-permute-start.19 = (bf16[512,1024]{1,0:T(8,128)(2,1)}, bf16[512,1024]{1,0:T(8,128)(2,1)S(1)}, u32[]{:S(2)}, u32[]{:S(2)}) collective-permute-start(bf16[512,1024]{1,0:T(8,128)(2,1)} %add_convert_fusion), channel_id=1, source_target_pairs={{0,1},{1,0},{2,3},{3,2},{4,5},{5,4},{6,7},{7,6},{8,9},{9,8},{10,11... | collective-permute-start | bytes 3145736 | tf_op jit(solution)/shard_map/ppermute | solution.py:270
  536.4 43.4 %collective-permute-start.10 = (bf16[512,1024]{1,0:T(8,128)(2,1)}, bf16[512,1024]{1,0:T(8,128)(2,1)}, u32[]{:S(2)}, u32[]{:S(2)}) collective-permute-start(bf16[512,1024]{1,0:T(8,128)(2,1)} %get-tuple-element.83), channel_id=1, source_target_pairs={{0,0},{2,4},{4,2},{6,6},{1,1},{3,5},{5,3},{7,7},{8,8},{10,12},{12,... | collective-permute-start | bytes 3145736 | tf_op jit(solution)/shard_map/ppermute | solution.py:274
  551.2 29.5 %collective-permute-start.27 = (bf16[512,768]{1,0:T(8,128)(2,1)}, bf16[512,768]{1,0:T(8,128)(2,1)}, u32[]{:S(2)}, u32[]{:S(2)}) collective-permute-start(bf16[512,768]{1,0:T(8,128)(2,1)} %maximum_select_fusion.2), channel_id=1, source_target_pairs={{0,16},{16,0},{1,17},{17,1},{2,18},{18,2},{3,19},{19,3},{4,20},{20... | collective-permute-start | bytes 2359304 | tf_op jit(solution)/shard_map/ppermute | solution.py:270
  577.9 104.0 %collective-permute-start.20 = (bf16[512,1024]{1,0:T(8,128)(2,1)}, bf16[512,1024]{1,0:T(8,128)(2,1)S(1)}, u32[]{:S(2)}, u32[]{:S(2)}) collective-permute-start(bf16[512,1024]{1,0:T(8,128)(2,1)} %fusion.15), channel_id=1, source_target_pairs={{0,0},{2,4},{4,2},{6,6},{1,1},{3,5},{5,3},{7,7},{8,8},{10,12},{12,... | collective-permute-start | bytes 3145736 | tf_op jit(solution)/shard_map/ppermute | solution.py:274
  (52 other events, 905.2 us)
Sparse Core Ops, SparseCore 0:
  11.4 73.4 all-gather.5
  88.2 98.7 all-gather.7
  190.4 74.2 all-gather.9
  331.2 93.8 reduce-scatter.9
  427.3 103.2 reduce-scatter.7
  532.7 138.8 reduce-scatter.5
  673.6 24.4 all-gather.11
  700.2 27.8 all-gather.13

commit v2 on v1

--- a/solution.py
+++ b/solution.py
@@ -2,6 +2,7 @@
 
 import jax
 import jax.numpy as jnp
+import numpy as np
 from jax import lax
 from jax.experimental import pallas as pl
 from jax.experimental.pallas import tpu as pltpu
@@ -151,14 +152,174 @@
     )(q, k, v)
 
 
-def backward_kernel(
-    q_ref, k_ref, v_ref, o_ref, do_ref, lse_ref, cos_ref, sin_ref, out_ref, dq, delta, *, rows
-):
+MESH = pl.DeviceIdType.MESH
+
+
+class Copies:
+    def __init__(self, send, recv):
+        self.send, self.recv, self.made = send, recv, {}
+
+    def start(self, name, source, target, device):
+        n = len(self.made)
+        copy = pltpu.make_async_remote_copy(
+            src_ref=source,
+            dst_ref=target,
+            send_sem=self.send.at[n],
+            recv_sem=self.recv.at[n],
+            device_id=device,
+            device_id_type=MESH,
+        )
+        self.made[name] = copy
+        copy.start()
+
+    def arrived(self, name):
+        self.made[name].wait_recv()
+
+    def drain(self):
+        for copy in self.made.values():
+            copy.wait_send()
+
+
+def flip(axis):
+    return {axis: 1 - lax.axis_index(axis)}
+
+
+def next_layer(step):
+    at = lax.rem(2 * lax.axis_index("h") + lax.axis_index("l") + step, 4)
+    return {"h": at // 2, "l": lax.rem(at, 2)}
+
+
+def greet(groups):
+    barrier = pltpu.get_barrier_semaphore()
+    friends = [flip(axis) for axis in groups + ("b",)] + [next_layer(1), next_layer(3)]
+    for friend in friends:
+        pl.semaphore_signal(barrier, inc=1, device_id=friend, device_id_type=MESH)
+    pl.semaphore_wait(barrier, len(friends))
+
+
+def add_into(total, term, rows=16):
+    lead, count = total.shape[:-2], total.shape[-2]
+    step = min(rows, count)
+
+    @pl.loop(0, count // step)
+    def _(i):
+        at = pl.ds(pl.multiple_of(i * step, step), step)
+        for index in np.ndindex(*lead):
+            total[index + (at,)] = (
+                total[index + (at,)].astype(f32) + term[index + (at,)].astype(f32)
+            ).astype(bf16)
+
+
+def sums_kernel(*refs, groups, rows):
+    (
+        q_ref, k_ref, v_ref, o_ref, do_ref, lse_ref, cos_ref, sin_ref,
+        up_ref, out_ref, down_ref,
+        mixed_ref, up_all, out_all, down_all,
+        dq, dk, dv, delta,
+        *rest,
+    ) = refs
+    bits = len(groups)
+    terms = (up_ref, out_ref, down_ref)
+    results = (up_all, out_all, down_all)
+    partial = [[rest[3 * s + a] for s in range(bits)] for a in range(3)]
+    rest = rest[3 * bits :]
+    passing, (send, recv, local) = rest[:3], rest[3:]
+    copies = Copies(send, recv)
+    place = [lax.axis_index(axis) for axis in groups]
+    layer = 2 * lax.axis_index("h") + lax.axis_index("l")
+    core = lax.axis_index("b")
+    orders = [tuple(range(bits)), tuple(range(bits)), tuple(reversed(range(bits)))]
+
+    def shard(k):
+        return lax.rem(layer + 4 - k, 4)
+
+    def index(order, stage, side):
+        at = []
+        for axis in range(bits):
+            when = order.index(axis)
+            if when < stage:
+                at.append(place[axis])
+            elif when == stage:
+                at.append(place[axis] if side == 0 else 1 - place[axis])
+            else:
+                at.append(slice(None))
+        return tuple(at)
+
+    def inner(order, stage, side):
+        at = []
+        for axis in range(bits):
+            when = order.index(axis)
+            if when == stage:
+                at.append(place[axis] if side == 0 else 1 - place[axis])
+            elif when > stage:
+                at.append(slice(None))
+        return tuple(at)
+
+    def source(a, k, stage, side):
+        order = orders[a]
+        if stage == 0:
+            return terms[a].at[(shard(k),) + index(order, 0, side)]
+        return partial[a][stage - 1].at[(k % 4,) + inner(order, stage, side)]
+
+    def plane_send(k, stage):
+        for a in range(3):
+            copies.start(
+                ("plane", a, k, stage),
+                source(a, k, stage, 1),
+                partial[a][stage].at[k % 4],
+                flip(groups[orders[a][stage]]),
+            )
+
+    def plane_add(k, stage):
+        for a in range(3):
+            copies.arrived(("plane", a, k, stage))
+            add_into(partial[a][stage].at[k % 4], source(a, k, stage, 0))
+
+    def ring_send(step):
+        for a in range(3):
+            held = partial[a][bits - 1].at[1] if step == 1 else passing[a].at[step - 2]
+            copies.start(("ring", a, step), held, passing[a].at[step - 1], next_layer(1))
+
+    def ring_add(step):
+        for a in range(3):
+            copies.arrived(("ring", a, step))
+            add_into(passing[a].at[step - 1], partial[a][bits - 1].at[(step + 1) % 4])
+
+    def gather_send(stage):
+        for a in range(3):
+            order = orders[a]
+            at = tuple(
+                place[axis] if order.index(axis) >= stage else slice(None) for axis in range(bits)
+            )
+            held = passing[a].at[2] if stage == 0 else results[a].at[(core,) + at]
+            copies.start(
+                ("gather", a, stage), held, results[a].at[(core,) + at], flip(groups[order[stage]])
+            )
+
+    def core_send(stage):
+        for a in range(3):
+            order = orders[a]
+            at = []
+            for axis in range(bits):
+                when = order.index(axis)
+                if stage == 0 or when > stage - 1:
+                    at.append(place[axis])
+                elif when == stage - 1:
+                    at.append(1 - place[axis])
+                else:
+                    at.append(slice(None))
+            spot = results[a].at[(core,) + tuple(at)]
+            held = passing[a].at[2] if stage == 0 else spot
+            copies.start(("core", a, stage), held, spot, flip("b"))
+
+    greet(groups)
     length, width = q_ref.shape
     heads = width // HEAD_DIM
     blocks = length // rows
     lane_head = lax.broadcasted_iota(jnp.int32, (8, width), 1) // HEAD_DIM
     marks = (lane_head == lax.broadcasted_iota(jnp.int32, (8, width), 0)).astype(f32)
+    for k in (1, 2):
+        plane_send(k, 0)
 
     def span(i):
         return pl.ds(pl.multiple_of(i * rows, rows), rows)
@@ -170,68 +331,142 @@
             marks, product, NT, precision=lax.Precision.HIGHEST, preferred_element_type=f32
         )
 
-    dq[...] = jnp.zeros_like(dq)
-
-    def tile(i, j, diagonal):
-        at = span(i)
-        keys, values = k_ref[span(j)], v_ref[span(j)]
+    for total in (dq, dk, dv):
+        total[...] = jnp.zeros_like(total)
+
+    def tile(i, j):
+        at, to = span(i), span(j)
+        keys, values = k_ref[to], v_ref[to]
         queries, grads = q_ref[at], do_ref[at]
-        dk = jnp.zeros((rows, width), f32)
-        dv = jnp.zeros((rows, width), f32)
-        dqi = dq[at]
+        dkj, dvj, dqi = dk[to], dv[to], dq[at]
         zero = jnp.zeros((), bf16)
+        key = j * rows + lax.broadcasted_iota(jnp.int32, (rows, rows), 0)
+        query = i * rows + lax.broadcasted_iota(jnp.int32, (rows, rows), 1)
+        allowed = key <= query
         for h in range(heads):
             mine = head_lanes((rows, width), h)
             qm = jnp.where(mine, queries, zero)
             dom = jnp.where(mine, grads, zero)
             km = jnp.where(mine, keys, zero)
             st = lax.dot_general(keys, qm, NT, preferred_element_type=f32)
-            pt = jnp.exp2(st * LOG2E - lse_ref[h : h + 1, at])
-            if diagonal:
-                key = lax.broadcasted_iota(jnp.int32, (rows, rows), 0)
-                query = lax.broadcasted_iota(jnp.int32, (rows, rows), 1)
-                pt = jnp.where(key <= query, pt, 0.0)
+            pt = jnp.where(allowed, jnp.exp2(st * LOG2E - lse_ref[h : h + 1, at]), 0.0)
             dpt = lax.dot_general(values, dom, NT, preferred_element_type=f32)
             dst = (pt * (dpt - delta[h : h + 1, at])).astype(bf16)
-            dv = dv + jnp.dot(pt.astype(bf16), dom, preferred_element_type=f32)
-            dk = dk + jnp.dot(dst, qm, preferred_element_type=f32)
+            dvj = dvj + jnp.dot(pt.astype(bf16), dom, preferred_element_type=f32)
+            dkj = dkj + jnp.dot(dst, qm, preferred_element_type=f32)
             dqi = dqi + lax.dot_general(dst, km, TN, preferred_element_type=f32)
-        dq[at] = dqi
-        return dk, dv
+        dq[at], dk[to], dv[to] = dqi, dkj, dvj
+
+    def tiles(low, high):
+        @pl.loop(low, high)
+        def _(t):
+            i = jnp.int32(0)
+            for n in range(1, blocks):
+                i = i + (t >= n * (n + 1) // 2).astype(jnp.int32)
+            tile(i, t - i * (i + 1) // 2)
+
+    count = blocks * (blocks + 1) // 2
+    tiles(0, 3 * count // 10)
+    plane_add(1, 0)
+    if bits > 1:
+        plane_send(1, 1)
+    plane_send(3, 0)
+    tiles(3 * count // 10, 8 * count // 10)
+    plane_add(2, 0)
+    if bits > 1:
+        plane_send(2, 1)
+    plane_send(4, 0)
+    tiles(8 * count // 10, count)
 
     def turn_back(grad, at):
         return grad * cos_ref[at] + swap_halves(grad, 1.0) * sin_ref[at]
 
     @pl.loop(0, blocks)
-    def _(j):
-        def more(i, carry):
-            dk, dv = tile(i, j, False)
-            return carry[0] + dk, carry[1] + dv
-
-        dk, dv = lax.fori_loop(j + 1, blocks, more, tile(j, j, True))
-        out_ref[span(j), width : 2 * width] = turn_back(dk, span(j)).astype(bf16)
-        out_ref[span(j), 2 * width :] = dv.astype(bf16)
-
-    @pl.loop(0, blocks)
     def _(i):
-        turned = turn_back(dq[span(i)], span(i))
-        out_ref[span(i), :width] = (HEAD_DIM ** (-0.5) * turned).astype(bf16)
-
-
-def attend_backward(q, k, v, o, do, lse, cosine, sine, rows=BLOCK):
+        at = span(i)
+        mixed_ref[at, :width] = (HEAD_DIM ** (-0.5) * turn_back(dq[at], at)).astype(bf16)
+        mixed_ref[at, width : 2 * width] = turn_back(dk[at], at).astype(bf16)
+        mixed_ref[at, 2 * width :] = dv[at].astype(bf16)
+
+    for stage in range(1, bits):
+        for k in (1, 2):
+            plane_add(k, stage)
+            if stage + 1 < bits:
+                plane_send(k, stage + 1)
+    ring_send(1)
+    plane_add(3, 0)
+    if bits > 1:
+        plane_send(3, 1)
+    ring_add(1)
+    ring_send(2)
+    plane_add(4, 0)
+    if bits > 1:
+        plane_send(4, 1)
+    for stage in range(1, bits):
+        plane_add(3, stage)
+        if stage + 1 < bits:
+            plane_send(3, stage + 1)
+    ring_add(2)
+    ring_send(3)
+    for stage in range(1, bits):
+        plane_add(4, stage)
+        if stage + 1 < bits:
+            plane_send(4, stage + 1)
+    ring_add(3)
+    core_send(0)
+    own = [
+        pltpu.make_async_copy(
+            passing[a].at[2], results[a].at[(core,) + tuple(place)], local.at[a]
+        )
+        for a in range(3)
+    ]
+    gather_send(0)
+    for copy in own:
+        copy.start()
+    for copy in own:
+        copy.wait()
+    for stage in range(bits):
+        for a in range(3):
+            copies.arrived(("gather", a, stage))
+        if stage + 1 < bits:
+            gather_send(stage + 1)
+        core_send(stage + 1)
+    for stage in range(bits + 1):
+        for a in range(3):
+            copies.arrived(("core", a, stage))
+    copies.drain()
+
+
+def attend_and_sum(q, k, v, o, do, lse, cosine, sine, up, out, down, groups, rows=BLOCK):
     length, width = q.shape
+    bits = len(groups)
+    terms = (up, out, down)
     vmem = pl.BlockSpec(memory_space=pltpu.VMEM)
+    anywhere = pl.BlockSpec(memory_space=pl.ANY)
+    scratch = [pltpu.VMEM((length, width), f32)] * 3 + [pltpu.VMEM((8, length), f32)]
+    for stage in range(bits):
+        for term in terms:
+            kept = (2,) * (bits - 1 - stage)
+            scratch.append(pltpu.VMEM((4,) + kept + term.shape[-2:], bf16))
+    for term in terms:
+        scratch.append(pltpu.VMEM((3,) + term.shape[-2:], bf16))
+    n = 3 * (4 * bits + 3 + bits + bits + 1)
+    scratch += [pltpu.SemaphoreType.DMA((n,)), pltpu.SemaphoreType.DMA((n,))]
+    scratch += [pltpu.SemaphoreType.DMA((3,))]
     return pl.pallas_call(
-        functools.partial(backward_kernel, rows=rows),
-        out_shape=jax.ShapeDtypeStruct((length, 3 * width), bf16),
-        in_specs=[vmem] * 8,
-        out_specs=vmem,
-        scratch_shapes=[pltpu.VMEM((length, width), f32), pltpu.VMEM((8, length), f32)],
-        compiler_params=pltpu.CompilerParams(vmem_limit_bytes=56 * 2**20),
+        functools.partial(sums_kernel, groups=groups, rows=rows),
+        out_shape=(jax.ShapeDtypeStruct((length, 3 * width), bf16),)
+        + tuple(jax.ShapeDtypeStruct((2,) + term.shape[1:], bf16) for term in terms),
+        in_specs=[vmem] * 11,
+        out_specs=(vmem,) + (anywhere,) * 3,
+        scratch_shapes=scratch,
+        compiler_params=pltpu.CompilerParams(
+            vmem_limit_bytes=60 * 2**20, collective_id=1, has_side_effects=True
+        ),
         cost_estimate=pl.CostEstimate(
-            flops=45_000_000_000, bytes_accessed=12 * 2**20, transcendentals=0
-        ),
-    )(q, k, v, o, do, lse, cosine, sine)
+            flops=100_000_000_000, bytes_accessed=32 * 2**20, transcendentals=0
+        ),
+    )(q, k, v, o, do, lse, cosine, sine, up, out, down)
 
 
 def norm_forward(value, gain, shift):
@@ -397,11 +632,7 @@
     grad_active = dot(pair_g, down_half, NT)
     grad_hidden = (slope.astype(f32) * grad_active).astype(bf16)
     down_grad = dot(active, pair_g, TN).astype(bf16)
-    up_grad = dot(pair_f, grad_hidden, TN).astype(bf16)
-    down_sum = lax.psum_scatter(down_grad, stack + groups, scatter_dimension=0, tiled=True)
-    up_sum = lax.psum_scatter(up_grad, stack + groups, scatter_dimension=1, tiled=True)
-    down_grad = lax.all_gather(down_sum, ("b",) + groups, axis=0, tiled=True).astype(f32)
-    up_grad = lax.all_gather(up_sum, ("b",) + groups, axis=1, tiled=True).astype(f32)
+    up_grad = dot(grad_hidden, pair_f, TN).astype(bf16)
 
     grad_f = dot(grad_hidden[part:], up_half, NT).astype(bf16)
     grad_f = dot(grad_hidden[:part], up_half, NT) + across(grad_f, "b").astype(f32)
@@ -422,12 +653,32 @@
         out_grad = lax.dynamic_update_slice_in_dim(
             out_grad, dot(heads[mask], grad_a, TN).astype(bf16), (place ^ mask) * cols, 0
         )
-    out_sum = lax.psum_scatter(
-        out_grad, stack + groups + ("b",), scatter_dimension=0, tiled=True
+    out_grad = out_grad.reshape(4, 2, cols // 2, depth)
+    sent = lax.dynamic_index_in_dim(out_grad, 1 - core, 1, False)
+    kept = lax.dynamic_index_in_dim(out_grad, core, 1, False)
+    out_grad = (kept.astype(f32) + across(sent, "b").astype(f32)).astype(bf16)
+    slots = (2,) * len(groups)
+
+    def pieces(value):
+        return value.reshape((4,) + slots + (value.size // (4 * n_groups * depth), depth))
+
+    grad_mixed, up_grad, out_grad, down_grad = attend_and_sum(
+        q,
+        k,
+        v,
+        attended,
+        grad_attended,
+        lse,
+        cosine,
+        sine,
+        pieces(up_grad),
+        pieces(out_grad),
+        pieces(down_grad),
+        groups,
     )
-    out_grad = lax.all_gather(out_sum, groups + ("b",), axis=0, tiled=True).astype(f32)
-
-    grad_mixed = attend_backward(q, k, v, attended, grad_attended, lse, cosine, sine)
+    up_grad = up_grad.reshape(units, depth).T.astype(f32)
+    out_grad = out_grad.reshape(cols, depth).astype(f32)
+    down_grad = down_grad.reshape(units, depth).astype(f32)
 
     pair = 2 * part
     sent = lax.dynamic_slice_in_dim(grad_mixed, (1 - core) * pair, pair, 0)

time: 751 us -> 661 us (0.88)
  waiting for transfers between devices: 277 us -> 137 us
  Pallas kernels: 93.8 us -> 172 us
  blocking collectives: 51.6 us -> 39.2 us
  matrix products: 94 us -> 83.6 us
  local copies, waits for them, and re-layouts: 38.5 us -> 30.3 us
    pallas_call x1, Pallas kernels: 45.1 us -> 128 us  [attend_and_sum(): pl.pallas_call(functools.partial(sums_kernel, groups=groups, rows=rows),...]
    ppermute x15 -> x16, waiting for transfers between devices: 86.9 us -> 34 us  [across(): return lax.ppermute(value, axis, SWAP)]
    reduce_scatter x2 -> x0, waiting for transfers between devices: 40.7 us -> none  [the longest x1 40.7 us: on_device(): lax.psum_scatter(out_grad, stack + groups + ('b',), scatter_dimension=0,...]
    all_gather x2 -> x0, waiting for transfers between devices: 40.6 us -> none  [the longest x1 25.9 us: on_device(): lax.all_gather(down_sum, ('b',) + groups, axis=0, tiled=True).astype(f32)]
    ppermute x15 -> x16, starting transfers between devices: 73.1 us -> 87.9 us  [across(): return lax.ppermute(value, axis, SWAP)]
    pallas_call x4, Pallas kernels: 28.8 us -> 15.1 us  [project(): pl.pallas_call(qkv_kernel, out_shape=tuple((jax.ShapeDtypeStruct((length,...]
    dot_general x24, matrix products: 94 us -> 83.6 us  [dot(): return lax.dot_general(left, right, dims, preferred_element_type=f32)]
    ppermute x6, waiting for transfers between devices: 33.1 us -> 22.9 us  [quad_swap(): return lax.ppermute(value, ('b', 'l'), [(i, i ^ mask) for i in range(4)])]
  transfers between devices with their start and end apart: 36 -> 32, of which waited for: 16 -> 11; matrix products, arithmetic and copies ran while one was open for 17% -> 15% of each run, Pallas kernels for 13% -> 7%
where the time goes in v2:
time: 661 us; the launch traced here: 653 us
  Pallas kernels  172 us (26%)
  waiting for transfers between devices  137 us (21%)
  starting transfers between devices  135 us (20%)
  matrix products  83.6 us (13%)
  other arithmetic  40 us (6%)
  blocking collectives  39.2 us (6%)
  local copies, waits for them, and re-layouts  30.3 us (5%)
  between operations  15.9 us (2%)
    pallas_call x1, Pallas kernels, attend_and_sum(): pl.pallas_call(functools.partial(sums_kernel, groups=groups, rows=rows),...  128 us
    ppermute x16, starting transfers between devices, across(): return lax.ppermute(value, axis, SWAP)  87.9 us
    dot_general x24, matrix products, dot(): return lax.dot_general(left, right, dims, preferred_element_type=f32)  83.6 us
    all_gather x1, waiting for transfers between devices, on_device(): down_half = lax.all_gather(down_piece, stack + groups, axis=0, tiled=True)  67 us
    psum x1, blocking collectives, on_device(): norm_grads = lax.psum(norm_grads, groups + ('b',) + stack)  39.2 us
    ppermute x16, waiting for transfers between devices, across(): return lax.ppermute(value, axis, SWAP)  34 us
    pallas_call x1, Pallas kernels, attend_forward(): pl.pallas_call(functools.partial(forward_kernel, rows=rows, blocks=blocks...  29.2 us
    ppermute x6, starting transfers between devices, quad_swap(): return lax.ppermute(value, ('b', 'l'), [(i, i ^ mask) for i in range(4)])  24.1 us
  transfers between devices with their start and end apart: 32, of which 11 were waited for; matrix products, arithmetic and copies ran while one was open for 15% of the time, Pallas kernels for 7%

profile of v2, /device:TPU:0, one launch (start us, length us, event | category | flops | bytes accessed | tf_op | source)
XLA Modules:
  0.0 652.6 jit_solution(5927298828148576495)
XLA Ops:
  19.9 13.3 %collective-permute-start.3 = (bf16[1024,768]{1,0:T(8,128)(2,1)}, bf16[1024,768]{1,0:T(8,128)(2,1)}, u32[]{:S(2)}, u32[]{:S(2)}) collective-permute-start(bf16[1024,768]{1,0:T(8,128)(2,1)} %copy.41), channel_id=1, source_target_pairs={{0,0},{2,4},{4,2},{6,6},{1,1},{3,5},{5,3},{7,7},{8,8},{10,12},{12,... | collective-permute-start | bytes 4718600 | tf_op jit(solution)/shard_map/ppermute | solution.py:509
  35.0 20.2 %collective-permute-start.4 = (bf16[512,1024]{1,0:T(8,128)(2,1)S(1)}, bf16[512,1024]{1,0:T(8,128)(2,1)S(1)}, u32[]{:S(2)}, u32[]{:S(2)}) collective-permute-start(bf16[512,1024]{1,0:T(8,128)(2,1)S(1)} %collective-permute-done.x_ref), channel_id=1, source_target_pairs={{0,4},{4,0},{1,5},{5,1},{2,6},{6,2},{3,7},{7,3},{8,12},{12,8},{9,1... | collective-permute-start | bytes 3145736 | tf_op jit(solution)/shard_map/ppermute | solution.py:505
  55.2 9.7 %collective-permute-start.2 = (bf16[512,1024]{1,0:T(8,128)(2,1)}, bf16[512,1024]{1,0:T(8,128)(2,1)S(1)}, u32[]{:S(2)}, u32[]{:S(2)}) collective-permute-start(bf16[512,1024]{1,0:T(8,128)(2,1)} %collective-permute-done.1.x_ref), channel_id=1, source_target_pairs={{0,4},{4,0},{1,5},{5,1},{2,6},{6,2},{3,7},{7,3},{8,12},{12,8},{9,1... | collective-permute-start | bytes 3145736 | tf_op jit(solution)/shard_map/ppermute | solution.py:505
  64.9 7.5 %fusion.30 = (f32[2048,256]{1,0:T(8,128)S(1)}, f32[2048,256]{1,0:T(8,128)S(1)}) fusion(f32[256]{0:T(256)S(1)} %fusion.80), kind=kLoop, calls=%fused_computation.65 | loop fusion | flops 524288 | bytes 4195328 | tf_op jit(solution)/shard_map/sin | solution.py:494
  87.9 29.2 %shard_map.165 = (bf16[2048,256]{1,0:T(8,128)(2,1)S(1)}, f32[8,2048]{1,0:T(8,128)S(1)}) custom-call(bf16[2048,256]{1,0:T(8,128)(2,1)S(1)} %get-tuple-element.42.q_ref.refs_0_, bf16[2048,256]{1,0:T(8,128)(2,1)S(1)} %get-tuple-element.43.k_ref.refs_1_, bf16[2048,256]{1,0:T(8,128)(2,1)S(1)} %get-tuple-element.44.v_ref.refs_2_), custom_call_target="tpu_custom_call" | custom-call | flops 20000000000 | bytes 6291456 | tf_op jit(solution)/shard_map/pallas_call | solution.py:132
  118.1 22.1 %collective-permute-start.7 = (bf16[512,256]{1,0:T(8,128)(2,1)S(1)}, bf16[512,256]{1,0:T(8,128)(2,1)}, u32[]{:S(2)}, u32[]{:S(2)}) collective-permute-start(bf16[512,256]{1,0:T(8,128)(2,1)S(1)} %get-tuple-element.85), channel_id=1, source_target_pairs={{0,5},{1,4},{4,1},{5,0},{2,7},{3,6},{6,3},{7,2},{8,13},{9,12},{12,... | collective-permute-start | bytes 786440 | tf_op jit(solution)/shard_map/ppermute | solution.py:514
  142.9 22.0 %collective-permute-done.7 = bf16[512,256]{1,0:T(8,128)(2,1)} collective-permute-done((bf16[512,256]{1,0:T(8,128)(2,1)S(1)}, bf16[512,256]{1,0:T(8,128)(2,1)}, u32[]{:S(2)}, u32[]{:S(2)}) %collective-permute-start.7) | collective-permute-done | bytes 262176 | tf_op jit(solution)/shard_map/ppermute | solution.py:514
  172.6 13.0 %all-gather.6.cloned.1.call-done = bf16[1024,2048]{1,0:T(8,128)(2,1)} async-done(((bf16[1024,128]{1,0:T(8,128)(2,1)}), bf16[1024,2048]{1,0:T(8,128)(2,1)}) %all-gather.6.cloned.1.call-update) | async-done | bytes 4194320 | tf_op jit(solution)/shard_map/all_gather | solution.py:574
  185.6 12.0 %multiply_convert_fusion.1 = (bf16[1024,2048]{1,0:T(8,128)(2,1)}, f32[1024,2048]{1,0:T(8,128)}) fusion(bf16[1024,2048]{1,0:T(8,128)(2,1)} %all-gather.6.cloned.1.call-done, bf16[512,1024]{1,0:T(8,128)(2,1)S(1)} %collective-permute-done.8, bf16[512,1024]{1,0:T(8,128)(2,1)S(1)} %add_convert_fusion.2), kind=kOutput, calls=%fused_computation.9 | convolution fusion | flops 4318035968 | bytes 18874368 | tf_op jit(solution)/shard_map/dot_general | solution.py:501
  197.6 67.0 %all-gather.8.cloned.1.call-done = bf16[2048,1024]{1,0:T(8,128)(2,1)} async-done(((bf16[128,1024]{1,0:T(8,128)(2,1)}), bf16[2048,1024]{1,0:T(8,128)(2,1)}) %all-gather.8.cloned.1.call-update) | async-done | bytes 4194320 | tf_op jit(solution)/shard_map/all_gather | solution.py:575
  264.6 5.3 fusion.34
  281.6 22.1 %collective-permute-start.13 = (bf16[512,1024]{1,0:T(8,128)(2,1)S(1)}, bf16[512,1024]{1,0:T(8,128)(2,1)S(1)}, u32[]{:S(2)}, u32[]{:S(2)}) collective-permute-start(bf16[512,1024]{1,0:T(8,128)(2,1)S(1)} %get-tuple-element.82), channel_id=1, source_target_pairs={{0,4},{4,0},{1,5},{5,1},{2,6},{6,2},{3,7},{7,3},{8,12},{12,8},{9,1... | collective-permute-start | bytes 3145736 | tf_op jit(solution)/shard_map/ppermute | solution.py:505
  306.0 12.7 %multiply_convert_fusion = bf16[1024,2048]{1,0:T(8,128)(2,1)S(1)} fusion(bf16[2048,1024]{1,0:T(8,128)(2,1)S(1)} %copy-done.49, f32[1024,2048]{1,0:T(8,128)} %get-tuple-element.103, bf16[512,1024]{1,0:T(8,128)(2,1)S(1)} %collective-permute-done.13, bf16[512,1024]{1,0:T(8,128)(2,1)S(1)} %get-tuple-element.82), kind=kOutput, calls=%fused_computation.8 | convolution fusion | flops 4343201792 | bytes 18874368 | tf_op jit(solution)/shard_map/dot_general | solution.py:501
  322.5 9.2 %convolution_convert_fusion.1 = bf16[2048,1024]{1,0:T(8,128)(2,1)} fusion(bf16[1024,2048]{1,0:T(8,128)(2,1)} %copy-done.57, bf16[512,1024]{1,0:T(8,128)(2,1)} %copy-done.53, bf16[512,1024]{1,0:T(8,128)(2,1)S(1)} %add_convert_fusion.2), kind=kOutput, calls=%fused_computation.11 | convolution fusion | flops 4301258752 | bytes 10485760 | tf_op jit(solution)/shard_map/dot_general | solution.py:501
  351.3 6.2 convolution_convert_fusion
  360.5 127.8 %shard_map.166 = (bf16[2048,768]{1,0:T(8,128)(2,1)}, bf16[2,2,2,128,1024]{4,3,2,1,0:T(8,128)(2,1)}, bf16[2,2,2,32,1024]{4,3,2,1,0:T(8,128)(2,1)}, bf16[2,2,2,128,1024]{4,3,2,1,0:T(8,128)(2,1)}) custom-call(bf16[2048,256]{1,0:T(8,128)(2,1)} %copy-done.7, bf16[2048,256]{1,0:T(8,128)(2,1)} %copy-done.8, bf16[2048,256]{1,0:T(8,128)(2,1)} %copy-done.9, ...), custom_call_target="tpu_custom_call" | custom-call | flops 99999997952 | bytes 33554432 | tf_op jit(solution)/shard_map/pallas_call | solution.py:456
  488.3 6.3 fusion.93
  498.1 5.2 convolution_convert_fusion.2
  503.4 12.9 %collective-permute-done.22 = bf16[512,768]{1,0:T(8,128)(2,1)S(1)} collective-permute-done((bf16[512,768]{1,0:T(8,128)(2,1)S(1)}, bf16[512,768]{1,0:T(8,128)(2,1)S(1)}, u32[]{:S(2)}, u32[]{:S(2)}) %collective-permute-start.22) | collective-permute-done | bytes 786464 | tf_op jit(solution)/shard_map/ppermute | solution.py:505
  520.3 7.2 %collective-permute-done.23 = bf16[256,768]{1,0:T(8,128)(2,1)S(1)} collective-permute-done((bf16[256,768]{1,0:T(8,128)(2,1)S(1)}, bf16[256,768]{1,0:T(8,128)(2,1)S(1)}, u32[]{:S(2)}, u32[]{:S(2)}) %collective-permute-start.23) | collective-permute-done | bytes 393248 | tf_op jit(solution)/shard_map/ppermute | solution.py:505
  528.6 25.3 %collective-permute-start.25 = (bf16[128,768]{1,0:T(8,128)(2,1)S(1)}, bf16[128,768]{1,0:T(8,128)(2,1)S(1)}, u32[]{:S(2)}, u32[]{:S(2)}) collective-permute-start(bf16[128,768]{1,0:T(8,128)(2,1)S(1)} %select_convert_fusion.2), channel_id=1, source_target_pairs={{0,4},{4,0},{1,5},{5,1},{2,6},{6,2},{3,7},{7,3},{8,12},{12,8},{9,1... | collective-permute-start | bytes 589832 | tf_op jit(solution)/shard_map/ppermute | solution.py:505
  565.5 5.3 copy.46
  576.7 8.3 %collective-permute-done.20 = bf16[512,1024]{1,0:T(8,128)(2,1)S(1)} collective-permute-done((bf16[512,1024]{1,0:T(8,128)(2,1)}, bf16[512,1024]{1,0:T(8,128)(2,1)S(1)}, u32[]{:S(2)}, u32[]{:S(2)}) %collective-permute-start.20) | collective-permute-done | bytes 1048608 | tf_op jit(solution)/shard_map/ppermute | solution.py:505
  602.0 39.2 %psum.7 = f32[8,1024]{1,0:T(8,128)S(1)} all-reduce(f32[8,1024]{1,0:T(8,128)S(1)} %stack.35), channel_id=1, replica_groups=mesh['g0'=2,'g1'=2,'b'=2,'h'=2,'l'=2] {'g0','g1','b','h','l'}, use_global_device_ids=true, to_apply=%region_24.25 | all-reduce | flops 8192 | bytes 65536 | tf_op jit(solution)/shard_map/psum | solution.py:708
  (262 shorter events, 127.8 us)
Async XLA Ops:
  7.2 133.0 %all-gather.4.cloned.1.call-start = ((), (), s32[]{:S(2)}) async-start(), calls=%async_computation | async-start | bytes 2162688 | tf_op jit(solution)/shard_map/all_gather | solution.py:569
  8.9 176.8 %all-gather.6.cloned.1.call-start = ((), (), s32[]{:S(2)}) async-start(), calls=%async_computation.1 | async-start | bytes 4456448 | tf_op jit(solution)/shard_map/all_gather | solution.py:574
  9.8 254.9 %all-gather.8.cloned.1.call-start = ((), (), s32[]{:S(2)}) async-start(), calls=%async_computation.2 | async-start | bytes 4456448 | tf_op jit(solution)/shard_map/all_gather | solution.py:575
  11.7 43.5 %collective-permute-start.1 = (bf16[512,1024]{1,0:T(8,128)(2,1)S(1)}, bf16[512,1024]{1,0:T(8,128)(2,1)}, u32[]{:S(2)}, u32[]{:S(2)}) collective-permute-start(bf16[512,1024]{1,0:T(8,128)(2,1)S(1)} %collective-permute-done.x_ref), channel_id=1, source_target_pairs={{0,1},{1,0},{2,3},{3,2},{4,5},{5,4},{6,7},{7,6},{8,9},{9,8},{10,11... | collective-permute-start | bytes 3145736 | tf_op jit(solution)/shard_map/ppermute | solution.py:505
  19.9 52.8 %collective-permute-start.3 = (bf16[1024,768]{1,0:T(8,128)(2,1)}, bf16[1024,768]{1,0:T(8,128)(2,1)}, u32[]{:S(2)}, u32[]{:S(2)}) collective-permute-start(bf16[1024,768]{1,0:T(8,128)(2,1)} %copy.41), channel_id=1, source_target_pairs={{0,0},{2,4},{4,2},{6,6},{1,1},{3,5},{5,3},{7,7},{8,8},{10,12},{12,... | collective-permute-start | bytes 4718600 | tf_op jit(solution)/shard_map/ppermute | solution.py:509
  35.0 42.4 %collective-permute-start.4 = (bf16[512,1024]{1,0:T(8,128)(2,1)S(1)}, bf16[512,1024]{1,0:T(8,128)(2,1)S(1)}, u32[]{:S(2)}, u32[]{:S(2)}) collective-permute-start(bf16[512,1024]{1,0:T(8,128)(2,1)S(1)} %collective-permute-done.x_ref), channel_id=1, source_target_pairs={{0,4},{4,0},{1,5},{5,1},{2,6},{6,2},{3,7},{7,3},{8,12},{12,8},{9,1... | collective-permute-start | bytes 3145736 | tf_op jit(solution)/shard_map/ppermute | solution.py:505
  55.2 29.2 %collective-permute-start.2 = (bf16[512,1024]{1,0:T(8,128)(2,1)}, bf16[512,1024]{1,0:T(8,128)(2,1)S(1)}, u32[]{:S(2)}, u32[]{:S(2)}) collective-permute-start(bf16[512,1024]{1,0:T(8,128)(2,1)} %collective-permute-done.1.x_ref), channel_id=1, source_target_pairs={{0,4},{4,0},{1,5},{5,1},{2,6},{6,2},{3,7},{7,3},{8,12},{12,8},{9,1... | collective-permute-start | bytes 3145736 | tf_op jit(solution)/shard_map/ppermute | solution.py:505
  118.1 23.8 %collective-permute-start.6 = (bf16[512,256]{1,0:T(8,128)(2,1)}, bf16[512,256]{1,0:T(8,128)(2,1)S(1)}, u32[]{:S(2)}, u32[]{:S(2)}) collective-permute-start(bf16[512,256]{1,0:T(8,128)(2,1)} %get-tuple-element.86), channel_id=1, source_target_pairs={{0,1},{1,0},{4,5},{5,4},{2,3},{3,2},{6,7},{7,6},{8,9},{9,8},{12,13... | collective-permute-start | bytes 786440 | tf_op jit(solution)/shard_map/ppermute | solution.py:514
  118.1 46.8 %collective-permute-start.7 = (bf16[512,256]{1,0:T(8,128)(2,1)S(1)}, bf16[512,256]{1,0:T(8,128)(2,1)}, u32[]{:S(2)}, u32[]{:S(2)}) collective-permute-start(bf16[512,256]{1,0:T(8,128)(2,1)S(1)} %get-tuple-element.85), channel_id=1, source_target_pairs={{0,5},{1,4},{4,1},{5,0},{2,7},{3,6},{6,3},{7,2},{8,13},{9,12},{12,... | collective-permute-start | bytes 786440 | tf_op jit(solution)/shard_map/ppermute | solution.py:514
  281.6 24.4 %collective-permute-start.13 = (bf16[512,1024]{1,0:T(8,128)(2,1)S(1)}, bf16[512,1024]{1,0:T(8,128)(2,1)S(1)}, u32[]{:S(2)}, u32[]{:S(2)}) collective-permute-start(bf16[512,1024]{1,0:T(8,128)(2,1)S(1)} %get-tuple-element.82), channel_id=1, source_target_pairs={{0,4},{4,0},{1,5},{5,1},{2,6},{6,2},{3,7},{7,3},{8,12},{12,8},{9,1... | collective-permute-start | bytes 3145736 | tf_op jit(solution)/shard_map/ppermute | solution.py:505
  322.1 9.5 %collective-permute-start.14 = (bf16[512,1024]{1,0:T(8,128)(2,1)}, bf16[512,1024]{1,0:T(8,128)(2,1)}, u32[]{:S(2)}, u32[]{:S(2)}) collective-permute-start(bf16[512,1024]{1,0:T(8,128)(2,1)} %fusion.37), channel_id=1, source_target_pairs={{0,4},{4,0},{1,5},{5,1},{2,6},{6,2},{3,7},{7,3},{8,12},{12,8},{9,1... | collective-permute-start | bytes 3145736 | tf_op jit(solution)/shard_map/ppermute | solution.py:505
  344.3 13.3 %collective-permute-start.15 = (bf16[512,256]{1,0:T(8,128)(2,1)S(1)}, bf16[512,256]{1,0:T(8,128)(2,1)S(1)}, u32[]{:S(2)}, u32[]{:S(2)}) collective-permute-start(bf16[512,256]{1,0:T(8,128)(2,1)S(1)} %convolution_convert_fusion.10), channel_id=1, source_target_pairs={{0,5},{1,4},{4,1},{5,0},{2,7},{3,6},{6,3},{7,2},{8,13},{9,12},{12,... | collective-permute-start | bytes 786440 | tf_op jit(solution)/shard_map/ppermute | solution.py:514
  344.8 13.7 %collective-permute-start.16 = (bf16[512,256]{1,0:T(8,128)(2,1)S(1)}, bf16[512,256]{1,0:T(8,128)(2,1)S(1)}, u32[]{:S(2)}, u32[]{:S(2)}) collective-permute-start(bf16[512,256]{1,0:T(8,128)(2,1)S(1)} %convolution_convert_fusion.9), channel_id=1, source_target_pairs={{0,1},{1,0},{4,5},{5,4},{2,3},{3,2},{6,7},{7,6},{8,9},{9,8},{12,13... | collective-permute-start | bytes 786440 | tf_op jit(solution)/shard_map/ppermute | solution.py:514
  347.1 11.4 %collective-permute-start.17 = (bf16[512,256]{1,0:T(8,128)(2,1)S(1)}, bf16[512,256]{1,0:T(8,128)(2,1)S(1)}, u32[]{:S(2)}, u32[]{:S(2)}) collective-permute-start(bf16[512,256]{1,0:T(8,128)(2,1)S(1)} %convolution_convert_fusion.8), channel_id=1, source_target_pairs={{0,4},{1,5},{4,0},{5,1},{2,6},{3,7},{6,2},{7,3},{8,12},{9,13},{12,... | collective-permute-start | bytes 786440 | tf_op jit(solution)/shard_map/ppermute | solution.py:514
  350.8 8.3 %collective-permute-start.18 = (bf16[4,128,1024]{2,1,0:T(8,128)(2,1)S(1)}, bf16[4,128,1024]{2,1,0:T(8,128)(2,1)S(1)}, u32[]{:S(2)}, u32[]{:S(2)}) collective-permute-start(bf16[4,128,1024]{2,1,0:T(8,128)(2,1)S(1)} %dynamic-slice_bitcast_fusion), channel_id=1, source_target_pairs={{0,4},{4,0},{1,5},{5,1},{2,6},{6,2},{3,7},{7,3},{8,12},{12,8},{9,1... | collective-permute-start | bytes 3145736 | tf_op jit(solution)/shard_map/ppermute | solution.py:505
  496.4 20.0 %collective-permute-start.22 = (bf16[512,768]{1,0:T(8,128)(2,1)S(1)}, bf16[512,768]{1,0:T(8,128)(2,1)S(1)}, u32[]{:S(2)}, u32[]{:S(2)}) collective-permute-start(bf16[512,768]{1,0:T(8,128)(2,1)S(1)} %select_convert_fusion), channel_id=1, source_target_pairs={{0,16},{16,0},{1,17},{17,1},{2,18},{18,2},{3,19},{19,3},{4,20},{20... | collective-permute-start | bytes 2359304 | tf_op jit(solution)/shard_map/ppermute | solution.py:505
  503.2 52.3 %collective-permute-start.19 = (bf16[1024,1024]{1,0:T(8,128)(2,1)}, bf16[1024,1024]{1,0:T(8,128)(2,1)}, u32[]{:S(2)}, u32[]{:S(2)}) collective-permute-start(bf16[1024,1024]{1,0:T(8,128)(2,1)} %convolution_convert_fusion.2), channel_id=1, source_target_pairs={{0,4},{4,0},{1,5},{5,1},{2,6},{6,2},{3,7},{7,3},{8,12},{12,8},{9,1... | collective-permute-start | bytes 6291464 | tf_op jit(solution)/shard_map/ppermute | solution.py:505
  516.7 10.7 %collective-permute-start.23 = (bf16[256,768]{1,0:T(8,128)(2,1)S(1)}, bf16[256,768]{1,0:T(8,128)(2,1)S(1)}, u32[]{:S(2)}, u32[]{:S(2)}) collective-permute-start(bf16[256,768]{1,0:T(8,128)(2,1)S(1)} %select_convert_fusion.1), channel_id=1, source_target_pairs={{0,8},{8,0},{1,9},{9,1},{2,10},{10,2},{3,11},{11,3},{4,12},{12,4},... | collective-permute-start | bytes 1179656 | tf_op jit(solution)/shard_map/ppermute | solution.py:505
  518.4 35.5 %collective-permute-start.10 = (bf16[512,1024]{1,0:T(8,128)(2,1)}, bf16[512,1024]{1,0:T(8,128)(2,1)S(1)}, u32[]{:S(2)}, u32[]{:S(2)}) collective-permute-start(bf16[512,1024]{1,0:T(8,128)(2,1)} %get-tuple-element.83), channel_id=1, source_target_pairs={{0,0},{2,4},{4,2},{6,6},{1,1},{3,5},{5,3},{7,7},{8,8},{10,12},{12,... | collective-permute-start | bytes 3145736 | tf_op jit(solution)/shard_map/ppermute | solution.py:509
  528.6 26.3 %collective-permute-start.25 = (bf16[128,768]{1,0:T(8,128)(2,1)S(1)}, bf16[128,768]{1,0:T(8,128)(2,1)S(1)}, u32[]{:S(2)}, u32[]{:S(2)}) collective-permute-start(bf16[128,768]{1,0:T(8,128)(2,1)S(1)} %select_convert_fusion.2), channel_id=1, source_target_pairs={{0,4},{4,0},{1,5},{5,1},{2,6},{6,2},{3,7},{7,3},{8,12},{12,8},{9,1... | collective-permute-start | bytes 589832 | tf_op jit(solution)/shard_map/ppermute | solution.py:505
  559.6 25.3 %collective-permute-start.20 = (bf16[512,1024]{1,0:T(8,128)(2,1)}, bf16[512,1024]{1,0:T(8,128)(2,1)S(1)}, u32[]{:S(2)}, u32[]{:S(2)}) collective-permute-start(bf16[512,1024]{1,0:T(8,128)(2,1)} %add_convert_fusion), channel_id=1, source_target_pairs={{0,1},{1,0},{2,3},{3,2},{4,5},{5,4},{6,7},{7,6},{8,9},{9,8},{10,11... | collective-permute-start | bytes 3145736 | tf_op jit(solution)/shard_map/ppermute | solution.py:505
  563.0 11.2 %collective-permute-start.27 = (bf16[256,768]{1,0:T(8,128)(2,1)S(1)}, bf16[256,768]{1,0:T(8,128)(2,1)S(1)}, u32[]{:S(2)}, u32[]{:S(2)}) collective-permute-start(bf16[256,768]{1,0:T(8,128)(2,1)S(1)} %maximum_select_fusion.4), channel_id=1, source_target_pairs={{0,8},{8,0},{1,9},{9,1},{2,10},{10,2},{3,11},{11,3},{4,12},{12,4},... | collective-permute-start | bytes 1179656 | tf_op jit(solution)/shard_map/ppermute | solution.py:505
  575.3 19.4 %collective-permute-start.28 = (bf16[512,768]{1,0:T(8,128)(2,1)}, bf16[512,768]{1,0:T(8,128)(2,1)}, u32[]{:S(2)}, u32[]{:S(2)}) collective-permute-start(bf16[512,768]{1,0:T(8,128)(2,1)} %maximum_select_fusion.2), channel_id=1, source_target_pairs={{0,16},{16,0},{1,17},{17,1},{2,18},{18,2},{3,19},{19,3},{4,20},{20... | collective-permute-start | bytes 2359304 | tf_op jit(solution)/shard_map/ppermute | solution.py:505
  589.4 52.4 %collective-permute-start.21 = (bf16[512,1024]{1,0:T(8,128)(2,1)}, bf16[512,1024]{1,0:T(8,128)(2,1)S(1)}, u32[]{:S(2)}, u32[]{:S(2)}) collective-permute-start(bf16[512,1024]{1,0:T(8,128)(2,1)} %fusion.15), channel_id=1, source_target_pairs={{0,0},{2,4},{4,2},{6,6},{1,1},{3,5},{5,3},{7,7},{8,8},{10,12},{12,... | collective-permute-start | bytes 3145736 | tf_op jit(solution)/shard_map/ppermute | solution.py:509
  (67 other events, 1082.7 us)
Sparse Core Ops, SparseCore 0:
  11.4 73.4 all-gather.3
  88.2 97.4 all-gather.5
  189.0 75.6 all-gather.7

commit v3 on v2

--- a/solution.py
+++ b/solution.py
@@ -32,126 +32,6 @@
     )
 
 
-def qkv_kernel(place_ref, x_ref, w_ref, gain_ref, shift_ref, cos_ref, sin_ref, *refs):
-    q_ref, k_ref, v_ref, normed_ref = refs[-4:]
-    width = q_ref.shape[1]
-    value = x_ref[...].astype(f32)
-    center = value - jnp.mean(value, axis=1, keepdims=True)
-    inverse = lax.rsqrt(jnp.mean(center * center, axis=1, keepdims=True) + EPS)
-    normed = (center * inverse * gain_ref[...] + shift_ref[...]).astype(bf16)
-    normed_ref[...] = normed
-    mixed = jnp.dot(normed, w_ref[...], preferred_element_type=f32)
-    cosine, sine = cos_ref[...], sin_ref[...]
-    query, key = mixed[:, :width], mixed[:, width : 2 * width]
-    query = HEAD_DIM ** (-0.5) * (query * cosine + swap_halves(query, -1.0) * sine)
-    q_ref[...] = query.astype(bf16)
-    k_ref[...] = (key * cosine + swap_halves(key, -1.0) * sine).astype(bf16)
-    v_ref[...] = mixed[:, 2 * width :].astype(bf16)
-
-
-def project(place, x, w, gain, shift, cosine, sine, length, filled, rows=256):
-    part, depth = x.shape
-    width = w.shape[1] // 3
-    steps = part // rows
-
-    def there(i, place_ref):
-        return (place_ref[0] * steps + i, 0)
-
-    def whole(i, place_ref):
-        return (0, 0)
-
-    return pl.pallas_call(
-        qkv_kernel,
-        out_shape=tuple(
-            jax.ShapeDtypeStruct((length, n), bf16) for n in (width, width, width, depth)
-        ),
-        grid_spec=pltpu.PrefetchScalarGridSpec(
-            num_scalar_prefetch=1,
-            grid=(steps,),
-            in_specs=[
-                pl.BlockSpec((rows, depth), lambda i, place_ref: (i, 0)),
-                pl.BlockSpec(w.shape, whole),
-                pl.BlockSpec((1, depth), whole),
-                pl.BlockSpec((1, depth), whole),
-                pl.BlockSpec((rows, width), there),
-                pl.BlockSpec((rows, width), there),
-            ]
-            + [pl.BlockSpec(memory_space=pl.ANY)] * len(filled),
-            out_specs=tuple(pl.BlockSpec((rows, n), there) for n in (width, width, width, depth)),
-        ),
-        input_output_aliases={7 + i: i for i in range(len(filled))},
-        compiler_params=pltpu.CompilerParams(vmem_limit_bytes=40 * 2**20),
-        cost_estimate=pl.CostEstimate(
-            flops=2 * part * depth * 3 * width, bytes_accessed=5 * 2**20, transcendentals=0
-        ),
-    )(place, x, w, gain, shift, cosine, sine, *filled)
-
-
-def forward_kernel(q_ref, k_ref, v_ref, o_ref, lse_ref, *, rows, blocks):
-    width = q_ref.shape[1]
-    heads = width // HEAD_DIM
-
-    def branch(last):
-        n = (last + 1) * rows
-        acc = jnp.zeros((rows, width), f32)
-        logs = jnp.zeros((rows, width), f32)
-        for h in range(heads):
-            mine = head_lanes((rows, width), h)
-            qm = jnp.where(mine, q_ref[...], jnp.zeros((), bf16))
-            s = lax.dot_general(qm, k_ref[:n], NT, preferred_element_type=f32)
-            row = lax.broadcasted_iota(jnp.int32, (rows, rows), 0)
-            column = lax.broadcasted_iota(jnp.int32, (rows, rows), 1)
-            tail = jnp.where(column <= row, s[:, n - rows :], -1e30)
-            top = jnp.max(tail, axis=1, keepdims=True)
-            if last:
-                top = jnp.maximum(top, jnp.max(s[:, : n - rows], axis=1, keepdims=True))
-            top = top * LOG2E
-            vm = jnp.where(head_lanes((n, width), h), v_ref[:n], jnp.ones((), bf16))
-            low = jnp.exp2(tail * LOG2E - top).astype(bf16)
-            out = lax.dot_general(low, vm[n - rows :], NN, preferred_element_type=f32)
-            if last:
-                low = jnp.exp2(s[:, : n - rows] * LOG2E - top).astype(bf16)
-                out = out + lax.dot_general(low, vm[: n - rows], NN, preferred_element_type=f32)
-            total = pltpu.roll(out, HEAD_DIM, 1)
-            acc = jnp.where(mine, out / total, acc)
-            logs = jnp.where(mine, top + jnp.log2(total), logs)
-        o_ref[...] = acc.astype(bf16)
-        lane = lax.broadcasted_iota(jnp.int32, (8, width), 1)
-        pick = (lane == HEAD_DIM * lax.broadcasted_iota(jnp.int32, (8, width), 0)).astype(f32)
-        lse_ref[...] = lax.dot_general(
-            pick, logs, NT, precision=lax.Precision.HIGHEST, preferred_element_type=f32
-        )
-
-    for i in range(blocks):
-        pl.when(pl.program_id(0) == i)(functools.partial(branch, i))
-
-
-def attend_forward(q, k, v, rows=BLOCK):
-    length, width = q.shape
-    blocks = length // rows
-    return pl.pallas_call(
-        functools.partial(forward_kernel, rows=rows, blocks=blocks),
-        grid=(blocks,),
-        out_shape=(
-            jax.ShapeDtypeStruct((length, width), bf16),
-            jax.ShapeDtypeStruct((8, length), f32),
-        ),
-        in_specs=[
-            pl.BlockSpec((rows, width), lambda i: (i, 0)),
-            pl.BlockSpec((length, width), lambda i: (0, 0)),
-            pl.BlockSpec((length, width), lambda i: (0, 0)),
-        ],
-        out_specs=(
-            pl.BlockSpec((rows, width), lambda i: (i, 0)),
-            pl.BlockSpec((8, rows), lambda i: (0, i)),
-        ),
-        compiler_params=pltpu.CompilerParams(vmem_limit_bytes=48 * 2**20),
-        cost_estimate=pl.CostEstimate(
-            flops=20_000_000_000, bytes_accessed=6 * 2**20, transcendentals=0
-        ),
-    )(q, k, v)
-
-
 MESH = pl.DeviceIdType.MESH
 
 
@@ -159,9 +39,10 @@
     def __init__(self, send, recv):
         self.send, self.recv, self.made = send, recv, {}
 
-    def start(self, name, source, target, device):
-        n = len(self.made)
-        copy = pltpu.make_async_remote_copy(
+    def describe(self, name):
+        n, build = self.made[name]
+        source, target, device = build()
+        return pltpu.make_async_remote_copy(
             src_ref=source,
             dst_ref=target,
             send_sem=self.send.at[n],
@@ -169,15 +50,25 @@
             device_id=device,
             device_id_type=MESH,
         )
-        self.made[name] = copy
-        copy.start()
+
+    def plan(self, name, build):
+        self.made[name] = (len(self.made), build)
+
+    def start(self, name, build=None):
+        if build is not None:
+            self.plan(name, build)
+        self.describe(name).start()
 
     def arrived(self, name):
-        self.made[name].wait_recv()
-
-    def drain(self):
-        for copy in self.made.values():
-            copy.wait_send()
+        self.describe(name).wait_recv()
+
+    def sent(self, name):
+        self.describe(name).wait_send()
+
+    def drain(self, but=()):
+        for name in self.made:
+            if name not in but:
+                self.sent(name)
 
 
 def flip(axis):
@@ -265,9 +156,11 @@
         for a in range(3):
             copies.start(
                 ("plane", a, k, stage),
-                source(a, k, stage, 1),
-                partial[a][stage].at[k % 4],
-                flip(groups[orders[a][stage]]),
+                lambda a=a: (
+                    source(a, k, stage, 1),
+                    partial[a][stage].at[k % 4],
+                    flip(groups[orders[a][stage]]),
+                ),
             )
 
     def plane_add(k, stage):
@@ -278,7 +171,10 @@
     def ring_send(step):
         for a in range(3):
             held = partial[a][bits - 1].at[1] if step == 1 else passing[a].at[step - 2]
-            copies.start(("ring", a, step), held, passing[a].at[step - 1], next_layer(1))
+            target = passing[a].at[step - 1]
+            copies.start(
+                ("ring", a, step), lambda held=held, target=target: (held, target, next_layer(1))
+            )
 
     def ring_add(step):
         for a in range(3):
@@ -292,8 +188,11 @@
                 place[axis] if order.index(axis) >= stage else slice(None) for axis in range(bits)
             )
             held = passing[a].at[2] if stage == 0 else results[a].at[(core,) + at]
+            spot = results[a].at[(core,) + at]
+            axis = groups[order[stage]]
             copies.start(
-                ("gather", a, stage), held, results[a].at[(core,) + at], flip(groups[order[stage]])
+                ("gather", a, stage),
+                lambda held=held, spot=spot, axis=axis: (held, spot, flip(axis)),
             )
 
     def core_send(stage):
@@ -310,7 +209,7 @@
                     at.append(slice(None))
             spot = results[a].at[(core,) + tuple(at)]
             held = passing[a].at[2] if stage == 0 else spot
-            copies.start(("core", a, stage), held, spot, flip("b"))
+            copies.start(("core", a, stage), lambda held=held, spot=spot: (held, spot, flip("b")))
 
     greet(groups)
     length, width = q_ref.shape
@@ -379,7 +278,9 @@
     tiles(8 * count // 10, count)
 
     def turn_back(grad, at):
-        return grad * cos_ref[at] + swap_halves(grad, 1.0) * sin_ref[at]
+        cosine = jnp.concatenate([cos_ref[at]] * (width // 128), axis=1)
+        sine = jnp.concatenate([sin_ref[at]] * (width // 128), axis=1)
+        return grad * cosine + swap_halves(grad, 1.0) * sine
 
     @pl.loop(0, blocks)
     def _(i):
@@ -468,6 +369,410 @@
         ),
     )(q, k, v, o, do, lse, cosine, sine, up, out, down)
 
+def exclusive(a, b):
+    return a + b - 2 * a * b
+
+
+def forward_branch(last, heads, rows, q_ref, k_ref, v_ref, o_ref, lse_ref):
+    width = q_ref.shape[1]
+    n = (last + 1) * rows
+    block = pl.ds(last * rows, rows)
+    acc = jnp.zeros((rows, width), f32)
+    logs = jnp.zeros((rows, width), f32)
+    for h in range(heads):
+        mine = head_lanes((rows, width), h)
+        qm = jnp.where(mine, q_ref[block], jnp.zeros((), bf16))
+        s = lax.dot_general(qm, k_ref[:n], NT, preferred_element_type=f32)
+        row = lax.broadcasted_iota(jnp.int32, (rows, rows), 0)
+        column = lax.broadcasted_iota(jnp.int32, (rows, rows), 1)
+        tail = jnp.where(column <= row, s[:, n - rows :], -1e30)
+        top = jnp.max(tail, axis=1, keepdims=True)
+        if last:
+            top = jnp.maximum(top, jnp.max(s[:, : n - rows], axis=1, keepdims=True))
+        top = top * LOG2E
+        vm = jnp.where(head_lanes((n, width), h), v_ref[:n], jnp.ones((), bf16))
+        low = jnp.exp2(tail * LOG2E - top).astype(bf16)
+        out = lax.dot_general(low, vm[n - rows :], NN, preferred_element_type=f32)
+        if last:
+            low = jnp.exp2(s[:, : n - rows] * LOG2E - top).astype(bf16)
+            out = out + lax.dot_general(low, vm[: n - rows], NN, preferred_element_type=f32)
+        total = pltpu.roll(out, HEAD_DIM, 1)
+        acc = jnp.where(mine, out / total, acc)
+        logs = jnp.where(mine, top + jnp.log2(total), logs)
+    o_ref[block] = acc.astype(bf16)
+    lane = lax.broadcasted_iota(jnp.int32, (8, width), 1)
+    pick = (lane == HEAD_DIM * lax.broadcasted_iota(jnp.int32, (8, width), 0)).astype(f32)
+    lse_ref[:, block] = lax.dot_general(
+        pick, logs, NT, precision=lax.Precision.HIGHEST, preferred_element_type=f32
+    )
+
+
+def front_kernel(*refs, groups, chunks):
+    (
+        tok_ref, cot_ref, wq_ref, up_ref, out_ref, down_ref, gain_ref, shift_ref, cos_ref, sin_ref,
+        q_ref, k_ref, v_ref, whole_ref, o_ref, lse_ref,
+        heads_ref, tok_home, cot_home, w_home, up_all, out_all, down_all,
+        row, w_att, send, recv, local, head_send, head_recv,
+    ) = refs
+    bits = len(groups)
+    part = tok_ref.shape[0]
+    depth = tok_ref.shape[1]
+    width = q_ref.shape[1]
+    heads = width // HEAD_DIM
+    core, half, near = lax.axis_index("b"), lax.axis_index("h"), lax.axis_index("l")
+    group = [lax.axis_index(axis) for axis in groups]
+    layer = 2 * half + near
+    place = 2 * core + near
+    stays = core == half
+    moves = core != half
+    partner = {"b": half, "h": core}
+    copies = Copies(send, recv)
+    locals_made, here = [], []
+
+    def copy_here(source, target):
+        copy = pltpu.make_async_copy(source, target, local.at[len(locals_made)])
+        locals_made.append(copy)
+        here.append(copy)
+        copy.start()
+
+    barrier = pltpu.get_barrier_semaphore()
+    friends = [flip(axis) for axis in groups + ("b",)] + [next_layer(1), next_layer(3)]
+    friends += [flip("l"), {"b": 1 - core, "l": 1 - near}]
+    for friend in friends:
+        pl.semaphore_signal(barrier, inc=1, device_id=friend, device_id_type=MESH)
+
+    @pl.when(moves)
+    def _():
+        pl.semaphore_signal(barrier, inc=1, device_id=partner, device_id_type=MESH)
+        pl.semaphore_wait(barrier, len(friends) + 1)
+
+    @pl.when(stays)
+    def _():
+        pl.semaphore_wait(barrier, len(friends))
+
+    size = part // chunks
+
+    def piece(c):
+        return pl.ds(c * size, size)
+
+    own = [
+        pltpu.make_async_copy(tok_ref.at[piece(c)], row.at[place, piece(c)], local.at[c])
+        for c in range(chunks)
+    ]
+    locals_made.extend(own)
+    turned = [("turn", c) for c in range(chunks)]
+    for c in range(chunks):
+        copies.plan(
+            turned[c],
+            lambda c=c: (tok_ref.at[piece(c)], row.at[layer, piece(c)], partner),
+        )
+    w_here = pltpu.make_async_copy(wq_ref, w_att, local.at[len(locals_made)])
+    locals_made.append(w_here)
+    copies.plan("wturn", lambda: (wq_ref.at[tuple(group)], w_att.at[tuple(group)], partner))
+    cot_here = pltpu.make_async_copy(cot_ref, cot_home, local.at[len(locals_made)])
+    locals_made.append(cot_here)
+    copies.plan("cot", lambda: (cot_ref, cot_home, partner))
+
+    @pl.when(moves)
+    def _():
+        for c in range(chunks):
+            copies.start(turned[c])
+        copies.start("wturn")
+
+    @pl.when(stays)
+    def _():
+        for c in range(chunks):
+            own[c].start()
+        w_here.start()
+
+    weights = (up_ref, out_ref, down_ref)
+    orders = [tuple(range(bits)), tuple(range(bits)), tuple(reversed(range(bits)))]
+    slab = up_ref.shape[-1] // 2
+
+    def slot(a, shard, at):
+        if a == 0:
+            return up_all.at[at + (slice(None), pl.ds(pl.multiple_of(shard * slab, slab), slab))]
+        if a == 1:
+            return out_all.at[(shard, core) + at]
+        return down_all.at[(shard,) + at]
+
+    def held(a, at):
+        if a == 0:
+            return up_ref.at[at + (slice(None), pl.ds(pl.multiple_of(core * slab, slab), slab))]
+        return weights[a].at[(core,) + at]
+
+    def shard(k):
+        return lax.rem(layer + 4 - k, 4)
+
+    def ring_send(step):
+        for a in range(3):
+
+            def build(a=a):
+                at = tuple(group)
+                spot = slot(a, shard(step - 1), at)
+                return (held(a, at) if step == 1 else spot, spot, next_layer(1))
+
+            copies.start(("ring", a, step), build)
+
+    def ring_wait(step):
+        for a in range(3):
+            copies.arrived(("ring", a, step))
+
+    def plane_send(k, stage):
+        for a in range(3):
+
+            def build(a=a):
+                order = orders[a]
+                at = tuple(
+                    group[axis] if order.index(axis) >= stage else slice(None)
+                    for axis in range(bits)
+                )
+                spot = slot(a, shard(k), at)
+                return (spot, spot, flip(groups[order[stage]]))
+
+            copies.start(("plane", a, k, stage), build)
+
+    def plane_wait(k, stage):
+        for a in range(3):
+            copies.arrived(("plane", a, k, stage))
+
+    def core_send(k):
+        def build():
+            spot = slot(1, shard(k), (slice(None),) * bits)
+            return (spot, spot, flip("b"))
+
+        copies.start(("core", k), build)
+
+    for a in range(3):
+        everything = (slice(None),) * bits
+        if a == 1:
+            copy_here(out_ref, out_all.at[layer])
+        else:
+            copy_here(held(a, everything), slot(a, layer, everything))
+
+    for c in range(chunks):
+        pl.when(moves)(functools.partial(copies.arrived, turned[c]))
+        pl.when(stays)(own[c].wait)
+        for name, axis in (("near", "l"), ("core own", "b")):
+            copies.start(
+                (name, c),
+                lambda c=c, axis=axis: (
+                    row.at[place, piece(c)],
+                    row.at[place, piece(c)],
+                    flip(axis),
+                ),
+            )
+    copy_here(row.at[place], tok_home)
+
+    @pl.when(stays)
+    def _():
+        w_here.wait()
+
+    parts = [pl.ds(i * (w_att.shape[-2] // 2), w_att.shape[-2] // 2) for i in range(2)]
+    w_orders = [orders[0], orders[2]]
+    for stage in range(bits):
+        for i in range(2):
+
+            def build(stage=stage, i=i):
+                order = w_orders[i]
+                at = tuple(
+                    group[axis] if order.index(axis) >= stage else slice(None)
+                    for axis in range(bits)
+                )
+                spot = w_att.at[at + (parts[i],)]
+                return (spot, spot, flip(groups[order[stage]]))
+
+            copies.plan(("w", stage, i), build)
+
+    @pl.when(moves)
+    def _():
+        copies.arrived("wturn")
+        for stage in range(bits):
+            for i in range(2):
+                copies.start(("w", stage, i))
+            for i in range(2):
+                copies.arrived(("w", stage, i))
+
+    copy_here(w_att, w_home)
+    near_block = 2 * core + 1 - near
+
+    def pass_on():
+        for c in range(chunks):
+            copies.arrived(("near", c))
+            copies.start(
+                ("core near", c),
+                lambda c=c: (row.at[near_block, piece(c)], row.at[near_block, piece(c)], flip("b")),
+            )
+        ring_send(1)
+
+    def wait_all(name):
+        def run():
+            for c in range(chunks):
+                copies.arrived((name, c))
+
+        return run
+
+    @pl.loop(0, 4)
+    def _(r):
+        far_core, far_near = lax.rem(r, 2), r // 2
+        block = 2 * exclusive(core, far_core) + exclusive(near, far_near)
+        pl.when(r == 1)(wait_all("core own"))
+        pl.when(r == 2)(pass_on)
+        pl.when(r == 3)(wait_all("core near"))
+
+        @pl.loop(0, 2)
+        def _(c):
+            rows = part // 2
+            inside = pl.ds(pl.multiple_of(c * rows, rows), rows)
+            at = pl.ds(pl.multiple_of(block * part + c * rows, rows), rows)
+            value = row[block, inside].astype(f32)
+            center = value - jnp.mean(value, axis=1, keepdims=True)
+            inverse = lax.rsqrt(jnp.mean(center * center, axis=1, keepdims=True) + EPS)
+            normed = (center * inverse * gain_ref[...] + shift_ref[...]).astype(bf16)
+            whole_ref[at] = normed
+            w = w_att[...].reshape(depth, 3 * width)
+            mixed = jnp.dot(normed, w, preferred_element_type=f32)
+            cosine = jnp.concatenate([cos_ref[at]] * (width // 128), axis=1)
+            sine = jnp.concatenate([sin_ref[at]] * (width // 128), axis=1)
+            query, key = mixed[:, :width], mixed[:, width : 2 * width]
+            query = HEAD_DIM ** (-0.5) * (query * cosine + swap_halves(query, -1.0) * sine)
+            q_ref[at] = query.astype(bf16)
+            k_ref[at] = (key * cosine + swap_halves(key, -1.0) * sine).astype(bf16)
+            v_ref[at] = mixed[:, 2 * width :].astype(bf16)
+
+    def head_copy(mask):
+        far_core, far_near = mask // 2, lax.rem(mask, 2)
+        to_core, to_near = exclusive(core, far_core), exclusive(near, far_near)
+        block = 2 * to_core + to_near
+        rows = pl.ds(pl.multiple_of(block * part, part), part)
+        columns = pl.ds(pl.multiple_of(place * width, width), width)
+        return pltpu.make_async_remote_copy(
+            src_ref=o_ref.at[rows],
+            dst_ref=heads_ref.at[:, columns],
+            send_sem=head_send.at[mask],
+            recv_sem=head_recv.at[mask],
+            device_id={"b": to_core, "l": to_near},
+            device_id_type=MESH,
+        )
+
+    def forward_weights():
+        ring_wait(1)
+        ring_send(2)
+        plane_send(1, 0)
+
+    @pl.loop(0, 4)
+    def _(r):
+        far_core, far_near = 1 - lax.rem(r, 2), 1 - r // 2
+        mask = 2 * far_core + far_near
+        block = 2 * exclusive(core, far_core) + exclusive(near, far_near)
+        pl.when(r == 2)(forward_weights)
+        for i in range(4):
+            pl.when(block == i)(
+                functools.partial(
+                    forward_branch, i, heads, part, q_ref, k_ref, v_ref, o_ref, lse_ref
+                )
+            )
+
+        @pl.when(r < 3)
+        def _():
+            head_copy(mask).start()
+
+    copy_here(
+        o_ref.at[pl.ds(pl.multiple_of(place * part, part), part)],
+        heads_ref.at[:, pl.ds(pl.multiple_of(place * width, width), width)],
+    )
+
+    @pl.when(moves)
+    def _():
+        copies.start("cot")
+
+    @pl.when(stays)
+    def _():
+        cot_here.start()
+
+    for k in (1, 2, 3):
+        if k > 1:
+            plane_send(k, 0)
+        for stage in range(bits):
+            plane_wait(k, stage)
+            if stage + 1 < bits:
+                plane_send(k, stage + 1)
+            if stage == 0 and k < 3:
+                ring_wait(k + 1)
+                if k < 2:
+                    ring_send(k + 2)
+        core_send(k)
+    for mask in (1, 2, 3):
+        copy = head_copy(jnp.int32(mask))
+        copy.wait_send()
+        copy.wait_recv()
+    for k in (1, 2, 3):
+        copies.arrived(("core", k))
+    sometimes = turned + ["wturn", "cot"] + [("w", s, i) for s in range(bits) for i in range(2)]
+
+    @pl.when(moves)
+    def _():
+        copies.arrived("cot")
+        for name in sometimes:
+            copies.sent(name)
+
+    @pl.when(stays)
+    def _():
+        cot_here.wait()
+
+    for copy in here:
+        copy.wait()
+    copies.drain(sometimes)
+
+
+def front(tok, cot, wq, up, out, down, gain, shift, cosine, sine, groups, chunks=2):
+    part, depth = tok.shape
+    length = 4 * part
+    width = wq.shape[-1] // 3
+    bits = len(groups)
+    vmem = pl.BlockSpec(memory_space=pltpu.VMEM)
+    anywhere = pl.BlockSpec(memory_space=pl.ANY)
+
+    def shape(*dims):
+        return jax.ShapeDtypeStruct(dims, bf16)
+
+    n = 2 * chunks + 2 + 3 * chunks + 2 * bits + 3 * 3 + 9 * bits + 3 + 4
+    return pl.pallas_call(
+        functools.partial(front_kernel, groups=groups, chunks=chunks),
+        out_shape=(
+            shape(length, width),
+            shape(length, width),
+            shape(length, width),
+            shape(length, depth),
+            shape(length, width),
+            jax.ShapeDtypeStruct((8, length), f32),
+            shape(part, depth),
+            shape(part, depth),
+            shape(part, depth),
+            shape(*wq.shape),
+            shape(*up.shape[:-1], 2 * up.shape[-1]),
+            shape(4, *out.shape),
+            shape(4, *down.shape[1:]),
+        ),
+        in_specs=[anywhere] * 6 + [vmem] * 4,
+        out_specs=(vmem,) * 6 + (anywhere,) * 7,
+        scratch_shapes=[
+            pltpu.VMEM((4, part, depth), bf16),
+            pltpu.VMEM(wq.shape, bf16),
+            pltpu.SemaphoreType.DMA((n,)),
+            pltpu.SemaphoreType.DMA((n,)),
+            pltpu.SemaphoreType.DMA((16,)),
+            pltpu.SemaphoreType.DMA((4,)),
+            pltpu.SemaphoreType.DMA((4,)),
+        ],
+        compiler_params=pltpu.CompilerParams(
+            vmem_limit_bytes=58 * 2**20, collective_id=2, has_side_effects=True
+        ),
+        cost_estimate=pl.CostEstimate(
+            flops=100_000_000_000, bytes_accessed=32 * 2**20, transcendentals=0
+        ),
+    )(tok, cot, wq, up, out, down, gain, shift, cosine, sine)
+
 
 def norm_forward(value, gain, shift):
     center = value - jnp.mean(value, axis=-1, keepdims=True)
@@ -488,10 +793,10 @@
 
 def rotary_tables(length, width):
     half = HEAD_DIM // 2
-    lane = jnp.arange(width, dtype=jnp.int32) % half
-    freqs = 10000.0 ** (-(lane.astype(f32) / half))
-    angles = jnp.arange(length, dtype=f32)[:, None] * freqs[None, :]
-    return (jnp.cos(angles), jnp.sin(angles))
+    steps = (np.arange(width) % half).astype(np.float32) / np.float32(half)
+    freqs = np.float32(10000.0) ** (-steps)
+    angles = np.arange(length, dtype=np.float32)[:, None] * freqs[None, :]
+    return (jnp.asarray(np.cos(angles)), jnp.asarray(np.sin(angles)))
 
 
 SWAP = [(0, 1), (1, 0)]
@@ -555,40 +860,28 @@
         group = 2 * group + lax.axis_index(axis)
     n_groups = 2 ** len(groups)
     stack = ("h", "l")
-    cosine, sine = rotary_tables(length, cols)
+    cosine, sine = rotary_tables(length, 128)
     gains = [norm_gains[i : i + 1] for i in range(4)]
     shifts = [norm_shifts[i : i + 1] for i in range(4)]
 
-    resid_low = turn(tokens[0])
-    w_attn = turn(w_qkv.reshape(depth, 3 * cols))
-    near_block = across(resid_low, "l")
-    blocks = [resid_low, across(resid_low, "b"), near_block, across(near_block, "b")]
-
-    slice_out = cols // (2 * n_groups)
-    out_piece = lax.dynamic_slice_in_dim(w_out, (2 * group + core) * slice_out, slice_out, 0)
-    out_whole = lax.all_gather(out_piece, stack + groups + ("b",), axis=0, tiled=True)
-    slice_unit = units // (2 * n_groups)
-    unit_at = (core * n_groups + group) * slice_unit
-    up_piece = lax.dynamic_slice_in_dim(w_up, unit_at, slice_unit, 1)
-    down_piece = lax.dynamic_slice_in_dim(w_down, unit_at, slice_unit, 0)
-    up_half = lax.all_gather(up_piece, stack + groups, axis=1, tiled=True)
-    down_half = lax.all_gather(down_piece, stack + groups, axis=0, tiled=True)
-
-    filled = ()
-    for mask, block in zip((0, 2, 1, 3), blocks):
-        filled = project(
-            jnp.reshape(place ^ mask, (1,)),
-            block,
-            w_attn,
-            gains[0],
-            shifts[0],
-            cosine,
-            sine,
-            length,
-            filled,
-        )
-    q, k, v, whole_a = filled
-    attended, lse = attend_forward(q, k, v)
+    slots = (2,) * len(groups)
+    q, k, v, whole_a, attended, lse, heads, resid_low, cotangent_low, w_attn, up_half, out_whole, down_half = front(
+        tokens[0],
+        cotangent[0],
+        w_qkv.reshape(slots + (depth // n_groups, 3 * cols)),
+        w_up.reshape(slots + (depth // n_groups, units)),
+        w_out.reshape((2,) + slots + (cols // (2 * n_groups), depth)),
+        w_down.reshape((2,) + slots + (units // (2 * n_groups), depth)),
+        gains[0],
+        shifts[0],
+        cosine,
+        sine,
+        groups,
+    )
+    up_half = up_half.reshape(depth, 2 * units)
+    out_whole = out_whole.reshape(4 * cols, depth)
+    down_half = down_half.reshape(2 * units, depth)
+    w_attn = w_attn.reshape(depth, 3 * cols)
 
     def block_of(value, mask):
         return lax.dynamic_slice_in_dim(value, (place ^ mask) * part, part, 0)
@@ -596,10 +889,7 @@
     def out_rows(mask):
         return lax.dynamic_slice_in_dim(out_whole, (place ^ mask) * cols, cols, 0)
 
-    heads = {0: block_of(attended, 0)}
-    for mask in (1, 3, 2):
-        heads[mask] = quad_swap(block_of(attended, mask), mask // 2, mask % 2)
-    branch_a = sum(dot(heads[mask], out_rows(mask)) for mask in (0, 2, 1, 3))
+    branch_a = dot(heads, out_whole)
 
     resid = resid_low.astype(f32)
     normed_a, unit_0, inverse_0 = norm_forward(resid, gains[0], shifts[0])
@@ -625,7 +915,7 @@
         corpus_ids[:, None] == jnp.arange(corpus_weight.shape[0], dtype=jnp.int32)[None, :]
     ).astype(f32)
     row_scale = turn(jnp.dot(picks, corpus_weight, precision=lax.Precision.HIGHEST))
-    grad_final = turn(cotangent[0]).astype(f32) * row_scale[:, None]
+    grad_final = cotangent_low.astype(f32) * row_scale[:, None]
     back_3, gain_3, shift_3 = norm_backward(grad_final, unit_3, inverse_3, gains[3])
     own_g = back_3.astype(bf16)
     pair_g = jnp.concatenate([own_g, across(own_g, "b")], axis=0)
@@ -648,17 +938,11 @@
         grad_attended = lax.dynamic_update_slice_in_dim(
             grad_attended, sent, (place ^ mask) * part, 0
         )
-    out_grad = jnp.zeros((4 * cols, depth), bf16)
-    for mask in range(4):
-        out_grad = lax.dynamic_update_slice_in_dim(
-            out_grad, dot(heads[mask], grad_a, TN).astype(bf16), (place ^ mask) * cols, 0
-        )
+    out_grad = dot(heads, grad_a, TN).astype(bf16)
     out_grad = out_grad.reshape(4, 2, cols // 2, depth)
     sent = lax.dynamic_index_in_dim(out_grad, 1 - core, 1, False)
     kept = lax.dynamic_index_in_dim(out_grad, core, 1, False)
     out_grad = (kept.astype(f32) + across(sent, "b").astype(f32)).astype(bf16)
-    slots = (2,) * len(groups)
-
     def pieces(value):
         return value.reshape((4,) + slots + (value.size // (4 * n_groups * depth), depth))
 

time: 661 us -> 560 us (0.85)
  Pallas kernels: 172 us -> 272 us
  waiting for transfers between devices: 137 us -> 53.6 us
  starting transfers between devices: 135 us -> 52.8 us
  between operations: 15.9 us -> 2.07 us
  matrix products: 83.6 us -> 74.4 us
  local copies, waits for them, and re-layouts: 30.3 us -> 21.8 us
    pallas_call x5 -> x1, Pallas kernels: 44.3 us -> 145 us  [front(): pl.pallas_call(functools.partial(front_kernel, groups=groups, chunks=chun...]
    all_gather x3 -> x0, waiting for transfers between devices: 80 us -> none  [the longest x1 67 us: on_device(): down_half = lax.all_gather(down_piece, stack + groups, axis=0, tiled=True)]
    ppermute x16 -> x13, starting transfers between devices: 87.9 us -> 28.8 us  [across(): return lax.ppermute(value, axis, SWAP)]
    ppermute x6 -> x3, waiting for transfers between devices: 22.9 us -> 4.07 us  [quad_swap(): return lax.ppermute(value, ('b', 'l'), [(i, i ^ mask) for i in range(4)])]
    ppermute x16 -> x13, waiting for transfers between devices: 34 us -> 49.5 us  [across(): return lax.ppermute(value, axis, SWAP)]
    ppermute x6 -> x3, starting transfers between devices: 24.1 us -> 9.97 us  [quad_swap(): return lax.ppermute(value, ('b', 'l'), [(i, i ^ mask) for i in range(4)])]
    dot_general x24 -> x18, matrix products: 83.6 us -> 74.4 us  [dot(): return lax.dot_general(left, right, dims, preferred_element_type=f32)]
    ppermute x7 -> x4, starting transfers between devices: 22.5 us -> 14 us  [turn(): return lax.ppermute(value, ('b', 'h'), [(0, 0), (1, 2), (2, 1), (3, 3)])]
  transfers between devices with their start and end apart: 32 -> 20, of which waited for: 11 -> 8; matrix products, arithmetic and copies ran while one was open for 15% -> 11% of each run, Pallas kernels for 7% -> 0%
where the time goes in v3:
time: 560 us; the launch traced here: 549 us
  Pallas kernels  272 us (49%)
  matrix products  74.4 us (13%)
  waiting for transfers between devices  53.6 us (10%)
  starting transfers between devices  52.8 us (9%)
  blocking collectives  37.7 us (7%)
  other arithmetic  35.4 us (6%)
  local copies, waits for them, and re-layouts  21.8 us (4%)
    pallas_call x1, Pallas kernels, front(): pl.pallas_call(functools.partial(front_kernel, groups=groups, chunks=chun...  145 us
    pallas_call x1, Pallas kernels, attend_and_sum(): pl.pallas_call(functools.partial(sums_kernel, groups=groups, rows=rows),...  127 us
    dot_general x18, matrix products, dot(): return lax.dot_general(left, right, dims, preferred_element_type=f32)  74.4 us
    ppermute x13, waiting for transfers between devices, across(): return lax.ppermute(value, axis, SWAP)  49.5 us
    psum x1, blocking collectives, on_device(): norm_grads = lax.psum(norm_grads, groups + ('b',) + stack)  37.7 us
    ppermute x13, starting transfers between devices, across(): return lax.ppermute(value, axis, SWAP)  28.8 us
    ppermute x4, starting transfers between devices, turn(): return lax.ppermute(value, ('b', 'h'), [(0, 0), (1, 2), (2, 1), (3, 3)])  14 us
  transfers between devices with their start and end apart: 20, of which 8 were waited for; matrix products, arithmetic and copies ran while one was open for 11% of the time, Pallas kernels for 0%

profile of v3, /device:TPU:0, one launch (start us, length us, event | category | flops | bytes accessed | tf_op | source)
XLA Modules:
  0.0 549.3 jit_solution(51636097607433560)
XLA Ops:
  3.4 2.9 reshape.185.refs_2_
  6.9 144.8 %shard_map.179 = (bf16[2048,256]{1,0:T(8,128)(2,1)}, bf16[2048,256]{1,0:T(8,128)(2,1)}, bf16[2048,256]{1,0:T(8,128)(2,1)}, bf16[2048,1024]{1,0:T(8,128)(2,1)}, b...) custom-call(bf16[512,1024]{1,0:T(8,128)(2,1)} %bitcast.110, ...), custom_call_target="tpu_custom_call" | custom-call | flops 99999997952 | bytes 33554432 | tf_op jit(solution)/shard_map/pallas_call | solution.py:740
  151.8 3.3 fusion.68
  162.6 9.1 %multiply_convert_fusion.1 = (bf16[1024,2048]{1,0:T(8,128)(2,1)S(1)}, f32[1024,2048]{1,0:T(8,128)}) fusion(bf16[1024,2048]{1,0:T(8,128)(2,1)S(1)} %bitcast.113, bf16[512,1024]{1,0:T(8,128)(2,1)S(1)} %collective-permute-done, bf16[512,1024]{1,0:T(8,128)(2,1)S(1)} %add_convert_fusion.2), kind=kOutput, calls=%fused_computation.9 | convolution fusion | flops 4318035968 | bytes 18874368 | tf_op jit(solution)/shard_map/dot_general | solution.py:806
  188.7 12.1 %multiply_convert_fusion = bf16[1024,2048]{1,0:T(8,128)(2,1)S(1)} fusion(bf16[2048,1024]{1,0:T(8,128)(2,1)S(1)} %bitcast.119, f32[1024,2048]{1,0:T(8,128)} %get-tuple-element.88, bf16[512,1024]{1,0:T(8,128)(2,1)S(1)} %collective-permute-done.4, bf16[512,1024]{1,0:T(8,128)(2,1)S(1)} %get-tuple-element.72), kind=kOutput, calls=%fused_computation.8 | convolution fusion | flops 4343201792 | bytes 18874368 | tf_op jit(solution)/shard_map/dot_general | solution.py:806
  200.9 3.3 fusion.35
  204.6 9.5 %convolution_convert_fusion.1 = bf16[2048,1024]{1,0:T(8,128)(2,1)} fusion(bf16[1024,2048]{1,0:T(8,128)(2,1)} %copy-done.37, bf16[512,1024]{1,0:T(8,128)(2,1)} %copy-done.28, bf16[512,1024]{1,0:T(8,128)(2,1)} %copy-done.9), kind=kOutput, calls=%fused_computation.11 | convolution fusion | flops 4301258752 | bytes 10485760 | tf_op jit(solution)/shard_map/dot_general | solution.py:806
  214.2 5.0 multiply_reduce_fusion.1
  219.2 4.2 multiply_reduce_fusion.2
  227.4 9.4 %collective-permute-start.6 = (bf16[512,256]{1,0:T(8,128)(2,1)S(1)}, bf16[512,256]{1,0:T(8,128)(2,1)S(1)}, u32[]{:S(2)}, u32[]{:S(2)}) collective-permute-start(bf16[512,256]{1,0:T(8,128)(2,1)S(1)} %convolution_convert_fusion.7), channel_id=1, source_target_pairs={{0,5},{1,4},{4,1},{5,0},{2,7},{3,6},{6,3},{7,2},{8,13},{9,12},{12,... | collective-permute-start | bytes 786440 | tf_op jit(solution)/shard_map/ppermute | solution.py:819
  238.9 6.2 %convolution_convert_fusion = bf16[2048,1024]{1,0:T(8,128)(2,1)} fusion(bf16[1024,2048]{1,0:T(8,128)(2,1)S(1)} %copy-done.36, bf16[512,1024]{1,0:T(8,128)(2,1)S(1)} %copy-done.27, bf16[512,1024]{1,0:T(8,128)(2,1)S(1)} %copy-done.14), kind=kOutput, calls=%fused_computation.10 | convolution fusion | flops 4301258752 | bytes 10485760 | tf_op jit(solution)/shard_map/dot_general | solution.py:806
  245.3 4.1 collective-permute-done.7
  251.3 126.7 %shard_map.180 = (bf16[2048,768]{1,0:T(8,128)(2,1)}, bf16[2,2,2,128,1024]{4,3,2,1,0:T(8,128)(2,1)}, bf16[2,2,2,32,1024]{4,3,2,1,0:T(8,128)(2,1)}, bf16[2,2,2,128,1024]{4,3,2,1,0:T(8,128)(2,1)}) custom-call(bf16[2048,256]{1,0:T(8,128)(2,1)} %get-tuple-element.31.refs_0_, bf16[2048,256]{1,0:T(8,128)(2,1)} %get-tuple-element.32.refs_1_, ...), custom_call_target="tpu_custom_call" | custom-call | flops 99999997952 | bytes 33554432 | tf_op jit(solution)/shard_map/pallas_call | solution.py:357
  378.1 6.2 %fusion.69 = f32[1024,768]{1,0:T(8,128)S(1)} fusion(bf16[2048,1024]{1,0:T(8,128)(2,1)} %get-tuple-element.38, bf16[2048,768]{1,0:T(8,128)(2,1)} %get-tuple-element.36), kind=kOutput, calls=%fused_computation.142 | convolution fusion | flops 3221225472 | bytes 10485760 | tf_op jit(solution)/shard_map/dot_general | solution.py:806
  386.1 5.0 convolution_convert_fusion.3
  391.3 14.2 %collective-permute-done.13 = bf16[512,768]{1,0:T(8,128)(2,1)} collective-permute-done((bf16[512,768]{1,0:T(8,128)(2,1)}, bf16[512,768]{1,0:T(8,128)(2,1)}, u32[]{:S(2)}, u32[]{:S(2)}) %collective-permute-start.13) | collective-permute-done | bytes 786464 | tf_op jit(solution)/shard_map/ppermute | solution.py:810
  408.3 9.4 %collective-permute-done.14 = bf16[256,768]{1,0:T(8,128)(2,1)S(1)} collective-permute-done((bf16[256,768]{1,0:T(8,128)(2,1)S(1)}, bf16[256,768]{1,0:T(8,128)(2,1)S(1)}, u32[]{:S(2)}, u32[]{:S(2)}) %collective-permute-start.14) | collective-permute-done | bytes 393248 | tf_op jit(solution)/shard_map/ppermute | solution.py:810
  420.8 21.5 %collective-permute-start.16 = (bf16[128,768]{1,0:T(8,128)(2,1)S(1)}, bf16[128,768]{1,0:T(8,128)(2,1)S(1)}, u32[]{:S(2)}, u32[]{:S(2)}) collective-permute-start(bf16[128,768]{1,0:T(8,128)(2,1)S(1)} %select_convert_fusion.2), channel_id=1, source_target_pairs={{0,4},{4,0},{1,5},{5,1},{2,6},{6,2},{3,7},{7,3},{8,12},{12,8},{9,1... | collective-permute-start | bytes 589832 | tf_op jit(solution)/shard_map/ppermute | solution.py:810
  443.9 3.9 add_convert_fusion
  457.1 18.9 %collective-permute-done.11 = bf16[512,1024]{1,0:T(8,128)(2,1)S(1)} collective-permute-done((bf16[512,1024]{1,0:T(8,128)(2,1)}, bf16[512,1024]{1,0:T(8,128)(2,1)S(1)}, u32[]{:S(2)}, u32[]{:S(2)}) %collective-permute-start.11) | collective-permute-done | bytes 1048608 | tf_op jit(solution)/shard_map/ppermute | solution.py:810
  480.4 9.4 %collective-permute-start.12 = (bf16[512,1024]{1,0:T(8,128)(2,1)}, bf16[512,1024]{1,0:T(8,128)(2,1)}, u32[]{:S(2)}, u32[]{:S(2)}) collective-permute-start(bf16[512,1024]{1,0:T(8,128)(2,1)} %fusion.15), channel_id=1, source_target_pairs={{0,0},{2,4},{4,2},{6,6},{1,1},{3,5},{5,3},{7,7},{8,8},{10,12},{12,... | collective-permute-start | bytes 3145736 | tf_op jit(solution)/shard_map/ppermute | solution.py:814
  492.5 5.4 copy.38
  500.8 37.7 %psum.7 = f32[8,1024]{1,0:T(8,128)S(1)} all-reduce(f32[8,1024]{1,0:T(8,128)S(1)} %stack.35), channel_id=1, replica_groups=mesh['g0'=2,'g1'=2,'b'=2,'h'=2,'l'=2] {'g0','g1','b','h','l'}, use_global_device_ids=true, to_apply=%region_24.25 | all-reduce | flops 8192 | bytes 65536 | tf_op jit(solution)/shard_map/psum | solution.py:992
  545.2 2.9 bitcast_convert_fusion.2
  (178 shorter events, 71.8 us)
Async XLA Ops:
  159.8 2.8 collective-permute-start
  174.1 3.5 collective-permute-start.1
  175.8 4.6 collective-permute-start.3
  186.0 14.9 %copy-start.13 = (bf16[512,1024]{1,0:T(8,128)(2,1)}, bf16[512,1024]{1,0:T(8,128)(2,1)S(1)}, u32[]{:S(2)}) copy-start(bf16[512,1024]{1,0:T(8,128)(2,1)S(1)} %get-tuple-element.72) | copy-start | bytes 3145732
  186.0 2.8 collective-permute-start.4
  204.2 9.9 %collective-permute-start.5 = (bf16[512,1024]{1,0:T(8,128)(2,1)}, bf16[512,1024]{1,0:T(8,128)(2,1)}, u32[]{:S(2)}, u32[]{:S(2)}) collective-permute-start(bf16[512,1024]{1,0:T(8,128)(2,1)} %fusion.35), channel_id=1, source_target_pairs={{0,4},{4,0},{1,5},{5,1},{2,6},{6,2},{3,7},{7,3},{8,12},{12,8},{9,1... | collective-permute-start | bytes 3145736 | tf_op jit(solution)/shard_map/ppermute | solution.py:810
  227.4 17.7 %collective-permute-start.6 = (bf16[512,256]{1,0:T(8,128)(2,1)S(1)}, bf16[512,256]{1,0:T(8,128)(2,1)S(1)}, u32[]{:S(2)}, u32[]{:S(2)}) collective-permute-start(bf16[512,256]{1,0:T(8,128)(2,1)S(1)} %convolution_convert_fusion.7), channel_id=1, source_target_pairs={{0,5},{1,4},{4,1},{5,0},{2,7},{3,6},{6,3},{7,2},{8,13},{9,12},{12,... | collective-permute-start | bytes 786440 | tf_op jit(solution)/shard_map/ppermute | solution.py:819
  237.4 12.0 %collective-permute-start.7 = (bf16[512,256]{1,0:T(8,128)(2,1)S(1)}, bf16[512,256]{1,0:T(8,128)(2,1)S(1)}, u32[]{:S(2)}, u32[]{:S(2)}) collective-permute-start(bf16[512,256]{1,0:T(8,128)(2,1)S(1)} %convolution_convert_fusion.6), channel_id=1, source_target_pairs={{0,1},{1,0},{4,5},{5,4},{2,3},{3,2},{6,7},{7,6},{8,9},{9,8},{12,13... | collective-permute-start | bytes 786440 | tf_op jit(solution)/shard_map/ppermute | solution.py:819
  238.2 11.2 %collective-permute-start.8 = (bf16[512,256]{1,0:T(8,128)(2,1)S(1)}, bf16[512,256]{1,0:T(8,128)(2,1)S(1)}, u32[]{:S(2)}, u32[]{:S(2)}) collective-permute-start(bf16[512,256]{1,0:T(8,128)(2,1)S(1)} %convolution_convert_fusion.5), channel_id=1, source_target_pairs={{0,4},{1,5},{4,0},{5,1},{2,6},{3,7},{6,2},{7,3},{8,12},{9,13},{12,... | collective-permute-start | bytes 786440 | tf_op jit(solution)/shard_map/ppermute | solution.py:819
  238.5 11.5 %collective-permute-start.9 = (bf16[4,128,1024]{2,1,0:T(8,128)(2,1)S(1)}, bf16[4,128,1024]{2,1,0:T(8,128)(2,1)S(1)}, u32[]{:S(2)}, u32[]{:S(2)}) collective-permute-start(bf16[4,128,1024]{2,1,0:T(8,128)(2,1)S(1)} %dynamic-slice_bitcast_fusion), channel_id=1, source_target_pairs={{0,4},{4,0},{1,5},{5,1},{2,6},{6,2},{3,7},{7,3},{8,12},{12,8},{9,1... | collective-permute-start | bytes 3145736 | tf_op jit(solution)/shard_map/ppermute | solution.py:810
  385.3 20.2 %collective-permute-start.13 = (bf16[512,768]{1,0:T(8,128)(2,1)}, bf16[512,768]{1,0:T(8,128)(2,1)}, u32[]{:S(2)}, u32[]{:S(2)}) collective-permute-start(bf16[512,768]{1,0:T(8,128)(2,1)} %select_convert_fusion), channel_id=1, source_target_pairs={{0,16},{16,0},{1,17},{17,1},{2,18},{18,2},{3,19},{19,3},{4,20},{20... | collective-permute-start | bytes 2359304 | tf_op jit(solution)/shard_map/ppermute | solution.py:810
  391.2 52.7 %collective-permute-start.10 = (bf16[1024,1024]{1,0:T(8,128)(2,1)}, bf16[1024,1024]{1,0:T(8,128)(2,1)}, u32[]{:S(2)}, u32[]{:S(2)}) collective-permute-start(bf16[1024,1024]{1,0:T(8,128)(2,1)} %convolution_convert_fusion.3), channel_id=1, source_target_pairs={{0,4},{4,0},{1,5},{5,1},{2,6},{6,2},{3,7},{7,3},{8,12},{12,8},{9,1... | collective-permute-start | bytes 6291464 | tf_op jit(solution)/shard_map/ppermute | solution.py:810
  407.0 10.8 %collective-permute-start.14 = (bf16[256,768]{1,0:T(8,128)(2,1)S(1)}, bf16[256,768]{1,0:T(8,128)(2,1)S(1)}, u32[]{:S(2)}, u32[]{:S(2)}) collective-permute-start(bf16[256,768]{1,0:T(8,128)(2,1)S(1)} %select_convert_fusion.1), channel_id=1, source_target_pairs={{0,8},{8,0},{1,9},{9,1},{2,10},{10,2},{3,11},{11,3},{4,12},{12,4},... | collective-permute-start | bytes 1179656 | tf_op jit(solution)/shard_map/ppermute | solution.py:810
  417.9 2.7 collective-permute-start.15
  418.6 29.2 %collective-permute-start.2 = (bf16[512,1024]{1,0:T(8,128)(2,1)}, bf16[512,1024]{1,0:T(8,128)(2,1)S(1)}, u32[]{:S(2)}, u32[]{:S(2)}) collective-permute-start(bf16[512,1024]{1,0:T(8,128)(2,1)} %get-tuple-element.73), channel_id=1, source_target_pairs={{0,0},{2,4},{4,2},{6,6},{1,1},{3,5},{5,3},{7,7},{8,8},{10,12},{12,... | collective-permute-start | bytes 3145736 | tf_op jit(solution)/shard_map/ppermute | solution.py:814
  420.8 22.6 %collective-permute-start.16 = (bf16[128,768]{1,0:T(8,128)(2,1)S(1)}, bf16[128,768]{1,0:T(8,128)(2,1)S(1)}, u32[]{:S(2)}, u32[]{:S(2)}) collective-permute-start(bf16[128,768]{1,0:T(8,128)(2,1)S(1)} %select_convert_fusion.2), channel_id=1, source_target_pairs={{0,4},{4,0},{1,5},{5,1},{2,6},{6,2},{3,7},{7,3},{8,12},{12,8},{9,1... | collective-permute-start | bytes 589832 | tf_op jit(solution)/shard_map/ppermute | solution.py:810
  443.4 4.4 collective-permute-start.17
  447.8 28.2 %collective-permute-start.11 = (bf16[512,1024]{1,0:T(8,128)(2,1)}, bf16[512,1024]{1,0:T(8,128)(2,1)S(1)}, u32[]{:S(2)}, u32[]{:S(2)}) collective-permute-start(bf16[512,1024]{1,0:T(8,128)(2,1)} %add_convert_fusion), channel_id=1, source_target_pairs={{0,1},{1,0},{2,3},{3,2},{4,5},{5,4},{6,7},{7,6},{8,9},{9,8},{10,11... | collective-permute-start | bytes 3145736 | tf_op jit(solution)/shard_map/ppermute | solution.py:810
  447.9 7.8 %collective-permute-start.18 = (bf16[256,768]{1,0:T(8,128)(2,1)S(1)}, bf16[256,768]{1,0:T(8,128)(2,1)S(1)}, u32[]{:S(2)}, u32[]{:S(2)}) collective-permute-start(bf16[256,768]{1,0:T(8,128)(2,1)S(1)} %maximum_select_fusion.4), channel_id=1, source_target_pairs={{0,8},{8,0},{1,9},{9,1},{2,10},{10,2},{3,11},{11,3},{4,12},{12,4},... | collective-permute-start | bytes 1179656 | tf_op jit(solution)/shard_map/ppermute | solution.py:810
  451.9 24.1 %copy-start.16 = (f32[1,1024]{1,0:T(1,128)S(1)}, f32[1,1024]{1,0:T(1,128)}, u32[]{:S(2)}) copy-start(f32[1,1024]{1,0:T(1,128)} %get-tuple-element.79.refs_6_) | copy-start | bytes 12292
  451.9 24.1 %copy-start.18 = (f32[512]{0:T(512)S(1)}, f32[512]{0:T(512)}, u32[]{:S(2)}) copy-start(f32[512]{0:T(512)} %copy-done.17) | copy-start | bytes 6148
  454.5 21.6 %copy-start.5 = (bf16[512,1024]{1,0:T(8,128)(2,1)S(1)}, bf16[512,1024]{1,0:T(8,128)(2,1)}, u32[]{:S(2)}) copy-start(bf16[512,1024]{1,0:T(8,128)(2,1)} %get-tuple-element.25) | copy-start | bytes 3145732
  456.1 83.0 %collective-permute-start.19 = (bf16[512,768]{1,0:T(8,128)(2,1)S(1)}, bf16[512,768]{1,0:T(8,128)(2,1)S(1)}, u32[]{:S(2)}, u32[]{:S(2)}) collective-permute-start(bf16[512,768]{1,0:T(8,128)(2,1)S(1)} %maximum_select_fusion.2), channel_id=1, source_target_pairs={{0,16},{16,0},{1,17},{17,1},{2,18},{18,2},{3,19},{19,3},{4,20},{20... | collective-permute-start | bytes 2359304 | tf_op jit(solution)/shard_map/ppermute | solution.py:810
  480.4 64.8 %collective-permute-start.12 = (bf16[512,1024]{1,0:T(8,128)(2,1)}, bf16[512,1024]{1,0:T(8,128)(2,1)}, u32[]{:S(2)}, u32[]{:S(2)}) collective-permute-start(bf16[512,1024]{1,0:T(8,128)(2,1)} %fusion.15), channel_id=1, source_target_pairs={{0,0},{2,4},{4,2},{6,6},{1,1},{3,5},{5,3},{7,7},{8,8},{10,12},{12,... | collective-permute-start | bytes 3145736 | tf_op jit(solution)/shard_map/ppermute | solution.py:814
  (35 other events, 160.4 us)

commit v4 on v3

--- a/solution.py
+++ b/solution.py
@@ -80,14 +80,6 @@
     return {"h": at // 2, "l": lax.rem(at, 2)}
 
 
-def greet(groups):
-    barrier = pltpu.get_barrier_semaphore()
-    friends = [flip(axis) for axis in groups + ("b",)] + [next_layer(1), next_layer(3)]
-    for friend in friends:
-        pl.semaphore_signal(barrier, inc=1, device_id=friend, device_id_type=MESH)
-    pl.semaphore_wait(barrier, len(friends))
-
-
 def add_into(total, term, rows=16):
     lead, count = total.shape[:-2], total.shape[-2]
     step = min(rows, count)
@@ -100,274 +92,6 @@
                 total[index + (at,)].astype(f32) + term[index + (at,)].astype(f32)
             ).astype(bf16)
 
-
-def sums_kernel(*refs, groups, rows):
-    (
-        q_ref, k_ref, v_ref, o_ref, do_ref, lse_ref, cos_ref, sin_ref,
-        up_ref, out_ref, down_ref,
-        mixed_ref, up_all, out_all, down_all,
-        dq, dk, dv, delta,
-        *rest,
-    ) = refs
-    bits = len(groups)
-    terms = (up_ref, out_ref, down_ref)
-    results = (up_all, out_all, down_all)
-    partial = [[rest[3 * s + a] for s in range(bits)] for a in range(3)]
-    rest = rest[3 * bits :]
-    passing, (send, recv, local) = rest[:3], rest[3:]
-    copies = Copies(send, recv)
-    place = [lax.axis_index(axis) for axis in groups]
-    layer = 2 * lax.axis_index("h") + lax.axis_index("l")
-    core = lax.axis_index("b")
-    orders = [tuple(range(bits)), tuple(range(bits)), tuple(reversed(range(bits)))]
-
-    def shard(k):
-        return lax.rem(layer + 4 - k, 4)
-
-    def index(order, stage, side):
-        at = []
-        for axis in range(bits):
-            when = order.index(axis)
-            if when < stage:
-                at.append(place[axis])
-            elif when == stage:
-                at.append(place[axis] if side == 0 else 1 - place[axis])
-            else:
-                at.append(slice(None))
-        return tuple(at)
-
-    def inner(order, stage, side):
-        at = []
-        for axis in range(bits):
-            when = order.index(axis)
-            if when == stage:
-                at.append(place[axis] if side == 0 else 1 - place[axis])
-            elif when > stage:
-                at.append(slice(None))
-        return tuple(at)
-
-    def source(a, k, stage, side):
-        order = orders[a]
-        if stage == 0:
-            return terms[a].at[(shard(k),) + index(order, 0, side)]
-        return partial[a][stage - 1].at[(k % 4,) + inner(order, stage, side)]
-
-    def plane_send(k, stage):
-        for a in range(3):
-            copies.start(
-                ("plane", a, k, stage),
-                lambda a=a: (
-                    source(a, k, stage, 1),
-                    partial[a][stage].at[k % 4],
-                    flip(groups[orders[a][stage]]),
-                ),
-            )
-
-    def plane_add(k, stage):
-        for a in range(3):
-            copies.arrived(("plane", a, k, stage))
-            add_into(partial[a][stage].at[k % 4], source(a, k, stage, 0))
-
-    def ring_send(step):
-        for a in range(3):
-            held = partial[a][bits - 1].at[1] if step == 1 else passing[a].at[step - 2]
-            target = passing[a].at[step - 1]
-            copies.start(
-                ("ring", a, step), lambda held=held, target=target: (held, target, next_layer(1))
-            )
-
-    def ring_add(step):
-        for a in range(3):
-            copies.arrived(("ring", a, step))
-            add_into(passing[a].at[step - 1], partial[a][bits - 1].at[(step + 1) % 4])
-
-    def gather_send(stage):
-        for a in range(3):
-            order = orders[a]
-            at = tuple(
-                place[axis] if order.index(axis) >= stage else slice(None) for axis in range(bits)
-            )
-            held = passing[a].at[2] if stage == 0 else results[a].at[(core,) + at]
-            spot = results[a].at[(core,) + at]
-            axis = groups[order[stage]]
-            copies.start(
-                ("gather", a, stage),
-                lambda held=held, spot=spot, axis=axis: (held, spot, flip(axis)),
-            )
-
-    def core_send(stage):
-        for a in range(3):
-            order = orders[a]
-            at = []
-            for axis in range(bits):
-                when = order.index(axis)
-                if stage == 0 or when > stage - 1:
-                    at.append(place[axis])
-                elif when == stage - 1:
-                    at.append(1 - place[axis])
-                else:
-                    at.append(slice(None))
-            spot = results[a].at[(core,) + tuple(at)]
-            held = passing[a].at[2] if stage == 0 else spot
-            copies.start(("core", a, stage), lambda held=held, spot=spot: (held, spot, flip("b")))
-
-    greet(groups)
-    length, width = q_ref.shape
-    heads = width // HEAD_DIM
-    blocks = length // rows
-    lane_head = lax.broadcasted_iota(jnp.int32, (8, width), 1) // HEAD_DIM
-    marks = (lane_head == lax.broadcasted_iota(jnp.int32, (8, width), 0)).astype(f32)
-    for k in (1, 2):
-        plane_send(k, 0)
-
-    def span(i):
-        return pl.ds(pl.multiple_of(i * rows, rows), rows)
-
-    @pl.loop(0, blocks)
-    def _(i):
-        product = do_ref[span(i)].astype(f32) * o_ref[span(i)].astype(f32)
-        delta[:, span(i)] = lax.dot_general(
-            marks, product, NT, precision=lax.Precision.HIGHEST, preferred_element_type=f32
-        )
-
-    for total in (dq, dk, dv):
-        total[...] = jnp.zeros_like(total)
-
-    def tile(i, j):
-        at, to = span(i), span(j)
-        keys, values = k_ref[to], v_ref[to]
-        queries, grads = q_ref[at], do_ref[at]
-        dkj, dvj, dqi = dk[to], dv[to], dq[at]
-        zero = jnp.zeros((), bf16)
-        key = j * rows + lax.broadcasted_iota(jnp.int32, (rows, rows), 0)
-        query = i * rows + lax.broadcasted_iota(jnp.int32, (rows, rows), 1)
-        allowed = key <= query
-        for h in range(heads):
-            mine = head_lanes((rows, width), h)
-            qm = jnp.where(mine, queries, zero)
-            dom = jnp.where(mine, grads, zero)
-            km = jnp.where(mine, keys, zero)
-            st = lax.dot_general(keys, qm, NT, preferred_element_type=f32)
-            pt = jnp.where(allowed, jnp.exp2(st * LOG2E - lse_ref[h : h + 1, at]), 0.0)
-            dpt = lax.dot_general(values, dom, NT, preferred_element_type=f32)
-            dst = (pt * (dpt - delta[h : h + 1, at])).astype(bf16)
-            dvj = dvj + jnp.dot(pt.astype(bf16), dom, preferred_element_type=f32)
-            dkj = dkj + jnp.dot(dst, qm, preferred_element_type=f32)
-            dqi = dqi + lax.dot_general(dst, km, TN, preferred_element_type=f32)
-        dq[at], dk[to], dv[to] = dqi, dkj, dvj
-
-    def tiles(low, high):
-        @pl.loop(low, high)
-        def _(t):
-            i = jnp.int32(0)
-            for n in range(1, blocks):
-                i = i + (t >= n * (n + 1) // 2).astype(jnp.int32)
-            tile(i, t - i * (i + 1) // 2)
-
-    count = blocks * (blocks + 1) // 2
-    tiles(0, 3 * count // 10)
-    plane_add(1, 0)
-    if bits > 1:
-        plane_send(1, 1)
-    plane_send(3, 0)
-    tiles(3 * count // 10, 8 * count // 10)
-    plane_add(2, 0)
-    if bits > 1:
-        plane_send(2, 1)
-    plane_send(4, 0)
-    tiles(8 * count // 10, count)
-
-    def turn_back(grad, at):
-        cosine = jnp.concatenate([cos_ref[at]] * (width // 128), axis=1)
-        sine = jnp.concatenate([sin_ref[at]] * (width // 128), axis=1)
-        return grad * cosine + swap_halves(grad, 1.0) * sine
-
-    @pl.loop(0, blocks)
-    def _(i):
-        at = span(i)
-        mixed_ref[at, :width] = (HEAD_DIM ** (-0.5) * turn_back(dq[at], at)).astype(bf16)
-        mixed_ref[at, width : 2 * width] = turn_back(dk[at], at).astype(bf16)
-        mixed_ref[at, 2 * width :] = dv[at].astype(bf16)
-
-    for stage in range(1, bits):
-        for k in (1, 2):
-            plane_add(k, stage)
-            if stage + 1 < bits:
-                plane_send(k, stage + 1)
-    ring_send(1)
-    plane_add(3, 0)
-    if bits > 1:
-        plane_send(3, 1)
-    ring_add(1)
-    ring_send(2)
-    plane_add(4, 0)
-    if bits > 1:
-        plane_send(4, 1)
-    for stage in range(1, bits):
-        plane_add(3, stage)
-        if stage + 1 < bits:
-            plane_send(3, stage + 1)
-    ring_add(2)
-    ring_send(3)
-    for stage in range(1, bits):
-        plane_add(4, stage)
-        if stage + 1 < bits:
-            plane_send(4, stage + 1)
-    ring_add(3)
-    core_send(0)
-    own = [
-        pltpu.make_async_copy(
-            passing[a].at[2], results[a].at[(core,) + tuple(place)], local.at[a]
-        )
-        for a in range(3)
-    ]
-    gather_send(0)
-    for copy in own:
-        copy.start()
-    for copy in own:
-        copy.wait()
-    for stage in range(bits):
-        for a in range(3):
-            copies.arrived(("gather", a, stage))
-        if stage + 1 < bits:
-            gather_send(stage + 1)
-        core_send(stage + 1)
-    for stage in range(bits + 1):
-        for a in range(3):
-            copies.arrived(("core", a, stage))
-    copies.drain()
-
-
-def attend_and_sum(q, k, v, o, do, lse, cosine, sine, up, out, down, groups, rows=BLOCK):
-    length, width = q.shape
-    bits = len(groups)
-    terms = (up, out, down)
-    vmem = pl.BlockSpec(memory_space=pltpu.VMEM)
-    anywhere = pl.BlockSpec(memory_space=pl.ANY)
-    scratch = [pltpu.VMEM((length, width), f32)] * 3 + [pltpu.VMEM((8, length), f32)]
-    for stage in range(bits):
-        for term in terms:
-            kept = (2,) * (bits - 1 - stage)
-            scratch.append(pltpu.VMEM((4,) + kept + term.shape[-2:], bf16))
-    for term in terms:
-        scratch.append(pltpu.VMEM((3,) + term.shape[-2:], bf16))
-    n = 3 * (4 * bits + 3 + bits + bits + 1)
-    scratch += [pltpu.SemaphoreType.DMA((n,)), pltpu.SemaphoreType.DMA((n,))]
-    scratch += [pltpu.SemaphoreType.DMA((3,))]
-    return pl.pallas_call(
-        functools.partial(sums_kernel, groups=groups, rows=rows),
-        out_shape=(jax.ShapeDtypeStruct((length, 3 * width), bf16),)
-        + tuple(jax.ShapeDtypeStruct((2,) + term.shape[1:], bf16) for term in terms),
-        in_specs=[vmem] * 11,
-        out_specs=(vmem,) + (anywhere,) * 3,
-        scratch_shapes=scratch,
-        compiler_params=pltpu.CompilerParams(
-            vmem_limit_bytes=60 * 2**20, collective_id=1, has_side_effects=True
-        ),
-        cost_estimate=pl.CostEstimate(
-            flops=100_000_000_000, bytes_accessed=32 * 2**20, transcendentals=0
-        ),
-    )(q, k, v, o, do, lse, cosine, sine, up, out, down)
 
 def exclusive(a, b):
     return a + b - 2 * a * b
@@ -773,6 +497,558 @@
         ),
     )(tok, cot, wq, up, out, down, gain, shift, cosine, sine)
 
+def back_kernel(*refs, groups, rows, chunks):
+    (
+        q_ref, k_ref, v_ref, o_ref, lse_ref, cos_ref, sin_ref, gain_ref, norms_ref,
+        da_ref, up_ref, out_ref, down_ref, whole_ref, w_ref, resid_ref, middle_ref,
+        norms_out, grad_home, qkv_all, up_all, out_all, down_all,
+        do, dq, dk, dv, delta, mixed, whole, w, resid, middle,
+        sent, from_core, from_near, grad_x, grad_low, qkv_sum, qkv_core, norm_sum, norm_in,
+        *rest,
+    ) = refs
+    bits = len(groups)
+    terms = (up_ref, out_ref, down_ref)
+    partial = [[rest[3 * s + a] for s in range(bits)] for a in range(3)]
+    rest = rest[3 * bits :]
+    passing, staged, rest = rest[:3], rest[3:6], rest[6:]
+    qkv_in, (send, recv, local) = rest[:bits], rest[bits:]
+    copies = Copies(send, recv)
+    group = [lax.axis_index(axis) for axis in groups]
+    core, half, near = lax.axis_index("b"), lax.axis_index("h"), lax.axis_index("l")
+    layer = 2 * half + near
+    place = 2 * core + near
+    moves, stays = core != half, core == half
+    partner = {"b": half, "h": core}
+    orders = [tuple(range(bits)), tuple(range(bits)), tuple(reversed(range(bits)))]
+    part, depth = da_ref.shape
+    length, width = q_ref.shape
+    heads = width // HEAD_DIM
+    blocks = length // rows
+    slab = up_ref.shape[-1] // 4
+    all_local = [0]
+
+    def local_copy(source, target):
+        n = all_local[0]
+        all_local[0] += 1
+        return pltpu.make_async_copy(source, target, local.at[n])
+
+    def columns(which, size):
+        return pl.ds(pl.multiple_of(which * size, size), size)
+
+    def shard(k):
+        return lax.rem(layer + 4 - k, 4)
+
+    def term(a, k, at):
+        if a == 0:
+            return up_ref.at[at + (slice(None), columns(shard(k), slab))]
+        return terms[a].at[(shard(k),) + at]
+
+    def result(a, at):
+        if a == 0:
+            return up_all.at[at + (slice(None), columns(core, slab))]
+        return (None, out_all, down_all)[a].at[(core,) + at]
+
+    def split(order, stage, side):
+        at = []
+        for axis in range(bits):
+            when = order.index(axis)
+            if when == stage:
+                at.append(group[axis] if side == 0 else 1 - group[axis])
+            elif when > stage:
+                at.append(slice(None))
+        return tuple(at)
+
+    def source(a, k, stage, side):
+        at = split(orders[a], stage, side)
+        if stage == 0:
+            return term(a, k, at) if side else staged[a].at[k % 2]
+        return partial[a][stage - 1].at[(k % 4,) + at]
+
+    loads = {}
+
+    def plane_send(k, stage):
+        for a in range(3):
+            copies.start(
+                ("plane", a, k, stage),
+                lambda a=a: (
+                    source(a, k, stage, 1),
+                    partial[a][stage].at[k % 4],
+                    flip(groups[orders[a][stage]]),
+                ),
+            )
+            if stage == 0:
+                loads[a, k] = local_copy(term(a, k, split(orders[a], 0, 0)), staged[a].at[k % 2])
+                loads[a, k].start()
+
+    def plane_add(k, stage):
+        for a in range(3):
+            copies.arrived(("plane", a, k, stage))
+            if stage == 0:
+                loads[a, k].wait()
+            add_into(partial[a][stage].at[k % 4], source(a, k, stage, 0))
+
+    def plane_step(k, stage):
+        plane_add(k, stage)
+        if stage + 1 < bits:
+            plane_send(k, stage + 1)
+
+    def ring_send(step):
+        for a in range(3):
+            held = partial[a][bits - 1].at[1] if step == 1 else passing[a].at[step - 2]
+            target = passing[a].at[step - 1]
+            copies.start(
+                ("ring", a, step), lambda held=held, target=target: (held, target, next_layer(1))
+            )
+
+    def ring_add(step):
+        for a in range(3):
+            copies.arrived(("ring", a, step))
+            add_into(passing[a].at[step - 1], partial[a][bits - 1].at[(step + 1) % 4])
+
+    def gather_send(stage):
+        for a in range(3):
+            order = orders[a]
+            at = tuple(
+                group[axis] if order.index(axis) >= stage else slice(None) for axis in range(bits)
+            )
+            held = passing[a].at[2] if stage == 0 else result(a, at)
+            spot, axis = result(a, at), groups[order[stage]]
+            copies.start(
+                ("gather", a, stage),
+                lambda held=held, spot=spot, axis=axis: (held, spot, flip(axis)),
+            )
+
+    def brought(order, stage):
+        at = []
+        for axis in range(bits):
+            when = order.index(axis)
+            if stage == 0 or when > stage - 1:
+                at.append(group[axis])
+            elif when == stage - 1:
+                at.append(1 - group[axis])
+            else:
+                at.append(slice(None))
+        return tuple(at)
+
+    def core_send(stage):
+        for a in range(3):
+            spot = result(a, brought(orders[a], stage))
+            held = passing[a].at[2] if stage == 0 else spot
+            copies.start(("core", a, stage), lambda held=held, spot=spot: (held, spot, flip("b")))
+
+    barrier = pltpu.get_barrier_semaphore()
+    friends = [flip(axis) for axis in groups + ("b", "h", "l")] + [next_layer(1), next_layer(3)]
+    friends += [{"b": 1 - core, "l": 1 - near}]
+    for friend in friends:
+        pl.semaphore_signal(barrier, inc=1, device_id=friend, device_id_type=MESH)
+
+    @pl.when(moves)
+    def _():
+        pl.semaphore_signal(barrier, inc=1, device_id=partner, device_id_type=MESH)
+        pl.semaphore_wait(barrier, len(friends) + 1)
+
+    @pl.when(stays)
+    def _():
+        pl.semaphore_wait(barrier, len(friends))
+
+    for mask in (3, 1, 2):
+        to_core, to_near = exclusive(core, mask // 2), exclusive(near, mask % 2)
+
+        def build(to_core=to_core, to_near=to_near):
+            return (
+                da_ref.at[:, columns(2 * to_core + to_near, width)],
+                do.at[columns(place, part)],
+                {"b": to_core, "l": to_near},
+            )
+
+        copies.start(("heads", mask), build)
+    own_heads = local_copy(da_ref.at[:, columns(place, width)], do.at[columns(place, part)])
+    own_heads.start()
+    for k in (1, 2):
+        plane_send(k, 0)
+    early = [
+        local_copy(whole_ref, whole),
+        local_copy(w_ref, w),
+        local_copy(resid_ref, resid),
+        local_copy(middle_ref, middle),
+    ]
+    for copy in early:
+        copy.start()
+    for total in (dq, dk, dv):
+        total[...] = jnp.zeros_like(total)
+    own_heads.wait()
+    for mask in (2, 1, 3):
+        copies.arrived(("heads", mask))
+
+    lane_head = lax.broadcasted_iota(jnp.int32, (8, width), 1) // HEAD_DIM
+    marks = (lane_head == lax.broadcasted_iota(jnp.int32, (8, width), 0)).astype(f32)
+
+    def span(i):
+        return pl.ds(pl.multiple_of(i * rows, rows), rows)
+
+    @pl.loop(0, blocks)
+    def _(i):
+        product = do[span(i)].astype(f32) * o_ref[span(i)].astype(f32)
+        delta[:, span(i)] = lax.dot_general(
+            marks, product, NT, precision=lax.Precision.HIGHEST, preferred_element_type=f32
+        )
+
+    def tile(i, j):
+        at, to = span(i), span(j)
+        keys, values = k_ref[to], v_ref[to]
+        queries, grads = q_ref[at], do[at]
+        dkj, dvj, dqi = dk[to], dv[to], dq[at]
+        zero = jnp.zeros((), bf16)
+        key = j * rows + lax.broadcasted_iota(jnp.int32, (rows, rows), 0)
+        query = i * rows + lax.broadcasted_iota(jnp.int32, (rows, rows), 1)
+        allowed = key <= query
+        for h in range(heads):
+            mine = head_lanes((rows, width), h)
+            qm = jnp.where(mine, queries, zero)
+            dom = jnp.where(mine, grads, zero)
+            km = jnp.where(mine, keys, zero)
+            st = lax.dot_general(keys, qm, NT, preferred_element_type=f32)
+            pt = jnp.where(allowed, jnp.exp2(st * LOG2E - lse_ref[h : h + 1, at]), 0.0)
+            dpt = lax.dot_general(values, dom, NT, preferred_element_type=f32)
+            dst = (pt * (dpt - delta[h : h + 1, at])).astype(bf16)
+            dvj = dvj + jnp.dot(pt.astype(bf16), dom, preferred_element_type=f32)
+            dkj = dkj + jnp.dot(dst, qm, preferred_element_type=f32)
+            dqi = dqi + lax.dot_general(dst, km, TN, preferred_element_type=f32)
+        dq[at], dk[to], dv[to] = dqi, dkj, dvj
+
+    count = blocks * (blocks + 1) // 2
+
+    def first_sums():
+        plane_step(1, 0)
+        plane_send(3, 0)
+
+    def second_sums():
+        plane_step(2, 0)
+        plane_send(4, 0)
+
+    plans = {3 * count // 10: first_sums, 7 * count // 10: second_sums}
+
+    def tiles(low, high):
+        @pl.loop(low, high)
+        def _(t):
+            i = jnp.int32(0)
+            for n in range(1, blocks):
+                i = i + (t >= n * (n + 1) // 2).astype(jnp.int32)
+            tile(i, t - i * (i + 1) // 2)
+
+    low = 0
+    for when, step in plans.items():
+        tiles(low, when)
+        step()
+        low = when
+    tiles(low, count)
+
+    def turn_back(grad, at):
+        cosine = jnp.concatenate([cos_ref[at]] * (width // 128), axis=1)
+        sine = jnp.concatenate([sin_ref[at]] * (width // 128), axis=1)
+        return grad * cosine + swap_halves(grad, 1.0) * sine
+
+    @pl.loop(0, blocks)
+    def _(i):
+        at = span(i)
+        mixed[at, :width] = (HEAD_DIM ** (-0.5) * turn_back(dq[at], at)).astype(bf16)
+        mixed[at, width : 2 * width] = turn_back(dk[at], at).astype(bf16)
+        mixed[at, 2 * width :] = dv[at].astype(bf16)
+
+    for copy in early:
+        copy.wait()
+    size = part // chunks
+
+    def input_part(block, c):
+        at = pl.ds(pl.multiple_of(block * part + c * size, size), size)
+        return lax.dot_general(
+            mixed[at], w[...].reshape(depth, 3 * width), NT, preferred_element_type=f32
+        )
+
+    def inside(c):
+        return pl.ds(pl.multiple_of(c * size, size), size)
+
+    for slot in range(2):
+        block = 2 * (1 - core) + (1 - near if slot == 0 else near)
+
+        @pl.loop(0, chunks)
+        def _(c):
+            sent[slot, inside(c)] = input_part(block, c).astype(bf16)
+
+        copies.start(
+            ("x core", slot),
+            lambda slot=slot: (sent.at[slot], from_core.at[slot], flip("b")),
+        )
+    for stage in range(1, bits):
+        plane_step(1, stage)
+    ring_send(1)
+    copies.arrived(("x core", 0))
+    for c in range(chunks):
+        total = input_part(2 * core + 1 - near, c) + from_core[0, inside(c)].astype(f32)
+        sent[2, inside(c)] = total.astype(bf16)
+        copies.start(
+            ("x near", c),
+            lambda c=c: (sent.at[2, inside(c)], from_near.at[inside(c)], flip("l")),
+        )
+    plane_step(3, 0)
+    copies.arrived(("x core", 1))
+
+    @pl.loop(0, chunks)
+    def _(c):
+        grad_x[inside(c)] = input_part(place, c) + from_core[1, inside(c)].astype(f32)
+
+    quarter = depth // 2**bits
+    side = quarter // 2
+    for index in np.ndindex(*(2,) * bits):
+        first = sum(bit << (bits - 1 - axis) for axis, bit in enumerate(index)) * quarter
+        block = lax.dot_general(
+            whole[:, first : first + quarter], mixed[...], TN, preferred_element_type=f32
+        ).astype(bf16)
+        for i in range(2):
+            qkv_sum[index + (i,)] = block[i * side : (i + 1) * side]
+    q_orders = [orders[0], orders[2]]
+
+    def q_slot(i, stage, side):
+        order = q_orders[i]
+        at = []
+        for axis in range(bits):
+            when = order.index(axis)
+            if when < stage:
+                at.append(group[axis])
+            elif when == stage:
+                at.append(group[axis] if side == 0 else 1 - group[axis])
+            else:
+                at.append(slice(None))
+        return qkv_sum.at[tuple(at) + (i,)]
+
+    def q_send(stage):
+        for i in range(2):
+            copies.start(
+                ("q", i, stage),
+                lambda i=i: (
+                    q_slot(i, stage, 1),
+                    qkv_in[stage].at[i],
+                    flip(groups[q_orders[i][stage]]),
+                ),
+            )
+
+    def q_add(stage):
+        for i in range(2):
+            copies.arrived(("q", i, stage))
+            add_into(q_slot(i, stage, 0), qkv_in[stage].at[i])
+
+    q_send(0)
+    for stage in range(1, bits):
+        plane_step(2, stage)
+    ring_add(1)
+    ring_send(2)
+    plane_step(4, 0)
+
+    norm_sum[...] = norms_ref[...]
+    fine = min(128, size)
+    for c in range(chunks):
+        copies.arrived(("x near", c))
+
+        @pl.loop(0, size // fine)
+        def _(s):
+            at = pl.ds(pl.multiple_of(c * size + s * fine, fine), fine)
+            grad = grad_x[at] + from_near[at].astype(f32)
+            value = resid[at].astype(f32)
+            center = value - jnp.mean(value, axis=1, keepdims=True)
+            inverse = lax.rsqrt(jnp.mean(center * center, axis=1, keepdims=True) + EPS)
+            unit = center * inverse
+            scaled = grad * gain_ref[...]
+            back = inverse * (
+                scaled
+                - jnp.mean(scaled, axis=1, keepdims=True)
+                - unit * jnp.mean(scaled * unit, axis=1, keepdims=True)
+            )
+            grad_low[at] = (middle[at] + back).astype(bf16)
+            norm_sum[0:1] += jnp.sum(grad * unit, axis=0, keepdims=True)
+            norm_sum[4:5] += jnp.sum(grad, axis=0, keepdims=True)
+
+        copies.plan(
+            ("home", c), lambda c=c: (grad_low.at[inside(c)], grad_home.at[inside(c)], partner)
+        )
+        pl.when(moves)(functools.partial(copies.start, ("home", c)))
+    stay = [local_copy(grad_low, grad_home)]
+    pl.when(stays)(stay[0].start)
+
+    axes = groups + ("b", "h", "l")
+
+    def norms_send(step):
+        copies.start(("norms", step), lambda: (norm_sum, norm_in.at[step], flip(axes[step])))
+
+    def norms_add(step):
+        copies.arrived(("norms", step))
+        copies.sent(("norms", step))
+        norm_sum[...] += norm_in[step]
+
+    norms_send(0)
+    q_add(0)
+    if bits > 1:
+        q_send(1)
+    for stage in range(1, bits):
+        plane_step(3, stage)
+    ring_add(2)
+    ring_send(3)
+    norms_add(0)
+    norms_send(1)
+    for stage in range(1, bits):
+        q_add(stage)
+        if stage + 1 < bits:
+            q_send(stage + 1)
+    own_q = tuple(group)
+
+    copies.plan("q turn", lambda: (qkv_sum.at[own_q], qkv_core.at[0], partner))
+    pl.when(moves)(functools.partial(copies.start, "q turn"))
+    norms_add(1)
+    norms_send(2)
+    for stage in range(1, bits):
+        plane_step(4, stage)
+    ring_add(3)
+    core_send(0)
+    own = [local_copy(passing[a].at[2], result(a, tuple(group))) for a in range(3)]
+    gather_send(0)
+    for copy in own:
+        copy.start()
+    norms_add(2)
+    norms_send(3)
+
+    @pl.when(moves)
+    def _():
+        copies.arrived("q turn")
+
+    @pl.when(stays)
+    def _():
+        qkv_core[0] = qkv_sum[own_q]
+
+    copies.start("q core", lambda: (qkv_core.at[0, 1 - core], qkv_core.at[1, 1 - core], flip("b")))
+    norms_add(3)
+    norms_send(4)
+    for copy in own:
+        copy.wait()
+    copies.arrived("q core")
+    add_into(qkv_core.at[1, core], qkv_core.at[0, core])
+
+    def q_spot(at):
+        return qkv_all.at[at + (core,)]
+
+    keep_q = local_copy(qkv_core.at[1, core], q_spot(own_q))
+    keep_q.start()
+
+    def q_gather(stage):
+        at = tuple(group[axis] if axis >= stage else slice(None) for axis in range(bits))
+        held = qkv_core.at[1, core] if stage == 0 else q_spot(at)
+        copies.start(
+            ("q gather", stage), lambda: (held, q_spot(at), flip(groups[stage]))
+        )
+
+    def q_core_send(stage):
+        spot = q_spot(brought(orders[0], stage))
+        held = qkv_core.at[1, core] if stage == 0 else spot
+        copies.start(("q both", stage), lambda: (held, spot, flip("b")))
+
+    q_gather(0)
+    q_core_send(0)
+    keep_q.wait()
+    for step in range(4, len(axes)):
+        norms_add(step)
+        if step + 1 < len(axes):
+            norms_send(step + 1)
+    for stage in range(bits):
+        for a in range(3):
+            copies.arrived(("gather", a, stage))
+        if stage + 1 < bits:
+            gather_send(stage + 1)
+        core_send(stage + 1)
+        copies.arrived(("q gather", stage))
+        if stage + 1 < bits:
+            q_gather(stage + 1)
+        q_core_send(stage + 1)
+    norms_out[...] = norm_sum[...]
+    for stage in range(bits + 1):
+        for a in range(3):
+            copies.arrived(("core", a, stage))
+        copies.arrived(("q both", stage))
+    sometimes = ["q turn"] + [("home", c) for c in range(chunks)]
+
+    @pl.when(moves)
+    def _():
+        for c in range(chunks):
+            copies.arrived(("home", c))
+        for name in sometimes:
+            copies.sent(name)
+
+    pl.when(stays)(stay[0].wait)
+    copies.drain(sometimes + [("norms", step) for step in range(len(axes))])
+
+
+def back(
+    q, k, v, o, lse, cosine, sine, gain, norms, da, up, out, down, whole, w, resid, middle,
+    groups, rows=BLOCK, chunks=2,
+):
+    length, width = q.shape
+    part, depth = da.shape
+    bits = len(groups)
+    slab = up.shape[-1] // 4
+    tails = (up.shape[-2:-1] + (slab,), out.shape[-2:], down.shape[-2:])
+    vmem = pl.BlockSpec(memory_space=pltpu.VMEM)
+    anywhere = pl.BlockSpec(memory_space=pl.ANY)
+    slots = (2,) * bits
+    quarter = depth // 2**bits
+    q_tail = (quarter // 2, 3 * width)
+    scratch = [pltpu.VMEM((length, width), bf16)]
+    scratch += [pltpu.VMEM((length, width), f32)] * 3 + [pltpu.VMEM((8, length), f32)]
+    scratch += [
+        pltpu.VMEM((length, 3 * width), bf16),
+        pltpu.VMEM(whole.shape, bf16),
+        pltpu.VMEM(w.shape, bf16),
+        pltpu.VMEM((part, depth), bf16),
+        pltpu.VMEM((part, depth), f32),
+        pltpu.VMEM((3, part, depth), bf16),
+        pltpu.VMEM((2, part, depth), bf16),
+        pltpu.VMEM((part, depth), bf16),
+        pltpu.VMEM((part, depth), f32),
+        pltpu.VMEM((part, depth), bf16),
+        pltpu.VMEM(slots + (2,) + q_tail, bf16),
+        pltpu.VMEM((2, 2) + q_tail, bf16),
+        pltpu.VMEM((8, depth), f32),
+        pltpu.VMEM((bits + 3, 8, depth), f32),
+    ]
+    for stage in range(bits):
+        for tail in tails:
+            scratch.append(pltpu.VMEM((4,) + (2,) * (bits - 1 - stage) + tail, bf16))
+    scratch += [pltpu.VMEM((3,) + tail, bf16) for tail in tails]
+    scratch += [pltpu.VMEM((2,) + (2,) * (bits - 1) + tail, bf16) for tail in tails]
+    scratch += [
+        pltpu.VMEM((2,) + (2,) * (bits - 1 - stage) + q_tail, bf16) for stage in range(bits)
+    ]
+    n = 3 + 3 * (4 * bits + 3 + bits + bits + 1)
+    n += 2 + chunks + 2 * bits + chunks + (bits + 3) + 2 + bits + bits + 1
+    scratch += [pltpu.SemaphoreType.DMA((n,)), pltpu.SemaphoreType.DMA((n,))]
+    scratch += [pltpu.SemaphoreType.DMA((1 + 12 + 4 + 1 + 3 + 1,))]
+    return pl.pallas_call(
+        functools.partial(back_kernel, groups=groups, rows=rows, chunks=chunks),
+        out_shape=(
+            jax.ShapeDtypeStruct((8, depth), f32),
+            jax.ShapeDtypeStruct((part, depth), bf16),
+            jax.ShapeDtypeStruct(slots + (2,) + q_tail, bf16),
+            jax.ShapeDtypeStruct(slots + (up.shape[-2], 2 * slab), bf16),
+            jax.ShapeDtypeStruct((2,) + out.shape[1:], bf16),
+            jax.ShapeDtypeStruct((2,) + down.shape[1:], bf16),
+        ),
+        in_specs=[vmem] * 9 + [anywhere] * 8,
+        out_specs=(vmem,) + (anywhere,) * 5,
+        scratch_shapes=scratch,
+        compiler_params=pltpu.CompilerParams(
+            vmem_limit_bytes=63 * 2**20, collective_id=1, has_side_effects=True
+        ),
+        cost_estimate=pl.CostEstimate(
+            flops=100_000_000_000, bytes_accessed=32 * 2**20, transcendentals=0
+        ),
+    )(q, k, v, o, lse, cosine, sine, gain, norms, da, up, out, down, whole, w, resid, middle)
+
 
 def norm_forward(value, gain, shift):
     center = value - jnp.mean(value, axis=-1, keepdims=True)
@@ -812,27 +1088,6 @@
 
 def turn(value):
     return lax.ppermute(value, ("b", "h"), [(0, 0), (1, 2), (2, 1), (3, 3)])
-
-
-def quad_swap(value, far_b, far_l):
-    mask = 2 * far_b + far_l
-    return lax.ppermute(value, ("b", "l"), [(i, i ^ mask) for i in range(4)])
-
-
-def gather_axis(value, axis, dim=0):
-    other = across(value, axis)
-    first = lax.axis_index(axis) == 0
-    return jnp.where(
-        first, jnp.concatenate([value, other], dim), jnp.concatenate([other, value], dim)
-    )
-
-
-def scatter_axis(value, axis):
-    low, high = jnp.split(value.astype(f32), 2, axis=0)
-    first = lax.axis_index(axis) == 0
-    kept = jnp.where(first, low, high)
-    sent = jnp.where(first, high, low).astype(bf16)
-    return kept + across(sent, axis).astype(f32)
 
 
 def on_device(
@@ -881,18 +1136,10 @@
     up_half = up_half.reshape(depth, 2 * units)
     out_whole = out_whole.reshape(4 * cols, depth)
     down_half = down_half.reshape(2 * units, depth)
-    w_attn = w_attn.reshape(depth, 3 * cols)
-
-    def block_of(value, mask):
-        return lax.dynamic_slice_in_dim(value, (place ^ mask) * part, part, 0)
-
-    def out_rows(mask):
-        return lax.dynamic_slice_in_dim(out_whole, (place ^ mask) * cols, cols, 0)
 
     branch_a = dot(heads, out_whole)
 
     resid = resid_low.astype(f32)
-    normed_a, unit_0, inverse_0 = norm_forward(resid, gains[0], shifts[0])
     out_a, unit_1, inverse_1 = norm_forward(branch_a, gains[1], shifts[1])
     middle = resid + out_a
     normed_f, unit_2, inverse_2 = norm_forward(middle, gains[2], shifts[2])
@@ -922,7 +1169,7 @@
     grad_active = dot(pair_g, down_half, NT)
     grad_hidden = (slope.astype(f32) * grad_active).astype(bf16)
     down_grad = dot(active, pair_g, TN).astype(bf16)
-    up_grad = dot(grad_hidden, pair_f, TN).astype(bf16)
+    up_grad = dot(pair_f, grad_hidden, TN).astype(bf16)
 
     grad_f = dot(grad_hidden[part:], up_half, NT).astype(bf16)
     grad_f = dot(grad_hidden[:part], up_half, NT) + across(grad_f, "b").astype(f32)
@@ -930,14 +1177,7 @@
     grad_middle = grad_final + back_2
     back_1, gain_1, shift_1 = norm_backward(grad_middle, unit_1, inverse_1, gains[1])
     grad_a = back_1.astype(bf16)
-    grad_attended = jnp.zeros((length, cols), bf16)
-    for mask in (3, 1, 2, 0):
-        sent = dot(grad_a, out_rows(mask), NT).astype(bf16)
-        if mask:
-            sent = quad_swap(sent, mask // 2, mask % 2)
-        grad_attended = lax.dynamic_update_slice_in_dim(
-            grad_attended, sent, (place ^ mask) * part, 0
-        )
+    grad_attended = dot(grad_a, out_whole, NT).astype(bf16)
     out_grad = dot(heads, grad_a, TN).astype(bf16)
     out_grad = out_grad.reshape(4, 2, cols // 2, depth)
     sent = lax.dynamic_index_in_dim(out_grad, 1 - core, 1, False)
@@ -946,50 +1186,33 @@
     def pieces(value):
         return value.reshape((4,) + slots + (value.size // (4 * n_groups * depth), depth))
 
-    grad_mixed, up_grad, out_grad, down_grad = attend_and_sum(
+    none = jnp.zeros_like(gain_1)
+    norms = jnp.stack([none, gain_1, gain_2, gain_3, none, shift_1, shift_2, shift_3])
+    norm_grads, input_grad, qkv_grad, up_grad, out_grad, down_grad = back(
         q,
         k,
         v,
         attended,
-        grad_attended,
         lse,
         cosine,
         sine,
-        pieces(up_grad),
+        gains[0],
+        norms,
+        grad_attended,
+        up_grad.reshape(slots + (depth // n_groups, 2 * units)),
         pieces(out_grad),
         pieces(down_grad),
+        whole_a,
+        w_attn,
+        resid_low,
+        grad_middle,
         groups,
     )
-    up_grad = up_grad.reshape(units, depth).T.astype(f32)
+    input_grad = input_grad.astype(f32)
+    qkv_grad = qkv_grad.reshape(depth, 3, cols).astype(f32)
+    up_grad = up_grad.reshape(depth, units).astype(f32)
     out_grad = out_grad.reshape(cols, depth).astype(f32)
     down_grad = down_grad.reshape(units, depth).astype(f32)
-
-    pair = 2 * part
-    sent = lax.dynamic_slice_in_dim(grad_mixed, (1 - core) * pair, pair, 0)
-    from_core = across(dot(sent, w_attn, NT).astype(bf16), "b")
-    sent = dot(block_of(grad_mixed, 1), w_attn, NT)
-    sent = sent + lax.dynamic_slice_in_dim(from_core, (1 - near) * part, part, 0).astype(f32)
-    from_near = across(sent.astype(bf16), "l")
-    grad_normed_a = dot(block_of(grad_mixed, 0), w_attn, NT)
-    grad_normed_a = grad_normed_a + lax.dynamic_slice_in_dim(
-        from_core, near * part, part, 0
-    ).astype(f32)
-    grad_normed_a = grad_normed_a + from_near.astype(f32)
-
-    qkv_grad = dot(whole_a, grad_mixed, TN)
-    for axis in groups:
-        qkv_grad = scatter_axis(qkv_grad, axis)
-    qkv_grad = turn(qkv_grad.astype(bf16))
-    qkv_grad = scatter_axis(qkv_grad, "b").astype(bf16)
-    qkv_grad = gather_axis(qkv_grad, "b")
-    for axis in reversed(groups):
-        qkv_grad = gather_axis(qkv_grad, axis)
-    qkv_grad = qkv_grad.astype(f32).reshape(depth, 3, cols)
-
-    back_0, gain_0, shift_0 = norm_backward(grad_normed_a, unit_0, inverse_0, gains[0])
-    input_grad = turn((grad_middle + back_0).astype(bf16)).astype(f32)
-    norm_grads = jnp.stack([gain_0, gain_1, gain_2, gain_3, shift_0, shift_1, shift_2, shift_3])
-    norm_grads = lax.psum(norm_grads, groups + ("b",) + stack)
     return (
         output[None],
         input_grad[None],

time: 560 us -> 464 us (0.83)
  Pallas kernels: 272 us -> 327 us
  waiting for transfers between devices: 53.6 us -> 2.3 us
  blocking collectives: 37.7 us -> 0 us
  starting transfers between devices: 52.8 us -> 16.4 us
  matrix products: 74.4 us -> 58.2 us
  other arithmetic: 35.4 us -> 22.5 us
    pallas_call x1, Pallas kernels: 127 us -> 182 us  [back(): pl.pallas_call(functools.partial(back_kernel, groups=groups, rows=rows, c...]
    ppermute x13 -> x5, waiting for transfers between devices: 49.5 us -> 2.3 us  [across(): return lax.ppermute(value, axis, SWAP)]
    psum x1 -> x0, blocking collectives: 37.7 us -> none  [on_device(): norm_grads = lax.psum(norm_grads, groups + ('b',) + stack)]
    ppermute x13 -> x5, starting transfers between devices: 28.8 us -> 4.97 us  [across(): return lax.ppermute(value, axis, SWAP)]
    dot_general x18 -> x11, matrix products: 74.4 us -> 58.2 us  [dot(): return lax.dot_general(left, right, dims, preferred_element_type=f32)]
    ppermute x3 -> x0, starting transfers between devices: 9.97 us -> none  [quad_swap(): return lax.ppermute(value, ('b', 'l'), [(i, i ^ mask) for i in range(4)])]
    reduce_sum x3 -> x1, other arithmetic: 8.97 us -> 1.68 us  [norm_backward(): return (back, jnp.sum(grad * unit, axis=0), jnp.sum(grad, axis=0))]
    ppermute x4 -> x2, starting transfers between devices: 14 us -> 11.5 us  [turn(): return lax.ppermute(value, ('b', 'h'), [(0, 0), (1, 2), (2, 1), (3, 3)])]
  transfers between devices with their start and end apart: 20 -> 7, of which waited for: 8 -> 1; matrix products, arithmetic and copies ran while one was open for 11% -> 9% of each run, Pallas kernels for 0% -> 0%
where the time goes in v4:
time: 464 us; the launch traced here: 455 us
  Pallas kernels  327 us (70%)
  matrix products  58.2 us (13%)
  local copies, waits for them, and re-layouts  26.3 us (6%)
  other arithmetic  22.5 us (5%)
  starting transfers between devices  16.4 us (4%)
    pallas_call x1, Pallas kernels, back(): pl.pallas_call(functools.partial(back_kernel, groups=groups, rows=rows, c...  182 us
    pallas_call x1, Pallas kernels, front(): pl.pallas_call(functools.partial(front_kernel, groups=groups, chunks=chun...  145 us
    dot_general x11, matrix products, dot(): return lax.dot_general(left, right, dims, preferred_element_type=f32)  58.2 us
    ppermute x2, starting transfers between devices, turn(): return lax.ppermute(value, ('b', 'h'), [(0, 0), (1, 2), (2, 1), (3, 3)])  11.5 us
    unnamed x52, local copies, waits for them, and re-layouts  10.8 us
  transfers between devices with their start and end apart: 7, of which 1 were waited for; matrix products, arithmetic and copies ran while one was open for 9% of the time, Pallas kernels for 0%

profile of v4, /device:TPU:0, one launch (start us, length us, event | category | flops | bytes accessed | tf_op | source)
XLA Modules:
  0.0 454.6 jit_solution(18431922300572203468)
XLA Ops:
  3.6 2.8 copy.30
  6.3 2.9 reshape.152.refs_2_
  9.2 145.0 %shard_map.179 = (bf16[2048,256]{1,0:T(8,128)(2,1)}, bf16[2048,256]{1,0:T(8,128)(2,1)}, bf16[2048,256]{1,0:T(8,128)(2,1)}, bf16[2048,1024]{1,0:T(8,128)(2,1)}, b...) custom-call(bf16[512,1024]{1,0:T(8,128)(2,1)} %bitcast.86, ...), custom_call_target="tpu_custom_call" | custom-call | flops 99999997952 | bytes 33554432 | tf_op jit(solution)/shard_map/pallas_call | solution.py:464
  154.2 3.3 fusion.36
  161.5 2.3 collective-permute-done
  163.8 9.1 %multiply_convert_fusion.1 = (bf16[1024,2048]{1,0:T(8,128)(2,1)S(1)}, f32[1024,2048]{1,0:T(8,128)}) fusion(bf16[1024,2048]{1,0:T(8,128)(2,1)S(1)} %bitcast.89, bf16[512,1024]{1,0:T(8,128)(2,1)S(1)} %collective-permute-done, bf16[512,1024]{1,0:T(8,128)(2,1)S(1)} %add_convert_fusion.1), kind=kOutput, calls=%fused_computation.9 | convolution fusion | flops 4318035968 | bytes 18874368 | tf_op jit(solution)/shard_map/dot_general | solution.py:1082
  173.0 2.3 fusion.18
  178.9 2.4 fusion.31
  184.3 2.6 multiply_convert_fusion.3
  187.4 9.6 %collective-permute-start.2 = (bf16[512,1024]{1,0:T(8,128)(2,1)}, bf16[512,1024]{1,0:T(8,128)(2,1)}, u32[]{:S(2)}, u32[]{:S(2)}) collective-permute-start(bf16[512,1024]{1,0:T(8,128)(2,1)} %get-tuple-element.80), channel_id=1, source_target_pairs={{0,0},{2,4},{4,2},{6,6},{1,1},{3,5},{5,3},{7,7},{8,8},{10,12},{12,... | collective-permute-start | bytes 3145736 | tf_op jit(solution)/shard_map/ppermute | solution.py:1090
  197.1 12.2 %multiply_convert_fusion = bf16[1024,2048]{1,0:T(8,128)(2,1)S(1)} fusion(bf16[2048,1024]{1,0:T(8,128)(2,1)S(1)} %bitcast.94, f32[1024,2048]{1,0:T(8,128)} %get-tuple-element.94, bf16[512,1024]{1,0:T(8,128)(2,1)S(1)} %collective-permute-done.4, bf16[512,1024]{1,0:T(8,128)(2,1)S(1)} %get-tuple-element.79), kind=kOutput, calls=%fused_computation.8 | convolution fusion | flops 4343201792 | bytes 18874368 | tf_op jit(solution)/shard_map/dot_general | solution.py:1082
  209.3 3.3 fusion.21
  212.6 9.4 %convolution_convert_fusion = bf16[2048,1024]{1,0:T(8,128)(2,1)} fusion(bf16[1024,2048]{1,0:T(8,128)(2,1)} %copy-done.22, bf16[512,1024]{1,0:T(8,128)(2,1)} %copy-done.16, bf16[512,1024]{1,0:T(8,128)(2,1)} %copy-done.11), kind=kOutput, calls=%fused_computation.10 | convolution fusion | flops 4301258752 | bytes 10485760 | tf_op jit(solution)/shard_map/dot_general | solution.py:1082
  222.1 4.4 multiply_reduce_fusion.2
  226.5 4.2 multiply_reduce_fusion
  234.2 3.4 collective-permute-start.6
  237.6 6.2 %convolution_convert_fusion.1 = bf16[1024,2048]{1,0:T(8,128)(2,1)} fusion(bf16[1024,2048]{1,0:T(8,128)(2,1)S(1)} %copy-done.24, bf16[512,1024]{1,0:T(8,128)(2,1)S(1)} %copy-done.15, bf16[512,1024]{1,0:T(8,128)(2,1)S(1)} %copy-done.8), kind=kOutput, calls=%fused_computation.11 | convolution fusion | flops 4301258752 | bytes 10485760 | tf_op jit(solution)/shard_map/dot_general | solution.py:1082
  244.6 4.2 convolution_convert_fusion.3.refs_9_
  248.7 2.6 fusion.14
  251.3 182.0 %shard_map.180 = (f32[8,1024]{1,0:T(8,128)}, bf16[512,1024]{1,0:T(8,128)(2,1)}, bf16[2,2,2,128,768]{4,3,2,1,0:T(8,128)(2,1)}, bf16[2,2,256,1024]{3,2,1,0:T(8,128...) custom-call(bf16[2048,256]{1,0:T(8,128)(2,1)} %get-tuple-element.32.refs_0_, ...), custom_call_target="tpu_custom_call" | custom-call | flops 99999997952 | bytes 33554432 | tf_op jit(solution)/shard_map/pallas_call | solution.py:1031
  433.4 5.6 %reshape.153 = f32[1024,3,256]{2,1,0:T(4,128)} reshape(bf16[2,2,2,128,768]{4,3,2,1,0:T(8,128)(2,1)} %get-tuple-element.41) | data formatting | bytes 4718592 | tf_op jit(solution)/shard_map/convert_element_type | solution.py:1212
  439.0 4.6 %copy.27 = f32[1024,3,256]{2,0,1:T(8,128)} copy(f32[1024,3,256]{2,1,0:T(4,128)} %reshape.153) | data formatting | bytes 6291456
  443.6 2.6 bitcast_convert_fusion
  446.2 2.6 bitcast_convert_fusion.1
  (90 shorter events, 23.0 us)
Async XLA Ops:
  157.5 2.7 copy-start
  160.2 3.6 copy-start.18
  161.0 11.9 %copy-start.7 = (bf16[512,1024]{1,0:T(8,128)(2,1)}, bf16[512,1024]{1,0:T(8,128)(2,1)S(1)}, u32[]{:S(2)}) copy-start(bf16[512,1024]{1,0:T(8,128)(2,1)S(1)} %add_convert_fusion.1) | copy-start | bytes 3145732
  161.0 2.8 collective-permute-start
  163.8 9.1 %copy-start.14 = (bf16[512,1024]{1,0:T(8,128)(2,1)}, bf16[512,1024]{1,0:T(8,128)(2,1)S(1)}, u32[]{:S(2)}) copy-start(bf16[512,1024]{1,0:T(8,128)(2,1)S(1)} %collective-permute-done) | copy-start | bytes 3145732
  163.8 9.1 %copy-start.20 = (bf16[4,2,2,128,1024]{4,3,2,1,0:T(8,128)(2,1)S(1)}, bf16[4,2,2,128,1024]{4,3,2,1,0:T(8,128)(2,1)}, u32[]{:S(2)}) copy-start(bf16[4,2,2,128,1024]{4,3,2,1,0:T(8,128)(2,1)} %get-tuple-element.31) | copy-start | bytes 12582916
  172.9 6.0 %copy-start.22 = (bf16[1024,2048]{1,0:T(8,128)(2,1)}, bf16[1024,2048]{1,0:T(8,128)(2,1)S(1)}, u32[]{:S(2)}) copy-start(bf16[1024,2048]{1,0:T(8,128)(2,1)S(1)} %get-tuple-element.93) | copy-start | bytes 12582916
  172.9 3.5 copy-start.17
  175.3 3.6 collective-permute-start.1
  177.0 4.7 %collective-permute-start.3 = (f32[1]{0:T(128)}, f32[1]{0:T(128)}, u32[]{:S(2)}, u32[]{:S(2)}) collective-permute-start(f32[1]{0:T(128)} %bitcast.16), channel_id=1, source_target_pairs={{0,0},{2,4},{4,2},{6,6},{1,1},{3,5},{5,3},{7,7},{8,8},{10,12},{12,... | collective-permute-start | bytes 20 | tf_op jit(solution)/shard_map/ppermute | solution.py:1090
  186.9 22.3 %copy-start.11 = (bf16[512,1024]{1,0:T(8,128)(2,1)}, bf16[512,1024]{1,0:T(8,128)(2,1)S(1)}, u32[]{:S(2)}) copy-start(bf16[512,1024]{1,0:T(8,128)(2,1)S(1)} %get-tuple-element.79) | copy-start | bytes 3145732
  186.9 10.1 %collective-permute-start.4 = (bf16[512,1024]{1,0:T(8,128)(2,1)S(1)}, bf16[512,1024]{1,0:T(8,128)(2,1)S(1)}, u32[]{:S(2)}, u32[]{:S(2)}) collective-permute-start(bf16[512,1024]{1,0:T(8,128)(2,1)S(1)} %get-tuple-element.79), channel_id=1, source_target_pairs={{0,4},{4,0},{1,5},{5,1},{2,6},{6,2},{3,7},{7,3},{8,12},{12,8},{9,1... | collective-permute-start | bytes 3145736 | tf_op jit(solution)/shard_map/ppermute | solution.py:1086
  187.4 25.2 %collective-permute-start.2 = (bf16[512,1024]{1,0:T(8,128)(2,1)}, bf16[512,1024]{1,0:T(8,128)(2,1)}, u32[]{:S(2)}, u32[]{:S(2)}) collective-permute-start(bf16[512,1024]{1,0:T(8,128)(2,1)} %get-tuple-element.80), channel_id=1, source_target_pairs={{0,0},{2,4},{4,2},{6,6},{1,1},{3,5},{5,3},{7,7},{8,8},{10,12},{12,... | collective-permute-start | bytes 3145736 | tf_op jit(solution)/shard_map/ppermute | solution.py:1090
  197.1 12.2 %copy-start.16 = (bf16[512,1024]{1,0:T(8,128)(2,1)}, bf16[512,1024]{1,0:T(8,128)(2,1)S(1)}, u32[]{:S(2)}) copy-start(bf16[512,1024]{1,0:T(8,128)(2,1)S(1)} %collective-permute-done.4) | copy-start | bytes 3145732
  209.3 3.4 copy-start.23
  212.6 9.5 %collective-permute-start.5 = (bf16[512,1024]{1,0:T(8,128)(2,1)}, bf16[512,1024]{1,0:T(8,128)(2,1)}, u32[]{:S(2)}, u32[]{:S(2)}) collective-permute-start(bf16[512,1024]{1,0:T(8,128)(2,1)} %fusion.21), channel_id=1, source_target_pairs={{0,4},{4,0},{1,5},{5,1},{2,6},{6,2},{3,7},{7,3},{8,12},{12,8},{9,1... | collective-permute-start | bytes 3145736 | tf_op jit(solution)/shard_map/ppermute | solution.py:1086
  212.6 9.5 %copy-start.19 = (bf16[2,2,256,2048]{3,2,1,0:T(8,128)(2,1)S(1)}, bf16[2,2,256,2048]{3,2,1,0:T(8,128)(2,1)}, u32[]{:S(2)}) copy-start(bf16[2,2,256,2048]{3,2,1,0:T(8,128)(2,1)} %get-tuple-element.30) | copy-start | bytes 12582916
  212.6 9.5 %copy-start.24 = (bf16[1024,2048]{1,0:T(8,128)(2,1)S(1)}, bf16[1024,2048]{1,0:T(8,128)(2,1)}, u32[]{:S(2)}) copy-start(bf16[1024,2048]{1,0:T(8,128)(2,1)} %copy-done.23) | copy-start | bytes 12582916
  222.1 4.4 copy-start.1
  234.1 3.5 copy-start.8
  234.1 3.5 copy-start.15
  234.2 14.5 %collective-permute-start.6 = (bf16[4,128,1024]{2,1,0:T(8,128)(2,1)S(1)}, bf16[4,128,1024]{2,1,0:T(8,128)(2,1)}, u32[]{:S(2)}, u32[]{:S(2)}) collective-permute-start(bf16[4,128,1024]{2,1,0:T(8,128)(2,1)S(1)} %dynamic-slice_bitcast_fusion), channel_id=1, source_target_pairs={{0,4},{4,0},{1,5},{5,1},{2,6},{6,2},{3,7},{7,3},{8,12},{12,8},{9,1... | collective-permute-start | bytes 3145736 | tf_op jit(solution)/shard_map/ppermute | solution.py:1086
  439.0 4.6 %copy-start.5 = (bf16[2,2,2,128,1024]{4,3,2,1,0:T(8,128)(2,1)S(1)}, bf16[2,2,2,128,1024]{4,3,2,1,0:T(8,128)(2,1)}, u32[]{:S(2)}) copy-start(bf16[2,2,2,128,1024]{4,3,2,1,0:T(8,128)(2,1)} %get-tuple-element.44) | copy-start | bytes 6291460
  448.8 2.7 copy-start.13
  (8 other events, 14.6 us)

commit v5 on v4

--- a/solution.py
+++ b/solution.py
@@ -33,6 +33,15 @@
 
 
 MESH = pl.DeviceIdType.MESH
+FRONT_PLAN = {
+    "own": "ring",
+    "near": "one",
+    0: "1a",
+    1: "two 1b",
+    2: "2a three",
+    3: "2b 3a",
+    "rest": "3b",
+}
 
 
 class Copies:
@@ -80,9 +89,9 @@
     return {"h": at // 2, "l": lax.rem(at, 2)}
 
 
-def add_into(total, term, rows=16):
+def add_into(total, term, rows=64):
     lead, count = total.shape[:-2], total.shape[-2]
-    step = min(rows, count)
+    step = next(n for n in (rows, 32, 16, 8) if count % n == 0)
 
     @pl.loop(0, count // step)
     def _(i):
@@ -136,7 +145,8 @@
         tok_ref, cot_ref, wq_ref, up_ref, out_ref, down_ref, gain_ref, shift_ref, cos_ref, sin_ref,
         q_ref, k_ref, v_ref, whole_ref, o_ref, lse_ref,
         heads_ref, tok_home, cot_home, w_home, up_all, out_all, down_all,
-        row, w_att, send, recv, local, head_send, head_recv,
+        row, w_att, bounce_up, bounce_out, bounce_down, bounce_cot,
+        send, recv, local, head_send, head_recv,
     ) = refs
     bits = len(groups)
     part = tok_ref.shape[0]
@@ -179,8 +189,116 @@
     def piece(c):
         return pl.ds(c * size, size)
 
+    weights = (up_ref, out_ref, down_ref)
+    orders = [tuple(range(bits)), tuple(range(bits)), tuple(reversed(range(bits)))]
+    slab = up_ref.shape[-1] // 2
+
+    def slot(a, shard, at):
+        if a == 0:
+            return up_all.at[at + (slice(None), pl.ds(pl.multiple_of(shard * slab, slab), slab))]
+        if a == 1:
+            return out_all.at[(shard, core) + at]
+        return down_all.at[(shard,) + at]
+
+    def held(a, at):
+        if a == 0:
+            return up_ref.at[at + (slice(None), pl.ds(pl.multiple_of(core * slab, slab), slab))]
+        return weights[a].at[(core,) + at]
+
+    def shard(k):
+        return lax.rem(layer + 4 - k, 4)
+
+    def ring_send(step):
+        for a in range(3):
+
+            def build(a=a):
+                at = tuple(group)
+                spot = slot(a, shard(step - 1), at)
+                return (held(a, at) if step == 1 else spot, spot, next_layer(1))
+
+            copies.start(("ring", a, step), build)
+
+    def ring_wait(step):
+        for a in range(3):
+            copies.arrived(("ring", a, step))
+
+    def plane_send(k, stage):
+        for a in range(3):
+
+            def build(a=a):
+                order = orders[a]
+                at = tuple(
+                    group[axis] if order.index(axis) >= stage else slice(None)
+                    for axis in range(bits)
+                )
+                spot = slot(a, shard(k), at)
+                return (spot, spot, flip(groups[order[stage]]))
+
+            copies.start(("plane", a, k, stage), build)
+
+    def plane_wait(k, stage):
+        for a in range(3):
+            copies.arrived(("plane", a, k, stage))
+
+    def core_send(k):
+        def build():
+            spot = slot(1, shard(k), (slice(None),) * bits)
+            return (spot, spot, flip("b"))
+
+        copies.start(("core", k), build)
+
+    def plane_next(k, stage):
+        plane_wait(k, stage)
+        if stage + 1 < bits:
+            plane_send(k, stage + 1)
+        else:
+            core_send(k)
+
+    def inner_stages(k):
+        for stage in range(1, bits):
+            plane_next(k, stage)
+
+    def arrive(k):
+        ring_wait(k)
+        if k < 3:
+            ring_send(k + 1)
+        plane_send(k, 0)
+
+    steps = {
+        "ring": lambda: ring_send(1),
+        "one": lambda: arrive(1),
+        "two": lambda: arrive(2),
+        "three": lambda: arrive(3),
+        "1a": lambda: plane_next(1, 0),
+        "1b": lambda: inner_stages(1),
+        "2a": lambda: plane_next(2, 0),
+        "2b": lambda: inner_stages(2),
+        "3a": lambda: plane_next(3, 0),
+        "3b": lambda: inner_stages(3),
+    }
+
+    def weights_at(point):
+        for name in FRONT_PLAN.get(point, "").split():
+            steps[name]()
+
+    everything = (slice(None),) * bits
+    bounces = [
+        (held(0, everything), bounce_up, slot(0, layer, everything)),
+        (out_ref, bounce_out, out_all.at[layer]),
+        (held(2, everything), bounce_down, slot(2, layer, everything)),
+    ]
+    inward = []
+    for source, buffer, _ in bounces:
+        copy = pltpu.make_async_copy(source, buffer, local.at[len(locals_made)])
+        locals_made.append(copy)
+        inward.append(copy)
+        copy.start()
+
+    weights_at("start")
     own = [
-        pltpu.make_async_copy(tok_ref.at[piece(c)], row.at[place, piece(c)], local.at[c])
+        pltpu.make_async_copy(
+            tok_ref.at[piece(c)], row.at[place, piece(c)], local.at[len(locals_made) + c]
+        )
         for c in range(chunks)
     ]
     locals_made.extend(own)
@@ -193,7 +311,9 @@
     w_here = pltpu.make_async_copy(wq_ref, w_att, local.at[len(locals_made)])
     locals_made.append(w_here)
     copies.plan("wturn", lambda: (wq_ref.at[tuple(group)], w_att.at[tuple(group)], partner))
-    cot_here = pltpu.make_async_copy(cot_ref, cot_home, local.at[len(locals_made)])
+    cot_in = pltpu.make_async_copy(cot_ref, bounce_cot, local.at[len(locals_made)])
+    locals_made.append(cot_in)
+    cot_here = pltpu.make_async_copy(bounce_cot, cot_home, local.at[len(locals_made)])
     locals_made.append(cot_here)
     copies.plan("cot", lambda: (cot_ref, cot_home, partner))
 
@@ -208,71 +328,7 @@
         for c in range(chunks):
             own[c].start()
         w_here.start()
-
-    weights = (up_ref, out_ref, down_ref)
-    orders = [tuple(range(bits)), tuple(range(bits)), tuple(reversed(range(bits)))]
-    slab = up_ref.shape[-1] // 2
-
-    def slot(a, shard, at):
-        if a == 0:
-            return up_all.at[at + (slice(None), pl.ds(pl.multiple_of(shard * slab, slab), slab))]
-        if a == 1:
-            return out_all.at[(shard, core) + at]
-        return down_all.at[(shard,) + at]
-
-    def held(a, at):
-        if a == 0:
-            return up_ref.at[at + (slice(None), pl.ds(pl.multiple_of(core * slab, slab), slab))]
-        return weights[a].at[(core,) + at]
-
-    def shard(k):
-        return lax.rem(layer + 4 - k, 4)
-
-    def ring_send(step):
-        for a in range(3):
-
-            def build(a=a):
-                at = tuple(group)
-                spot = slot(a, shard(step - 1), at)
-                return (held(a, at) if step == 1 else spot, spot, next_layer(1))
-
-            copies.start(("ring", a, step), build)
-
-    def ring_wait(step):
-        for a in range(3):
-            copies.arrived(("ring", a, step))
-
-    def plane_send(k, stage):
-        for a in range(3):
-
-            def build(a=a):
-                order = orders[a]
-                at = tuple(
-                    group[axis] if order.index(axis) >= stage else slice(None)
-                    for axis in range(bits)
-                )
-                spot = slot(a, shard(k), at)
-                return (spot, spot, flip(groups[order[stage]]))
-
-            copies.start(("plane", a, k, stage), build)
-
-    def plane_wait(k, stage):
-        for a in range(3):
-            copies.arrived(("plane", a, k, stage))
-
-    def core_send(k):
-        def build():
-            spot = slot(1, shard(k), (slice(None),) * bits)
-            return (spot, spot, flip("b"))
-
-        copies.start(("core", k), build)
-
-    for a in range(3):
-        everything = (slice(None),) * bits
-        if a == 1:
-            copy_here(out_ref, out_all.at[layer])
-        else:
-            copy_here(held(a, everything), slot(a, layer, everything))
+        cot_in.start()
 
     for c in range(chunks):
         pl.when(moves)(functools.partial(copies.arrived, turned[c]))
@@ -287,6 +343,11 @@
                 ),
             )
     copy_here(row.at[place], tok_home)
+    for copy in inward:
+        copy.wait()
+    for _, buffer, target in bounces:
+        copy_here(buffer, target)
+    weights_at("own")
 
     @pl.when(stays)
     def _():
@@ -327,7 +388,7 @@
                 ("core near", c),
                 lambda c=c: (row.at[near_block, piece(c)], row.at[near_block, piece(c)], flip("b")),
             )
-        ring_send(1)
+        weights_at("near")
 
     def wait_all(name):
         def run():
@@ -379,17 +440,13 @@
             device_id_type=MESH,
         )
 
-    def forward_weights():
-        ring_wait(1)
-        ring_send(2)
-        plane_send(1, 0)
-
     @pl.loop(0, 4)
     def _(r):
         far_core, far_near = 1 - lax.rem(r, 2), 1 - r // 2
         mask = 2 * far_core + far_near
         block = 2 * exclusive(core, far_core) + exclusive(near, far_near)
-        pl.when(r == 2)(forward_weights)
+        for n in range(4):
+            pl.when(r == n)(functools.partial(weights_at, n))
         for i in range(4):
             pl.when(block == i)(
                 functools.partial(
@@ -412,20 +469,10 @@
 
     @pl.when(stays)
     def _():
+        cot_in.wait()
         cot_here.start()
 
-    for k in (1, 2, 3):
-        if k > 1:
-            plane_send(k, 0)
-        for stage in range(bits):
-            plane_wait(k, stage)
-            if stage + 1 < bits:
-                plane_send(k, stage + 1)
-            if stage == 0 and k < 3:
-                ring_wait(k + 1)
-                if k < 2:
-                    ring_send(k + 2)
-        core_send(k)
+    weights_at("rest")
     for mask in (1, 2, 3):
         copy = head_copy(jnp.int32(mask))
         copy.wait_send()
@@ -483,9 +530,13 @@
         scratch_shapes=[
             pltpu.VMEM((4, part, depth), bf16),
             pltpu.VMEM(wq.shape, bf16),
+            pltpu.VMEM(up.shape[:-1] + (up.shape[-1] // 2,), bf16),
+            pltpu.VMEM(out.shape, bf16),
+            pltpu.VMEM(down.shape[1:], bf16),
+            pltpu.VMEM((part, depth), bf16),
             pltpu.SemaphoreType.DMA((n,)),
             pltpu.SemaphoreType.DMA((n,)),
-            pltpu.SemaphoreType.DMA((16,)),
+            pltpu.SemaphoreType.DMA((32,)),
             pltpu.SemaphoreType.DMA((4,)),
             pltpu.SemaphoreType.DMA((4,)),
         ],
@@ -500,8 +551,11 @@
 def back_kernel(*refs, groups, rows, chunks):
     (
         q_ref, k_ref, v_ref, o_ref, lse_ref, cos_ref, sin_ref, gain_ref, norms_ref,
-        da_ref, up_ref, out_ref, down_ref, whole_ref, w_ref, resid_ref, middle_ref,
-        norms_out, grad_home, qkv_all, up_all, out_all, down_all,
+        da_ref, low_ref, inputs_ref, branches_ref, hidden_ref, active_ref, heads_ref, branch_ref,
+        whole_ref, w_ref, resid_ref, middle_ref,
+        norms_out, grad_home, low_home, qkv_all, up_all, out_all, down_all,
+        up_ref, out_ref, down_ref,
+        out_part, out_in, up_tile, down_tile, turned,
         do, dq, dk, dv, delta, mixed, whole, w, resid, middle,
         sent, from_core, from_near, grad_x, grad_low, qkv_sum, qkv_core, norm_sum, norm_in,
         *rest,
@@ -525,6 +579,7 @@
     heads = width // HEAD_DIM
     blocks = length // rows
     slab = up_ref.shape[-1] // 4
+    quarter = depth // 2**bits
     all_local = [0]
 
     def local_copy(source, target):
@@ -664,8 +719,104 @@
         copies.start(("heads", mask), build)
     own_heads = local_copy(da_ref.at[:, columns(place, width)], do.at[columns(place, part)])
     own_heads.start()
-    for k in (1, 2):
-        plane_send(k, 0)
+    low_in = local_copy(low_ref, grad_low)
+    low_here = local_copy(grad_low, low_home)
+    copies.plan("low", lambda: (low_ref, low_home, partner))
+    pl.when(moves)(functools.partial(copies.start, "low"))
+    pl.when(stays)(low_in.start)
+
+    pieces = 2
+    thin = slab // pieces
+    pair = whole.shape[0] // 2
+    units = [local_copy(inputs_ref, whole.at[:pair]), local_copy(branches_ref, whole.at[pair:])]
+    units += [local_copy(heads_ref, sent.at[0]), local_copy(branch_ref, sent.at[1])]
+    for copy in units:
+        copy.start()
+
+    def hidden_load(u):
+        spot = columns(pieces * shard(1 + u // pieces) + lax.rem(u, pieces), thin)
+        at = columns(lax.rem(u, 3), thin)
+        semaphore = hidden_local + 2 * lax.rem(u, 3)
+        return (
+            pltpu.make_async_copy(
+                hidden_ref.at[:, spot], mixed.at[:pair, at], local.at[semaphore]
+            ),
+            pltpu.make_async_copy(
+                active_ref.at[:, spot], mixed.at[pair:, at], local.at[semaphore + 1]
+            ),
+        )
+
+    hidden_local = all_local[0]
+    all_local[0] += 6
+    for u in range(2):
+        for copy in hidden_load(jnp.int32(u)):
+            copy.start()
+    for copy in units:
+        copy.wait()
+    @pl.loop(0, 4)
+    def _(s):
+        block = lax.dot_general(
+            sent[0, :, columns(s, width)], sent[1], TN, preferred_element_type=f32
+        ).astype(bf16)
+        out_part[s] = block.reshape(out_part.shape[1:])
+
+    @pl.loop(0, 4)
+    def _(c):
+        turned[columns(c, depth // 4)] = whole[:pair, columns(c, depth // 4)].T
+
+    copies.start("out core", lambda: (out_part.at[:, 1 - core], out_in, flip("b")))
+    def shard_gradients(k):
+        @pl.loop(0, pieces)
+        def _(n):
+            u = pieces * (k - 1) + n
+            for copy in hidden_load(u):
+                copy.wait()
+
+            @pl.when(u + 2 < 4 * pieces)
+            def _():
+                for copy in hidden_load(u + 2):
+                    copy.start()
+
+            buffer = columns(lax.rem(u, 3), thin)
+
+            @pl.loop(0, 2**bits)
+            def _(c):
+                slot = tuple(lax.rem(c // 2 ** (bits - 1 - i), 2) for i in range(bits))
+                up_tile[(n,) + slot] = jnp.dot(
+                    turned[columns(c, quarter)],
+                    mixed[:pair, buffer],
+                    preferred_element_type=f32,
+                ).astype(bf16)
+
+            block = lax.dot_general(
+                mixed[pair:, buffer], whole[pair:], TN, preferred_element_type=f32
+            )
+            down_tile[n] = block.astype(bf16).reshape(down_tile.shape[1:])
+
+        if k == 1:
+            copies.arrived("out core")
+
+            @pl.loop(0, 4)
+            def _(s):
+                out_in[s] = (out_in[s].astype(f32) + out_part[s, core].astype(f32)).astype(bf16)
+
+            put = local_copy(out_in, out_ref)
+            put.start()
+            put.wait()
+        made = []
+        for u in range(pieces):
+            spot = (slice(None),) * (bits + 1) + (columns(pieces * shard(k) + u, thin),)
+            made.append(local_copy(up_tile.at[u], up_ref.at[spot]))
+            made.append(local_copy(down_tile.at[u], down_ref.at[shard(k), u]))
+        for copy in made:
+            copy.start()
+        for copy in made:
+            copy.wait()
+
+    for k in (1, 2, 3, 4):
+        shard_gradients(k)
+        if k < 3:
+            plane_send(k, 0)
     early = [
         local_copy(whole_ref, whole),
         local_copy(w_ref, w),
@@ -674,6 +825,12 @@
     ]
     for copy in early:
         copy.start()
+
+    @pl.when(stays)
+    def _():
+        low_in.wait()
+        low_here.start()
+
     for total in (dq, dk, dv):
         total[...] = jnp.zeros_like(total)
     own_heads.wait()
@@ -718,15 +875,31 @@
 
     count = blocks * (blocks + 1) // 2
 
-    def first_sums():
+    def last_stages(k):
+        for stage in range(1, bits):
+            plane_step(k, stage)
+
+    def sums_a():
         plane_step(1, 0)
         plane_send(3, 0)
 
-    def second_sums():
+    def sums_b():
         plane_step(2, 0)
         plane_send(4, 0)
 
-    plans = {3 * count // 10: first_sums, 7 * count // 10: second_sums}
+    def sums_c():
+        last_stages(1)
+        ring_send(1)
+
+    def sums_d():
+        plane_step(3, 0)
+
+    def sums_e():
+        last_stages(2)
+        ring_add(1)
+        ring_send(2)
+
+    plans = ((0, sums_a), (2, sums_b), (4, sums_c), (6, sums_d), (8, sums_e))
 
     def tiles(low, high):
         @pl.loop(low, high)
@@ -737,8 +910,10 @@
             tile(i, t - i * (i + 1) // 2)
 
     low = 0
-    for when, step in plans.items():
-        tiles(low, when)
+    for when, step in plans:
+        when = when * count // 10
+        if when > low:
+            tiles(low, when)
         step()
         low = when
     tiles(low, count)
@@ -779,9 +954,6 @@
             ("x core", slot),
             lambda slot=slot: (sent.at[slot], from_core.at[slot], flip("b")),
         )
-    for stage in range(1, bits):
-        plane_step(1, stage)
-    ring_send(1)
     copies.arrived(("x core", 0))
     for c in range(chunks):
         total = input_part(2 * core + 1 - near, c) + from_core[0, inside(c)].astype(f32)
@@ -790,14 +962,7 @@
             ("x near", c),
             lambda c=c: (sent.at[2, inside(c)], from_near.at[inside(c)], flip("l")),
         )
-    plane_step(3, 0)
-    copies.arrived(("x core", 1))
-
-    @pl.loop(0, chunks)
-    def _(c):
-        grad_x[inside(c)] = input_part(place, c) + from_core[1, inside(c)].astype(f32)
-
-    quarter = depth // 2**bits
+    plane_step(4, 0)
     side = quarter // 2
     for index in np.ndindex(*(2,) * bits):
         first = sum(bit << (bits - 1 - axis) for axis, bit in enumerate(index)) * quarter
@@ -838,15 +1003,31 @@
             add_into(q_slot(i, stage, 0), qkv_in[stage].at[i])
 
     q_send(0)
-    for stage in range(1, bits):
-        plane_step(2, stage)
-    ring_add(1)
-    ring_send(2)
-    plane_step(4, 0)
-
+    last_stages(3)
+    ring_add(2)
+    ring_send(3)
+    copies.arrived(("x core", 1))
+
+    @pl.loop(0, chunks)
+    def _(c):
+        grad_x[inside(c)] = input_part(place, c) + from_core[1, inside(c)].astype(f32)
+
+    own_q = tuple(group)
+    axes = groups + ("b", "h", "l")
+
+    def norms_send(step):
+        copies.start(("norms", step), lambda: (norm_sum, norm_in.at[step], flip(axes[step])))
+
+    def norms_add(step):
+        copies.arrived(("norms", step))
+        copies.sent(("norms", step))
+        norm_sum[...] += norm_in[step]
+
+    pl.when(stays)(low_here.wait)
     norm_sum[...] = norms_ref[...]
     fine = min(128, size)
-    for c in range(chunks):
+
+    def home(c):
         copies.arrived(("x near", c))
 
         @pl.loop(0, size // fine)
@@ -871,110 +1052,96 @@
             ("home", c), lambda c=c: (grad_low.at[inside(c)], grad_home.at[inside(c)], partner)
         )
         pl.when(moves)(functools.partial(copies.start, ("home", c)))
-    stay = [local_copy(grad_low, grad_home)]
-    pl.when(stays)(stay[0].start)
-
-    axes = groups + ("b", "h", "l")
-
-    def norms_send(step):
-        copies.start(("norms", step), lambda: (norm_sum, norm_in.at[step], flip(axes[step])))
-
-    def norms_add(step):
-        copies.arrived(("norms", step))
-        copies.sent(("norms", step))
-        norm_sum[...] += norm_in[step]
-
-    norms_send(0)
-    q_add(0)
-    if bits > 1:
-        q_send(1)
-    for stage in range(1, bits):
-        plane_step(3, stage)
-    ring_add(2)
-    ring_send(3)
-    norms_add(0)
-    norms_send(1)
-    for stage in range(1, bits):
-        q_add(stage)
-        if stage + 1 < bits:
-            q_send(stage + 1)
-    own_q = tuple(group)
-
-    copies.plan("q turn", lambda: (qkv_sum.at[own_q], qkv_core.at[0], partner))
-    pl.when(moves)(functools.partial(copies.start, "q turn"))
-    norms_add(1)
-    norms_send(2)
-    for stage in range(1, bits):
-        plane_step(4, stage)
-    ring_add(3)
-    core_send(0)
-    own = [local_copy(passing[a].at[2], result(a, tuple(group))) for a in range(3)]
-    gather_send(0)
-    for copy in own:
-        copy.start()
-    norms_add(2)
-    norms_send(3)
-
-    @pl.when(moves)
-    def _():
-        copies.arrived("q turn")
-
-    @pl.when(stays)
-    def _():
-        qkv_core[0] = qkv_sum[own_q]
-
-    copies.start("q core", lambda: (qkv_core.at[0, 1 - core], qkv_core.at[1, 1 - core], flip("b")))
-    norms_add(3)
-    norms_send(4)
-    for copy in own:
-        copy.wait()
-    copies.arrived("q core")
-    add_into(qkv_core.at[1, core], qkv_core.at[0, core])
-
-    def q_spot(at):
-        return qkv_all.at[at + (core,)]
-
-    keep_q = local_copy(qkv_core.at[1, core], q_spot(own_q))
-    keep_q.start()
-
-    def q_gather(stage):
-        at = tuple(group[axis] if axis >= stage else slice(None) for axis in range(bits))
-        held = qkv_core.at[1, core] if stage == 0 else q_spot(at)
-        copies.start(
-            ("q gather", stage), lambda: (held, q_spot(at), flip(groups[stage]))
-        )
-
-    def q_core_send(stage):
-        spot = q_spot(brought(orders[0], stage))
-        held = qkv_core.at[1, core] if stage == 0 else spot
-        copies.start(("q both", stage), lambda: (held, spot, flip("b")))
-
-    q_gather(0)
-    q_core_send(0)
-    keep_q.wait()
-    for step in range(4, len(axes)):
-        norms_add(step)
-        if step + 1 < len(axes):
-            norms_send(step + 1)
-    for stage in range(bits):
+
+    def gather_next(stage):
         for a in range(3):
             copies.arrived(("gather", a, stage))
         if stage + 1 < bits:
             gather_send(stage + 1)
         core_send(stage + 1)
+
+    def q_spot(at):
+        return qkv_all.at[at + (core,)]
+
+    keep_q = local_copy(qkv_core.at[1, core], q_spot(own_q))
+    own = [local_copy(passing[a].at[2], result(a, tuple(group))) for a in range(3)]
+
+    def q_gather(stage):
+        at = tuple(group[axis] if axis >= stage else slice(None) for axis in range(bits))
+        held = qkv_core.at[1, core] if stage == 0 else q_spot(at)
+        copies.start(("q gather", stage), lambda: (held, q_spot(at), flip(groups[stage])))
+
+    def q_core_send(stage):
+        spot = q_spot(brought(orders[0], stage))
+        held = qkv_core.at[1, core] if stage == 0 else spot
+        copies.start(("q both", stage), lambda: (held, spot, flip("b")))
+
+    half_way = chunks // 2
+    for c in range(half_way):
+        home(c)
+    for stage in range(bits):
+        q_add(stage)
+        if stage + 1 < bits:
+            q_send(stage + 1)
+
+    copies.plan("q turn", lambda: (qkv_sum.at[own_q], qkv_core.at[0], partner))
+    pl.when(moves)(functools.partial(copies.start, "q turn"))
+    last_stages(4)
+    ring_add(3)
+    core_send(0)
+    gather_send(0)
+    for copy in own:
+        copy.start()
+    for c in range(half_way, chunks):
+        home(c)
+    stay = [local_copy(grad_low, grad_home)]
+    pl.when(stays)(stay[0].start)
+    norms_send(0)
+    for copy in own:
+        copy.wait()
+    if bits > 0:
+        gather_next(0)
+
+    @pl.when(moves)
+    def _():
+        copies.arrived("q turn")
+
+    @pl.when(stays)
+    def _():
+        qkv_core[0] = qkv_sum[own_q]
+
+    copies.start("q core", lambda: (qkv_core.at[0, 1 - core], qkv_core.at[1, 1 - core], flip("b")))
+    norms_add(0)
+    norms_send(1)
+    copies.arrived("q core")
+    add_into(qkv_core.at[1, core], qkv_core.at[0, core])
+    keep_q.start()
+    q_gather(0)
+    q_core_send(0)
+    keep_q.wait()
+    norms_add(1)
+    norms_send(2)
+    for stage in range(1, bits):
+        gather_next(stage)
+    for stage in range(bits):
         copies.arrived(("q gather", stage))
         if stage + 1 < bits:
             q_gather(stage + 1)
         q_core_send(stage + 1)
+    for step in range(2, len(axes)):
+        norms_add(step)
+        if step + 1 < len(axes):
+            norms_send(step + 1)
     norms_out[...] = norm_sum[...]
     for stage in range(bits + 1):
         for a in range(3):
             copies.arrived(("core", a, stage))
         copies.arrived(("q both", stage))
-    sometimes = ["q turn"] + [("home", c) for c in range(chunks)]
+    sometimes = ["q turn", "low"] + [("home", c) for c in range(chunks)]
 
     @pl.when(moves)
     def _():
+        copies.arrived("low")
         for c in range(chunks):
             copies.arrived(("home", c))
         for name in sometimes:
@@ -985,20 +1152,31 @@
 
 
 def back(
-    q, k, v, o, lse, cosine, sine, gain, norms, da, up, out, down, whole, w, resid, middle,
-    groups, rows=BLOCK, chunks=2,
+    q, k, v, o, lse, cosine, sine, gain, norms, da, low, inputs, branches, hidden, active,
+    heads, branch, whole, w, resid, middle, groups, rows=BLOCK, chunks=2,
 ):
     length, width = q.shape
     part, depth = da.shape
     bits = len(groups)
-    slab = up.shape[-1] // 4
-    tails = (up.shape[-2:-1] + (slab,), out.shape[-2:], down.shape[-2:])
+    slots = (2,) * bits
+    slab = hidden.shape[1] // 4
+    up_shape = slots + (depth // 2**bits, 4 * slab)
+    out_shape = (4,) + slots + (width // 2 ** (bits + 1), depth)
+    down_shape = (4,) + slots + (slab // 2**bits, depth)
+    tails = (up_shape[-2:-1] + (slab,), out_shape[-2:], down_shape[-2:])
     vmem = pl.BlockSpec(memory_space=pltpu.VMEM)
     anywhere = pl.BlockSpec(memory_space=pl.ANY)
-    slots = (2,) * bits
     quarter = depth // 2**bits
     q_tail = (quarter // 2, 3 * width)
-    scratch = [pltpu.VMEM((length, width), bf16)]
+    thin = slab // 2
+    scratch = [
+        pltpu.VMEM((4, 2) + out_shape[1:], bf16),
+        pltpu.VMEM(out_shape, bf16),
+        pltpu.VMEM((2,) + up_shape[:-1] + (thin,), bf16),
+        pltpu.VMEM((2,) + down_shape[2:], bf16),
+        pltpu.VMEM((depth, length // 2), bf16),
+    ]
+    scratch += [pltpu.VMEM((length, width), bf16)]
     scratch += [pltpu.VMEM((length, width), f32)] * 3 + [pltpu.VMEM((8, length), f32)]
     scratch += [
         pltpu.VMEM((length, 3 * width), bf16),
@@ -1024,22 +1202,26 @@
     scratch += [
         pltpu.VMEM((2,) + (2,) * (bits - 1 - stage) + q_tail, bf16) for stage in range(bits)
     ]
-    n = 3 + 3 * (4 * bits + 3 + bits + bits + 1)
+    n = 5 + 3 * (4 * bits + 3 + bits + bits + 1)
     n += 2 + chunks + 2 * bits + chunks + (bits + 3) + 2 + bits + bits + 1
     scratch += [pltpu.SemaphoreType.DMA((n,)), pltpu.SemaphoreType.DMA((n,))]
-    scratch += [pltpu.SemaphoreType.DMA((1 + 12 + 4 + 1 + 3 + 1,))]
+    scratch += [pltpu.SemaphoreType.DMA((64,))]
     return pl.pallas_call(
         functools.partial(back_kernel, groups=groups, rows=rows, chunks=chunks),
         out_shape=(
             jax.ShapeDtypeStruct((8, depth), f32),
             jax.ShapeDtypeStruct((part, depth), bf16),
+            jax.ShapeDtypeStruct((part, depth), bf16),
             jax.ShapeDtypeStruct(slots + (2,) + q_tail, bf16),
-            jax.ShapeDtypeStruct(slots + (up.shape[-2], 2 * slab), bf16),
-            jax.ShapeDtypeStruct((2,) + out.shape[1:], bf16),
-            jax.ShapeDtypeStruct((2,) + down.shape[1:], bf16),
+            jax.ShapeDtypeStruct(up_shape[:-1] + (2 * slab,), bf16),
+            jax.ShapeDtypeStruct((2,) + out_shape[1:], bf16),
+            jax.ShapeDtypeStruct((2,) + down_shape[1:], bf16),
+            jax.ShapeDtypeStruct(up_shape, bf16),
+            jax.ShapeDtypeStruct(out_shape, bf16),
+            jax.ShapeDtypeStruct(down_shape, bf16),
         ),
-        in_specs=[vmem] * 9 + [anywhere] * 8,
-        out_specs=(vmem,) + (anywhere,) * 5,
+        in_specs=[vmem] * 9 + [anywhere] * 12,
+        out_specs=(vmem,) + (anywhere,) * 9,
         scratch_shapes=scratch,
         compiler_params=pltpu.CompilerParams(
             vmem_limit_bytes=63 * 2**20, collective_id=1, has_side_effects=True
@@ -1047,7 +1229,10 @@
         cost_estimate=pl.CostEstimate(
             flops=100_000_000_000, bytes_accessed=32 * 2**20, transcendentals=0
         ),
-    )(q, k, v, o, lse, cosine, sine, gain, norms, da, up, out, down, whole, w, resid, middle)
+    )(
+        q, k, v, o, lse, cosine, sine, gain, norms, da, low, inputs, branches, hidden, active, heads,
+        branch, whole, w, resid, middle,
+    )[:7]
 
 
 def norm_forward(value, gain, shift):
@@ -1156,7 +1341,7 @@
     branch_f = dot(active[part:], down_half).astype(bf16)
     branch_f = dot(active[:part], down_half) + across(branch_f, "b").astype(f32)
     out_f, unit_3, inverse_3 = norm_forward(branch_f, gains[3], shifts[3])
-    output = turn((middle + out_f).astype(bf16))
+    output = (middle + out_f).astype(bf16)
 
     picks = (
         corpus_ids[:, None] == jnp.arange(corpus_weight.shape[0], dtype=jnp.int32)[None, :]
@@ -1168,9 +1353,6 @@
     pair_g = jnp.concatenate([own_g, across(own_g, "b")], axis=0)
     grad_active = dot(pair_g, down_half, NT)
     grad_hidden = (slope.astype(f32) * grad_active).astype(bf16)
-    down_grad = dot(active, pair_g, TN).astype(bf16)
-    up_grad = dot(pair_f, grad_hidden, TN).astype(bf16)
-
     grad_f = dot(grad_hidden[part:], up_half, NT).astype(bf16)
     grad_f = dot(grad_hidden[:part], up_half, NT) + across(grad_f, "b").astype(f32)
     back_2, gain_2, shift_2 = norm_backward(grad_f, unit_2, inverse_2, gains[2])
@@ -1178,17 +1360,10 @@
     back_1, gain_1, shift_1 = norm_backward(grad_middle, unit_1, inverse_1, gains[1])
     grad_a = back_1.astype(bf16)
     grad_attended = dot(grad_a, out_whole, NT).astype(bf16)
-    out_grad = dot(heads, grad_a, TN).astype(bf16)
-    out_grad = out_grad.reshape(4, 2, cols // 2, depth)
-    sent = lax.dynamic_index_in_dim(out_grad, 1 - core, 1, False)
-    kept = lax.dynamic_index_in_dim(out_grad, core, 1, False)
-    out_grad = (kept.astype(f32) + across(sent, "b").astype(f32)).astype(bf16)
-    def pieces(value):
-        return value.reshape((4,) + slots + (value.size // (4 * n_groups * depth), depth))
 
     none = jnp.zeros_like(gain_1)
     norms = jnp.stack([none, gain_1, gain_2, gain_3, none, shift_1, shift_2, shift_3])
-    norm_grads, input_grad, qkv_grad, up_grad, out_grad, down_grad = back(
+    norm_grads, input_grad, output, qkv_grad, up_grad, out_grad, down_grad = back(
         q,
         k,
         v,
@@ -1199,9 +1374,13 @@
         gains[0],
         norms,
         grad_attended,
-        up_grad.reshape(slots + (depth // n_groups, 2 * units)),
-        pieces(out_grad),
-        pieces(down_grad),
+        output,
+        pair_f,
+        pair_g,
+        grad_hidden,
+        active,
+        heads,
+        grad_a,
         whole_a,
         w_attn,
         resid_low,

time: 464 us -> 428 us (0.922)
  matrix products: 58.2 us -> 36.7 us
  starting transfers between devices: 16.4 us -> 3.84 us
    dot_general x11 -> x8, matrix products: 58.2 us -> 36.7 us  [dot(): return lax.dot_general(left, right, dims, preferred_element_type=f32)]
    ppermute x2 -> x1, starting transfers between devices: 11.5 us -> 1.88 us  [turn(): return lax.ppermute(value, ('b', 'h'), [(0, 0), (1, 2), (2, 1), (3, 3)])]
    unnamed x52 -> x32, local copies, waits for them, and re-layouts: 10.8 us -> 9.04 us
  transfers between devices with their start and end apart: 7 -> 5, of which waited for: 1 -> 2; matrix products, arithmetic and copies ran while one was open for 9% -> 2% of each run, Pallas kernels for 0% -> 0%
where the time goes in v5:
time: 428 us; the launch traced here: 420 us
  Pallas kernels  328 us (77%)
  matrix products  36.7 us (9%)
  local copies, waits for them, and re-layouts  22.9 us (5%)
  other arithmetic  22.6 us (5%)
  waiting for transfers between devices  4.58 us (1%)
    pallas_call x1, Pallas kernels, back(): pl.pallas_call(functools.partial(back_kernel, groups=groups, rows=rows, c...  185 us
    pallas_call x1, Pallas kernels, front(): pl.pallas_call(functools.partial(front_kernel, groups=groups, chunks=chun...  142 us
    dot_general x8, matrix products, dot(): return lax.dot_general(left, right, dims, preferred_element_type=f32)  36.7 us
    unnamed x32, local copies, waits for them, and re-layouts  9.04 us
  transfers between devices with their start and end apart: 5, of which 2 were waited for; matrix products, arithmetic and copies ran while one was open for 2% of the time, Pallas kernels for 0%

profile of v5, /device:TPU:0, one launch (start us, length us, event | category | flops | bytes accessed | tf_op | source)
XLA Modules:
  0.0 420.0 jit_solution(4388608484922800038)
XLA Ops:
  3.6 2.8 copy.28
  6.3 2.9 reshape.133.refs_2_
  9.2 142.4 %shard_map.179 = (bf16[2048,256]{1,0:T(8,128)(2,1)}, bf16[2048,256]{1,0:T(8,128)(2,1)}, bf16[2048,256]{1,0:T(8,128)(2,1)}, bf16[2048,1024]{1,0:T(8,128)(2,1)}, b...) custom-call(bf16[512,1024]{1,0:T(8,128)(2,1)} %bitcast.69, ...), custom_call_target="tpu_custom_call" | custom-call | flops 99999997952 | bytes 33554432 | tf_op jit(solution)/shard_map/pallas_call | solution.py:511
  151.6 3.3 fusion.31
  158.1 2.3 collective-permute-done.1
  160.4 9.1 %multiply_convert_fusion.1 = (bf16[1024,2048]{1,0:T(8,128)(2,1)S(1)}, f32[1024,2048]{1,0:T(8,128)}) fusion(bf16[1024,2048]{1,0:T(8,128)(2,1)S(1)} %bitcast.72, bf16[512,1024]{1,0:T(8,128)(2,1)S(1)} %collective-permute-done.1, bf16[512,1024]{1,0:T(8,128)(2,1)S(1)} %add_convert_fusion.1), kind=kOutput, calls=%fused_computation.9 | convolution fusion | flops 4318035968 | bytes 18874368 | tf_op jit(solution)/shard_map/dot_general | solution.py:1267
  169.5 2.3 fusion.17
  173.5 1.9 collective-permute-start
  175.4 2.4 fusion.26
  179.1 1.6 multiply_reduce_fusion.1
  180.7 2.6 add_convert_fusion
  183.9 2.3 collective-permute-done.3
  186.1 11.9 %multiply_convert_fusion.refs_13_ = bf16[1024,2048]{1,0:T(8,128)(2,1)S(1)} fusion(bf16[2048,1024]{1,0:T(8,128)(2,1)S(1)} %bitcast.77, f32[1024,2048]{1,0:T(8,128)} %get-tuple-element.96, bf16[512,1024]{1,0:T(8,128)(2,1)S(1)} %collective-permute-done.3, bf16[512,1024]{1,0:T(8,128)(2,1)S(1)} %get-tuple-element.82), kind=kOutput, calls=%fused_computation.8 | convolution fusion | flops 4343201792 | bytes 18874368 | tf_op jit(solution)/shard_map/dot_general | solution.py:1267
  198.1 2.4 fusion.20
  203.8 3.0 multiply_reduce_fusion.2
  206.9 2.9 multiply_reduce_fusion
  212.2 2.3 convolution_convert_fusion.refs_9_
  215.1 185.4 %shard_map.180 = (f32[8,1024]{1,0:T(8,128)}, bf16[512,1024]{1,0:T(8,128)(2,1)}, bf16[512,1024]{1,0:T(8,128)(2,1)}, bf16[2,2,2,128,768]{4,3,2,1,0:T(8,128)(2,1)},...) custom-call(bf16[2048,256]{1,0:T(8,128)(2,1)} %get-tuple-element.28., ...), custom_call_target="tpu_custom_call" | custom-call | flops 99999997952 | bytes 33554432 | tf_op jit(solution)/shard_map/pallas_call | solution.py:1209
  402.0 2.2 bitcast_convert_fusion.3
  404.3 1.6 bitcast_convert_fusion.2
  405.8 3.2 reshape.134
  409.0 4.6 %copy.25 = f32[1024,3,256]{2,0,1:T(8,128)} copy(f32[1024,3,256]{2,1,0:T(4,128)} %reshape.134) | data formatting | bytes 6291456
  413.6 2.6 bitcast_convert_fusion.1
  416.3 2.6 bitcast_convert_fusion
  (63 shorter events, 17.9 us)
Async XLA Ops:
  154.9 1.2 copy-start.7
  156.8 3.6 copy-start.10
  157.6 2.8 collective-permute-start.1
  160.4 9.1 %copy-start.11 = (bf16[4,2,2,128,1024]{4,3,2,1,0:T(8,128)(2,1)S(1)}, bf16[4,2,2,128,1024]{4,3,2,1,0:T(8,128)(2,1)}, u32[]{:S(2)}) copy-start(bf16[4,2,2,128,1024]{4,3,2,1,0:T(8,128)(2,1)} %get-tuple-element.38) | copy-start | bytes 12582916
  169.5 5.9 %copy-start.13 = (bf16[1024,2048]{1,0:T(8,128)(2,1)}, bf16[1024,2048]{1,0:T(8,128)(2,1)S(1)}, u32[]{:S(2)}) copy-start(bf16[1024,2048]{1,0:T(8,128)(2,1)S(1)} %get-tuple-element.95.refs_14_) | copy-start | bytes 12582916
  169.5 3.4 copy-start.9
  171.8 3.6 collective-permute-start.2
  173.5 4.7 %collective-permute-start = (f32[1]{0:T(128)}, f32[1]{0:T(128)}, u32[]{:S(2)}, u32[]{:S(2)}) collective-permute-start(f32[1]{0:T(128)} %bitcast.6), channel_id=1, source_target_pairs={{0,0},{2,4},{4,2},{6,6},{1,1},{3,5},{5,3},{7,7},{8,8},{10,12},{12,... | collective-permute-start | bytes 20 | tf_op jit(solution)/shard_map/ppermute | solution.py:1275
  177.8 1.2 copy-start
  183.2 2.9 collective-permute-start.3
  198.1 5.8 %copy-start.14 = (bf16[1024,2048]{1,0:T(8,128)(2,1)}, bf16[1024,2048]{1,0:T(8,128)(2,1)S(1)}, u32[]{:S(2)}) copy-start(bf16[1024,2048]{1,0:T(8,128)(2,1)S(1)} %multiply_convert_fusion.refs_13_) | copy-start | bytes 12582916
  200.5 3.4 collective-permute-start.4
  209.8 1.4 copy-start.1
  209.9 2.3 copy-start.12
  212.2 2.3 copy-start.8
  400.5 3.7 copy-start.5
  402.0 3.8 copy-start.4
  409.0 4.6 %copy-start.3 = (bf16[2,2,256,1024]{3,2,1,0:T(8,128)(2,1)S(1)}, bf16[2,2,256,1024]{3,2,1,0:T(8,128)(2,1)}, u32[]{:S(2)}) copy-start(bf16[2,2,256,1024]{3,2,1,0:T(8,128)(2,1)} %get-tuple-element.45) | copy-start | bytes 6291460
  413.6 2.6 copy-start.2
  416.3 2.6 copy-start.6

commit v6 on v5

--- a/solution.py
+++ b/solution.py
@@ -33,6 +33,18 @@
 
 
 MESH = pl.DeviceIdType.MESH
+BACK_PLAN = {
+    "front": "s1 s2",
+    0: "a1 s3",
+    1: "a2",
+    3: "b1 r1",
+    4: "s4",
+    6: "a3",
+    7: "b2 r2",
+    9: "b3 r3",
+    "x0": "a4",
+    "x3": "b4 r4 end",
+}
 FRONT_PLAN = {
     "own": "ring",
     "near": "one",
@@ -413,7 +425,7 @@
             value = row[block, inside].astype(f32)
             center = value - jnp.mean(value, axis=1, keepdims=True)
             inverse = lax.rsqrt(jnp.mean(center * center, axis=1, keepdims=True) + EPS)
-            normed = (center * inverse * gain_ref[...] + shift_ref[...]).astype(bf16)
+            normed = (center * inverse * gain_ref[0:1] + shift_ref[0:1]).astype(bf16)
             whole_ref[at] = normed
             w = w_att[...].reshape(depth, 3 * width)
             mixed = jnp.dot(normed, w, preferred_element_type=f32)
@@ -553,7 +565,7 @@
         q_ref, k_ref, v_ref, o_ref, lse_ref, cos_ref, sin_ref, gain_ref, norms_ref,
         da_ref, low_ref, inputs_ref, branches_ref, hidden_ref, active_ref, heads_ref, branch_ref,
         whole_ref, w_ref, resid_ref, middle_ref,
-        norms_out, grad_home, low_home, qkv_all, up_all, out_all, down_all,
+        gains_out, shifts_out, grad_home, low_home, qkv_all, up_all, out_all, down_all,
         up_ref, out_ref, down_ref,
         out_part, out_in, up_tile, down_tile, turned,
         do, dq, dk, dv, delta, mixed, whole, w, resid, middle,
@@ -813,12 +825,43 @@
         for copy in made:
             copy.wait()
 
-    for k in (1, 2, 3, 4):
+    whole_load = local_copy(whole_ref, whole)
+
+    def begin(k):
         shard_gradients(k)
-        if k < 3:
-            plane_send(k, 0)
+        if k == 4:
+            whole_load.start()
+        plane_send(k, 0)
+
+    def last_stages(k):
+        for stage in range(1, bits):
+            plane_step(k, stage)
+
+    def ring(step):
+        if step > 1:
+            ring_add(step - 1)
+        if step < 4:
+            ring_send(step)
+
+    own = [local_copy(passing[a].at[2], result(a, tuple(group))) for a in range(3)]
+
+    def finish():
+        core_send(0)
+        gather_send(0)
+        for copy in own:
+            copy.start()
+
+    kinds = {"s": begin, "a": lambda k: plane_step(k, 0), "b": last_stages, "r": ring}
+
+    def sums_at(point):
+        for name in BACK_PLAN.get(point, "").split():
+            if name == "end":
+                finish()
+            else:
+                kinds[name[0]](int(name[1]))
+
+    sums_at("front")
     early = [
-        local_copy(whole_ref, whole),
         local_copy(w_ref, w),
         local_copy(resid_ref, resid),
         local_copy(middle_ref, middle),
@@ -875,32 +918,6 @@
 
     count = blocks * (blocks + 1) // 2
 
-    def last_stages(k):
-        for stage in range(1, bits):
-            plane_step(k, stage)
-
-    def sums_a():
-        plane_step(1, 0)
-        plane_send(3, 0)
-
-    def sums_b():
-        plane_step(2, 0)
-        plane_send(4, 0)
-
-    def sums_c():
-        last_stages(1)
-        ring_send(1)
-
-    def sums_d():
-        plane_step(3, 0)
-
-    def sums_e():
-        last_stages(2)
-        ring_add(1)
-        ring_send(2)
-
-    plans = ((0, sums_a), (2, sums_b), (4, sums_c), (6, sums_d), (8, sums_e))
-
     def tiles(low, high):
         @pl.loop(low, high)
         def _(t):
@@ -910,12 +927,13 @@
             tile(i, t - i * (i + 1) // 2)
 
     low = 0
-    for when, step in plans:
-        when = when * count // 10
-        if when > low:
-            tiles(low, when)
-        step()
-        low = when
+    for point in range(10):
+        when = point * count // 10
+        if point in BACK_PLAN:
+            if when > low:
+                tiles(low, when)
+            sums_at(point)
+            low = when
     tiles(low, count)
 
     def turn_back(grad, at):
@@ -954,6 +972,7 @@
             ("x core", slot),
             lambda slot=slot: (sent.at[slot], from_core.at[slot], flip("b")),
         )
+    sums_at("x0")
     copies.arrived(("x core", 0))
     for c in range(chunks):
         total = input_part(2 * core + 1 - near, c) + from_core[0, inside(c)].astype(f32)
@@ -962,7 +981,8 @@
             ("x near", c),
             lambda c=c: (sent.at[2, inside(c)], from_near.at[inside(c)], flip("l")),
         )
-    plane_step(4, 0)
+    sums_at("x1")
+    whole_load.wait()
     side = quarter // 2
     for index in np.ndindex(*(2,) * bits):
         first = sum(bit << (bits - 1 - axis) for axis, bit in enumerate(index)) * quarter
@@ -1003,9 +1023,7 @@
             add_into(q_slot(i, stage, 0), qkv_in[stage].at[i])
 
     q_send(0)
-    last_stages(3)
-    ring_add(2)
-    ring_send(3)
+    sums_at("x2")
     copies.arrived(("x core", 1))
 
     @pl.loop(0, chunks)
@@ -1038,7 +1056,7 @@
             center = value - jnp.mean(value, axis=1, keepdims=True)
             inverse = lax.rsqrt(jnp.mean(center * center, axis=1, keepdims=True) + EPS)
             unit = center * inverse
-            scaled = grad * gain_ref[...]
+            scaled = grad * gain_ref[0:1]
             back = inverse * (
                 scaled
                 - jnp.mean(scaled, axis=1, keepdims=True)
@@ -1064,8 +1082,6 @@
         return qkv_all.at[at + (core,)]
 
     keep_q = local_copy(qkv_core.at[1, core], q_spot(own_q))
-    own = [local_copy(passing[a].at[2], result(a, tuple(group))) for a in range(3)]
-
     def q_gather(stage):
         at = tuple(group[axis] if axis >= stage else slice(None) for axis in range(bits))
         held = qkv_core.at[1, core] if stage == 0 else q_spot(at)
@@ -1076,9 +1092,11 @@
         held = qkv_core.at[1, core] if stage == 0 else spot
         copies.start(("q both", stage), lambda: (held, spot, flip("b")))
 
+    sums_at("x3")
     half_way = chunks // 2
     for c in range(half_way):
         home(c)
+    sums_at("x4")
     for stage in range(bits):
         q_add(stage)
         if stage + 1 < bits:
@@ -1086,21 +1104,16 @@
 
     copies.plan("q turn", lambda: (qkv_sum.at[own_q], qkv_core.at[0], partner))
     pl.when(moves)(functools.partial(copies.start, "q turn"))
-    last_stages(4)
-    ring_add(3)
-    core_send(0)
-    gather_send(0)
-    for copy in own:
-        copy.start()
+    sums_at("x5")
     for c in range(half_way, chunks):
         home(c)
     stay = [local_copy(grad_low, grad_home)]
     pl.when(stays)(stay[0].start)
     norms_send(0)
+    sums_at("x6")
     for copy in own:
         copy.wait()
-    if bits > 0:
-        gather_next(0)
+    gather_next(0)
 
     @pl.when(moves)
     def _():
@@ -1132,7 +1145,8 @@
         norms_add(step)
         if step + 1 < len(axes):
             norms_send(step + 1)
-    norms_out[...] = norm_sum[...]
+    gains_out[...] = norm_sum[0:4]
+    shifts_out[...] = norm_sum[4:8]
     for stage in range(bits + 1):
         for a in range(3):
             copies.arrived(("core", a, stage))
@@ -1209,7 +1223,8 @@
     return pl.pallas_call(
         functools.partial(back_kernel, groups=groups, rows=rows, chunks=chunks),
         out_shape=(
-            jax.ShapeDtypeStruct((8, depth), f32),
+            jax.ShapeDtypeStruct((4, depth), f32),
+            jax.ShapeDtypeStruct((4, depth), f32),
             jax.ShapeDtypeStruct((part, depth), bf16),
             jax.ShapeDtypeStruct((part, depth), bf16),
             jax.ShapeDtypeStruct(slots + (2,) + q_tail, bf16),
@@ -1221,7 +1236,7 @@
             jax.ShapeDtypeStruct(down_shape, bf16),
         ),
         in_specs=[vmem] * 9 + [anywhere] * 12,
-        out_specs=(vmem,) + (anywhere,) * 9,
+        out_specs=(vmem,) * 2 + (anywhere,) * 9,
         scratch_shapes=scratch,
         compiler_params=pltpu.CompilerParams(
             vmem_limit_bytes=63 * 2**20, collective_id=1, has_side_effects=True
@@ -1232,7 +1247,7 @@
     )(
         q, k, v, o, lse, cosine, sine, gain, norms, da, low, inputs, branches, hidden, active, heads,
         branch, whole, w, resid, middle,
-    )[:7]
+    )[:8]
 
 
 def norm_forward(value, gain, shift):
@@ -1312,8 +1327,8 @@
         w_up.reshape(slots + (depth // n_groups, units)),
         w_out.reshape((2,) + slots + (cols // (2 * n_groups), depth)),
         w_down.reshape((2,) + slots + (units // (2 * n_groups), depth)),
-        gains[0],
-        shifts[0],
+        norm_gains,
+        norm_shifts,
         cosine,
         sine,
         groups,
@@ -1363,7 +1378,7 @@
 
     none = jnp.zeros_like(gain_1)
     norms = jnp.stack([none, gain_1, gain_2, gain_3, none, shift_1, shift_2, shift_3])
-    norm_grads, input_grad, output, qkv_grad, up_grad, out_grad, down_grad = back(
+    gain_grad, shift_grad, input_grad, output, qkv_grad, up_grad, out_grad, down_grad = back(
         q,
         k,
         v,
@@ -1371,7 +1386,7 @@
         lse,
         cosine,
         sine,
-        gains[0],
+        norm_gains,
         norms,
         grad_attended,
         output,
@@ -1388,7 +1403,8 @@
         groups,
     )
     input_grad = input_grad.astype(f32)
-    qkv_grad = qkv_grad.reshape(depth, 3, cols).astype(f32)
+    qkv_grad = qkv_grad.reshape(depth, 3 * cols).astype(f32)
+    qkv_grad = jnp.stack(jnp.split(qkv_grad, 3, axis=1), axis=1)
     up_grad = up_grad.reshape(depth, units).astype(f32)
     out_grad = out_grad.reshape(cols, depth).astype(f32)
     down_grad = down_grad.reshape(units, depth).astype(f32)
@@ -1399,8 +1415,8 @@
         out_grad,
         up_grad,
         down_grad,
-        norm_grads[:4],
-        norm_grads[4:],
+        gain_grad,
+        shift_grad,
     )
 
 

time: 428 us -> 418 us (0.977); the launches traced: 420 us -> 415 us
  local copies, waits for them, and re-layouts: 22.9 us -> 15.2 us
  Pallas kernels: 328 us -> 322 us
  starting transfers between devices: 3.84 us -> 9.31 us
    pallas_call x1, Pallas kernels: 185 us -> 176 us  [back(): pl.pallas_call(functools.partial(back_kernel, groups=groups, rows=rows, c...]
    ppermute x4, starting transfers between devices: 1.96 us -> 7.43 us  [across(): return lax.ppermute(value, axis, SWAP)]
    unnamed x32 -> x37, local copies, waits for them, and re-layouts: 9.04 us -> 6.9 us
where the time goes in v6:
time: 418 us; the launch traced here: 415 us
  Pallas kernels  322 us (77%)
  matrix products  36.7 us (9%)
  other arithmetic  24.8 us (6%)
  local copies, waits for them, and re-layouts  15.2 us (4%)
  starting transfers between devices  9.31 us (2%)
  waiting for transfers between devices  4.58 us (1%)
    pallas_call x1, Pallas kernels, back(): pl.pallas_call(functools.partial(back_kernel, groups=groups, rows=rows, c...  176 us
    pallas_call x1, Pallas kernels, front(): pl.pallas_call(functools.partial(front_kernel, groups=groups, chunks=chun...  146 us
    dot_general x8, matrix products, dot(): return lax.dot_general(left, right, dims, preferred_element_type=f32)  36.7 us
  transfers between devices with their start and end apart: 5, of which 2 were waited for; matrix products, arithmetic and copies ran while one was open for 2% of the time, Pallas kernels for 0%

profile of v6, /device:TPU:0, one launch (start us, length us, event | category | flops | bytes accessed | tf_op | source)
XLA Modules:
  0.0 414.6 jit_solution(17660503574756489037)
XLA Ops:
  2.3 2.8 copy.25
  5.1 2.9 reshape.133.refs_2_
  8.0 146.3 %shard_map.179 = (bf16[2048,256]{1,0:T(8,128)(2,1)}, bf16[2048,256]{1,0:T(8,128)(2,1)}, bf16[2048,256]{1,0:T(8,128)(2,1)}, bf16[2048,1024]{1,0:T(8,128)(2,1)}, b...) custom-call(bf16[512,1024]{1,0:T(8,128)(2,1)} %bitcast.76, ...), custom_call_target="tpu_custom_call" | custom-call | flops 99999997952 | bytes 33554432 | tf_op jit(solution)/shard_map/pallas_call | solution.py:523
  154.3 3.3 fusion.30
  160.3 3.0 collective-permute-start.1
  163.2 2.3 collective-permute-done.1
  165.5 9.1 %multiply_convert_fusion.1 = (bf16[1024,2048]{1,0:T(8,128)(2,1)S(1)}, f32[1024,2048]{1,0:T(8,128)}) fusion(bf16[1024,2048]{1,0:T(8,128)(2,1)S(1)} %bitcast.79, bf16[512,1024]{1,0:T(8,128)(2,1)S(1)} %collective-permute-done.1, bf16[512,1024]{1,0:T(8,128)(2,1)S(1)} %add_convert_fusion.1), kind=kOutput, calls=%fused_computation.9 | convolution fusion | flops 4318035968 | bytes 18874368 | tf_op jit(solution)/shard_map/dot_general | solution.py:1282
  174.6 2.3 fusion.17
  178.6 1.9 collective-permute-start
  180.5 2.4 fusion.26
  184.2 1.6 multiply_reduce_fusion.1
  185.8 2.6 add_convert_fusion
  188.4 3.6 collective-permute-start.3
  192.0 2.3 collective-permute-done.3
  194.2 11.9 %multiply_convert_fusion.refs_13_ = bf16[1024,2048]{1,0:T(8,128)(2,1)S(1)} fusion(bf16[2048,1024]{1,0:T(8,128)(2,1)S(1)} %bitcast.84, f32[1024,2048]{1,0:T(8,128)} %get-tuple-element.81, bf16[512,1024]{1,0:T(8,128)(2,1)S(1)} %collective-permute-done.3, bf16[512,1024]{1,0:T(8,128)(2,1)S(1)} %get-tuple-element.71), kind=kOutput, calls=%fused_computation.8 | convolution fusion | flops 4343201792 | bytes 18874368 | tf_op jit(solution)/shard_map/dot_general | solution.py:1282
  206.2 2.4 fusion.20
  212.0 3.0 multiply_reduce_fusion.2
  215.0 2.9 multiply_reduce_fusion
  220.3 2.3 convolution_convert_fusion.refs_9_
  223.3 176.0 %shard_map.180 = (f32[4,1024]{1,0:T(4,128)}, f32[4,1024]{1,0:T(4,128)}, bf16[512,1024]{1,0:T(8,128)(2,1)}, bf16[512,1024]{1,0:T(8,128)(2,1)}, bf16[2,2,2,128,768...) custom-call(bf16[2048,256]{1,0:T(8,128)(2,1)} %get-tuple-element.29., ...), custom_call_target="tpu_custom_call" | custom-call | flops 99999997952 | bytes 33554432 | tf_op jit(solution)/shard_map/pallas_call | solution.py:1223
  399.3 2.3 bitcast_convert_fusion.4
  405.1 2.6 bitcast_convert_fusion.1
  407.7 2.6 bitcast_convert_fusion
  410.3 1.9 pad_maximum_fusion
  (69 shorter events, 18.8 us)
Async XLA Ops:
  157.5 1.2 copy-start.7
  159.5 6.0 %copy-start.12 = (bf16[2,2,256,2048]{3,2,1,0:T(8,128)(2,1)S(1)}, bf16[2,2,256,2048]{3,2,1,0:T(8,128)(2,1)}, u32[]{:S(2)}) copy-start(bf16[2,2,256,2048]{3,2,1,0:T(8,128)(2,1)} %get-tuple-element.38) | copy-start | bytes 12582916
  160.3 5.2 %collective-permute-start.1 = (bf16[512,1024]{1,0:T(8,128)(2,1)S(1)}, bf16[512,1024]{1,0:T(8,128)(2,1)S(1)}, u32[]{:S(2)}, u32[]{:S(2)}) collective-permute-start(bf16[512,1024]{1,0:T(8,128)(2,1)S(1)} %add_convert_fusion.1), channel_id=1, source_target_pairs={{0,4},{4,0},{1,5},{5,1},{2,6},{6,2},{3,7},{7,3},{8,12},{12,8},{9,1... | collective-permute-start | bytes 3145736 | tf_op jit(solution)/shard_map/ppermute | solution.py:1286
  165.5 9.1 %copy-start.13 = (bf16[4,2,2,128,1024]{4,3,2,1,0:T(8,128)(2,1)S(1)}, bf16[4,2,2,128,1024]{4,3,2,1,0:T(8,128)(2,1)}, u32[]{:S(2)}) copy-start(bf16[4,2,2,128,1024]{4,3,2,1,0:T(8,128)(2,1)} %get-tuple-element.39) | copy-start | bytes 12582916
  174.6 5.9 %copy-start.15 = (bf16[1024,2048]{1,0:T(8,128)(2,1)}, bf16[1024,2048]{1,0:T(8,128)(2,1)S(1)}, u32[]{:S(2)}) copy-start(bf16[1024,2048]{1,0:T(8,128)(2,1)S(1)} %get-tuple-element.80.refs_14_) | copy-start | bytes 12582916
  174.6 3.4 copy-start.11
  176.9 3.6 collective-permute-start.2
  178.6 4.7 %collective-permute-start = (f32[1]{0:T(128)}, f32[1]{0:T(128)}, u32[]{:S(2)}, u32[]{:S(2)}) collective-permute-start(f32[1]{0:T(128)} %bitcast.6), channel_id=1, source_target_pairs={{0,0},{2,4},{4,2},{6,6},{1,1},{3,5},{5,3},{7,7},{8,8},{10,12},{12,... | collective-permute-start | bytes 20 | tf_op jit(solution)/shard_map/ppermute | solution.py:1290
  182.9 1.2 copy-start
  188.4 5.9 %collective-permute-start.3 = (bf16[512,1024]{1,0:T(8,128)(2,1)S(1)}, bf16[512,1024]{1,0:T(8,128)(2,1)S(1)}, u32[]{:S(2)}, u32[]{:S(2)}) collective-permute-start(bf16[512,1024]{1,0:T(8,128)(2,1)S(1)} %get-tuple-element.71), channel_id=1, source_target_pairs={{0,4},{4,0},{1,5},{5,1},{2,6},{6,2},{3,7},{7,3},{8,12},{12,8},{9,1... | collective-permute-start | bytes 3145736 | tf_op jit(solution)/shard_map/ppermute | solution.py:1286
  206.2 5.8 %copy-start.16 = (bf16[1024,2048]{1,0:T(8,128)(2,1)}, bf16[1024,2048]{1,0:T(8,128)(2,1)S(1)}, u32[]{:S(2)}) copy-start(bf16[1024,2048]{1,0:T(8,128)(2,1)S(1)} %multiply_convert_fusion.refs_13_) | copy-start | bytes 12582916
  208.6 3.4 collective-permute-start.4
  218.0 1.4 copy-start.1
  218.0 2.3 copy-start.14
  220.3 2.3 copy-start.8
  399.3 2.3 copy-start.5
  399.3 3.9 copy-start.4
  403.5 1.6 copy-start.3
  405.1 2.6 copy-start.2
  410.3 1.9 copy-start.6
  412.2 1.0 copy-start.10
  412.2 1.6 copy-start.9
